TPU v7x, 256 devices: a whole 4x4x8 slice. The times are simulated.
256 devices in a mesh: grp: 16 (over y, x_hi, core), leaf: 16 (over x_lo, z).
Axes of the slice: x: 4 (x_hi: 2, x_lo: 2; x = x_hi * 2 + x_lo), y: 4, z: 8, core: 2. Of those that a mesh axis runs over, the one named last changes fastest.
Arguments:
- labels: int32 [131072], P(('grp', 'leaf')), may hold values from 0 to 255
- leaf_inverse: float32 [131072, 512], P(('grp', 'leaf')), may hold values from -1 to 4
- leaf_basis: float32 [131072, 128], P(('grp', 'leaf')), may hold values from -0.25 to 0.25
- leaf_solved: float32 [131072, 128], P(('grp', 'leaf')), may hold values from -0.5 to 0.5
- group_capacitance: float32 [32768, 2048], P(('grp', 'leaf')), may hold values from -1 to 4
- top_basis: float32 [131072, 128], P(('grp', 'leaf')), may hold values from -0.0625 to 0.0625
- top_solved: float32 [131072, 128], P(('grp', 'leaf')), may hold values from -0.5 to 0.5
- top_capacitance: float32 [2048, 2048], P('grp'), may hold values from -1 to 4
Outputs:
- dual_box: float32 [131072, 256], P(('grp', 'leaf'))
- scaled_dual: float32 [131072, 256], P(('grp', 'leaf'))
All inputs are finite; a program needn't handle non-finite values.
Results may differ from a plain program's by a relative error of at most 0.0003.
Values sent between devices are 32-bit elements; how exact they have to be, the bound alone decides.
No kernel may reach another device: no remote copies, remote signals or barrier semaphores. Data moves between devices by JAX's collectives and lax.ppermute only.
A program may use at most 64 MiB of HBM per device.

v0:
```python
import jax
import jax.numpy as jnp
from jax import lax
from jax.sharding import PartitionSpec as P

CLASSES = 256
ITERS = 2


high = lax.Precision.HIGHEST


def laid_out(tiles, dim):
    dims = list(tiles.shape[1:])
    dims[dim] *= tiles.shape[0]
    return jnp.moveaxis(tiles, 0, dim).reshape(dims)


def from_everyone(shard, axis):
    devices = lax.axis_size(axis)
    return lax.all_to_all(
        jnp.broadcast_to(shard[None], (devices, *shard.shape)), axis, 0, 0, tiled=True
    )


def gather_directly(shard, axis, dim):
    return laid_out(from_everyone(shard, axis), dim)


def in_blocks(shard, dim, devices):
    dims = shard.shape
    tiles = shard.reshape(*dims[:dim], devices, dims[dim] // devices, *dims[dim + 1 :])
    return jnp.moveaxis(tiles, dim, 0)


def summed_on_arrival(shard, axis, dim):
    devices = lax.axis_size(axis)
    tiles = lax.all_to_all(in_blocks(shard, dim, devices), axis, 0, 0, tiled=True)
    return jnp.sum(tiles, axis=0)


def matmul(left, right):
    return jnp.dot(left, right, precision=high, preferred_element_type=jnp.float32)


def project_rows(basis, values):
    return lax.dot_general(
        basis, values, (((0,), (0,)), ((), ())), precision=high, preferred_element_type=jnp.float32
    )


def column_product(matrix, piece):
    return matmul(matrix, piece)


def shards(
    labels,
    leaf_inverse,
    leaf_basis,
    leaf_solved,
    group_capacitance,
    top_basis,
    top_solved,
    top_capacitance,
):
    columns = lax.broadcasted_iota(jnp.int32, (labels.shape[0], CLASSES), 1)
    label_sign = jnp.where(labels[:, None] == columns, 1.0, -1.0).astype(jnp.float32)
    dual_box = jnp.zeros((labels.shape[0], CLASSES), jnp.float32)
    scaled_dual = jnp.zeros((labels.shape[0], CLASSES), jnp.float32)
    for iteration in range(ITERS):
        rhs = label_sign * (1.0 + 1.0 * (dual_box - scaled_dual))
        local = matmul(leaf_inverse, rhs)
        coeffs = project_rows(leaf_basis, local)
        group_coef = column_product(group_capacitance, gather_directly(coeffs, "leaf", 0))
        inner = local - matmul(leaf_solved, group_coef)
        partial_proj = project_rows(top_basis, inner)
        share = summed_on_arrival(partial_proj, "leaf", 1)
        share_coef = column_product(top_capacitance, gather_directly(share, "grp", 0))
        top_coef = gather_directly(share_coef, "leaf", 1)
        solved = inner - matmul(top_solved, top_coef)
        moved = scaled_dual + label_sign * solved
        dual_box = jnp.clip(moved, 0.0, 1.0)
        scaled_dual = moved - dual_box
    return (dual_box, scaled_dual)


def solution(mesh):
    return jax.shard_map(
        shards,
        mesh=mesh,
        in_specs=(
            P(("grp", "leaf")),
            P(("grp", "leaf"), None),
            P(("grp", "leaf"), None),
            P(("grp", "leaf"), None),
            P(("grp", "leaf"), None),
            P(("grp", "leaf"), None),
            P(("grp", "leaf"), None),
            P("grp", None),
        ),
        out_specs=(P(("grp", "leaf"), None), P(("grp", "leaf"), None)),
        check_vma=False,
    )
```

profile of v0, /device:TPU:32, one launch (start us, length us, event | category | flops | bytes accessed | tf_op | source)
XLA Modules:
  0.0 213.1 jit_solution(9570797944302551494)
XLA Ops:
  0.6 0.0 copy-start
  0.6 1.2 copy-done
  1.9 1.8 fusion.5
  3.6 1.5 convolution_bitcast_fusion.1
  5.2 0.1 copy.24
  5.3 0.2 broadcast_in_dim.19
  5.5 0.0 copy-start.1
  5.5 58.1 %all_to_all.40 = f32[16,128,256]{2,1,0:T(8,128)S(1)} all-to-all(f32[16,128,256]{2,1,0:T(8,128)S(1)} %broadcast_in_dim.19), channel_id=1, replica_groups=mesh['grp'=16,'leaf'=16] {'leaf'}, dimensions={0} | all-to-all | bytes 4194304 | tf_op jit(solution)/shard_map/all_to_all | solution.py:21
  63.6 0.0 copy-start.4
  63.6 0.0 copy-done.1
  63.6 0.0 copy-start.3
  63.6 3.5 %fusion.26 = f32[256,128]{1,0:T(8,128)S(1)} fusion(f32[2048,256]{1,0:T(8,128)S(1)} %bitcast.74, f32[128,2048]{1,0:T(8,128)S(1)} %copy-done.1), kind=kOutput, calls=%fused_computation.39 | convolution fusion | flops 805306368 | bytes 3276800 | tf_op jit(solution)/shard_map/dot_general | solution.py:43
  67.1 0.0 copy-done.4
  67.1 0.0 copy-start.6
  67.1 0.6 convolution_subtract_fusion.3
  67.7 0.0 copy-done.3
  67.7 0.6 fusion.27
  68.3 13.0 %all_to_all.41 = f32[16,128,16]{1,2,0:T(8,128)S(1)} all-to-all(f32[16,128,16]{1,2,0:T(8,128)S(1)} %bitcast.77), channel_id=1, replica_groups=mesh['grp'=16,'leaf'=16] {'leaf'}, dimensions={0} | all-to-all | bytes 262144 | tf_op jit(solution)/shard_map/all_to_all | solution.py:38
  81.3 14.7 %all_to_all.42 = f32[16,128,16]{1,2,0:T(8,128)S(1)} all-to-all(f32[16,128,16]{1,2,0:T(8,128)S(1)} %broadcast_in_dim.20), channel_id=1, replica_groups=mesh['grp'=16,'leaf'=16] {'grp'}, dimensions={0} | all-to-all | bytes 262144 | tf_op jit(solution)/shard_map/all_to_all | solution.py:21
  96.1 2.1 %convolution_bitcast_fusion.3 = f32[128,16]{0,1:T(8,128)S(1)} fusion(f32[128,2048]{1,0:T(8,128)} %param.15, f32[16,128,16]{1,2,0:T(8,128)S(1)} %all_to_all.42), kind=kOutput, calls=%fused_computation.12 | convolution fusion | flops 50331648 | bytes 1187840 | tf_op jit(solution)/shard_map/dot_general | solution.py:43
  98.2 0.0 copy-start.2
  98.3 11.8 %all_to_all.43 = f32[16,128,16]{1,2,0:T(8,128)S(1)} all-to-all(f32[16,128,16]{1,2,0:T(8,128)S(1)} %broadcast_in_dim.21), channel_id=1, replica_groups=mesh['grp'=16,'leaf'=16] {'leaf'}, dimensions={0} | all-to-all | bytes 262144 | tf_op jit(solution)/shard_map/all_to_all | solution.py:21
  110.0 0.0 copy-done.6
  110.0 1.6 fusion.4
  111.6 1.2 fusion.8
  112.8 0.0 copy-done.2
  112.8 1.2 convolution_bitcast_fusion
  114.0 1.0 copy.26
  115.0 0.2 broadcast_in_dim.22
  115.2 51.3 %all_to_all.44 = f32[16,128,256]{2,1,0:T(8,128)S(1)} all-to-all(f32[16,128,256]{2,1,0:T(8,128)S(1)} %broadcast_in_dim.22), channel_id=1, replica_groups=mesh['grp'=16,'leaf'=16] {'leaf'}, dimensions={0} | all-to-all | bytes 4194304 | tf_op jit(solution)/shard_map/all_to_all | solution.py:21
  166.5 0.0 copy-start.5
  166.5 3.5 %fusion.28 = f32[256,128]{1,0:T(8,128)S(1)} fusion(f32[2048,256]{1,0:T(8,128)S(1)} %bitcast.75, f32[128,2048]{1,0:T(8,128)S(1)} %copy-done.1), kind=kOutput, calls=%fused_computation.41 | convolution fusion | flops 805306368 | bytes 3276800 | tf_op jit(solution)/shard_map/dot_general | solution.py:43
  170.0 0.0 copy-done.5
  170.0 0.6 convolution_subtract_fusion.1
  170.6 0.6 fusion.29
  171.2 13.0 %all_to_all.45 = f32[16,128,16]{1,2,0:T(8,128)S(1)} all-to-all(f32[16,128,16]{1,2,0:T(8,128)S(1)} %bitcast.78), channel_id=1, replica_groups=mesh['grp'=16,'leaf'=16] {'leaf'}, dimensions={0} | all-to-all | bytes 262144 | tf_op jit(solution)/shard_map/all_to_all | solution.py:38
  184.2 11.6 %all_to_all.46 = f32[16,128,16]{1,2,0:T(8,128)S(1)} all-to-all(f32[16,128,16]{1,2,0:T(8,128)S(1)} %broadcast_in_dim.23), channel_id=1, replica_groups=mesh['grp'=16,'leaf'=16] {'grp'}, dimensions={0} | all-to-all | bytes 262144 | tf_op jit(solution)/shard_map/all_to_all | solution.py:21
  195.8 2.1 %convolution_bitcast_fusion.2 = f32[128,16]{0,1:T(8,128)S(1)} fusion(f32[128,2048]{1,0:T(8,128)} %param.15, f32[16,128,16]{1,2,0:T(8,128)S(1)} %all_to_all.46), kind=kOutput, calls=%fused_computation.11 | convolution fusion | flops 50331648 | bytes 1187840 | tf_op jit(solution)/shard_map/dot_general | solution.py:43
  198.0 11.5 %all_to_all.47 = f32[16,128,16]{1,2,0:T(8,128)S(1)} all-to-all(f32[16,128,16]{1,2,0:T(8,128)S(1)} %broadcast_in_dim.24), channel_id=1, replica_groups=mesh['grp'=16,'leaf'=16] {'leaf'}, dimensions={0} | all-to-all | bytes 262144 | tf_op jit(solution)/shard_map/all_to_all | solution.py:21
  209.5 1.6 fusion.16
  211.1 1.0 copy.29
  212.1 1.0 copy.28
  (6 shorter events, 0.1 us)
Async XLA Ops:
  0.6 1.2 copy-start
  5.5 58.1 %copy-start.1 = (f32[128,2048]{1,0:T(8,128)S(1)}, f32[128,2048]{1,0:T(8,128)}, u32[]{:S(2)}) copy-start(f32[128,2048]{1,0:T(8,128)} %param.12) | copy-start | bytes 3145732
  63.6 3.5 %copy-start.4 = (f32[512,128]{1,0:T(8,128)S(1)}, f32[512,128]{1,0:T(8,128)}, u32[]{:S(2)}) copy-start(f32[512,128]{1,0:T(8,128)} %param.11) | copy-start | bytes 786436
  63.6 4.1 %copy-start.3 = (f32[512,128]{1,0:T(8,128)S(1)}, f32[512,128]{1,0:T(8,128)}, u32[]{:S(2)}) copy-start(f32[512,128]{1,0:T(8,128)} %param.13) | copy-start | bytes 786436
  67.1 42.9 %copy-start.6 = (s32[512]{0:T(512)S(1)}, s32[512]{0:T(512)}, u32[]{:S(2)}) copy-start(s32[512]{0:T(512)} %param.8) | copy-start | bytes 6148
  98.2 14.6 %copy-start.2 = (f32[512,128]{1,0:T(8,128)S(1)}, f32[512,128]{1,0:T(8,128)}, u32[]{:S(2)}) copy-start(f32[512,128]{1,0:T(8,128)} %param.10) | copy-start | bytes 786436
  166.5 3.5 %copy-start.5 = (f32[512,128]{1,0:T(8,128)S(1)}, f32[512,128]{1,0:T(8,128)}, u32[]{:S(2)}) copy-start(f32[512,128]{1,0:T(8,128)} %param.11) | copy-start | bytes 786436
where the time goes:
time: 214 us; the launch traced here: 213 us
  blocking collectives  185 us (86%)
  matrix products  22.5 us (11%)
  local copies, waits for them, and re-layouts  4.79 us (2%)
    all_to_all x6, blocking collectives, from_everyone(): lax.all_to_all(jnp.broadcast_to(shard[None], (devices, *shard.shape)), ax...  159 us
    all_to_all x2, blocking collectives, summed_on_arrival(): lax.all_to_all(in_blocks(shard, dim, devices), axis, 0, 0, tiled=True)  26 us
    dot_general x10, matrix products, matmul(): jnp.dot(left, right, precision=high, preferred_element_type=jnp.float32)  18.6 us

commit v1 on v0

v1 whole, which is shorter than its diff:
```python
import jax
import jax.numpy as jnp
from jax import lax
from jax.sharding import PartitionSpec as P

CLASSES = 256
ITERS = 2
RANK = 128

SQUARES = [[0, 1, 8, 9], [2, 3, 10, 11], [4, 5, 12, 13], [6, 7, 14, 15]]
STRIDES = [[0, 2, 4, 6], [1, 3, 5, 7], [8, 10, 12, 14], [9, 11, 13, 15]]


def dot(left, right, left_dim, right_dim):
    return lax.dot_general(
        left,
        right,
        (((left_dim,), (right_dim,)), ((), ())),
        precision=lax.Precision.HIGH,
        preferred_element_type=jnp.float32,
    )


def from_everyone(shard, axis):
    devices = lax.axis_size(axis)
    return lax.all_to_all(
        jnp.broadcast_to(shard[None], (devices, *shard.shape)), axis, 0, 0, tiled=True
    )


def in_place(blocks, positions):
    height = blocks[0].shape[0]
    stack = jnp.zeros((height * len(blocks), *blocks[0].shape[1:]), blocks[0].dtype)
    for block, position in zip(blocks, positions):
        stack = lax.dynamic_update_slice(stack, block, (position * height, 0))
    return stack


def across_square(pieces):
    moved = [pieces[0]]
    for q in range(1, 4):
        away = (q // 2) * 8 + q % 2
        moved.append(lax.ppermute(pieces[q], "leaf", [(i, i ^ away) for i in range(16)]))
    return moved


def along_stride(block):
    found = [block]
    for k in range(1, 4):
        pairs = [(i, (i // 8) * 8 + (i % 8 - 2 * k) % 8) for i in range(16)]
        found.append(lax.ppermute(block, "leaf", pairs))
    return found


def shards(
    labels,
    leaf_inverse,
    leaf_basis,
    leaf_solved,
    group_capacitance,
    top_basis,
    top_solved,
    top_capacitance,
):
    leaf = lax.axis_index("leaf")
    x, z = leaf // 8, leaf % 8
    parity, step = z % 2, z // 2
    place = x * 2 + parity

    lifted = dot(leaf_solved, top_basis, 0, 0)
    pieces = []
    for q in range(4):
        first = (x ^ (q // 2)) * 8 + (parity ^ (q % 2))
        columns = [
            lax.dynamic_slice(group_capacitance, (0, (first + 2 * j) * RANK), (RANK, RANK))
            for j in range(4)
        ]
        pieces.append(jnp.concatenate(columns + [lifted], axis=1))
    square = in_place(across_square(pieces), [place ^ q for q in range(4)])
    block, lifts = square[:, : 4 * RANK], square[:, 4 * RANK :]

    columns = lax.broadcasted_iota(jnp.int32, (labels.shape[0], CLASSES), 1)
    label_sign = jnp.where(labels[:, None] == columns, 1.0, -1.0).astype(jnp.float32)
    dual_box = jnp.zeros((labels.shape[0], CLASSES), jnp.float32)
    scaled_dual = jnp.zeros((labels.shape[0], CLASSES), jnp.float32)
    for iteration in range(ITERS):
        rhs = label_sign * (1.0 + 1.0 * (dual_box - scaled_dual))
        local = dot(leaf_inverse, rhs, 1, 0)
        coeffs = dot(leaf_basis, local, 0, 0)
        stacked = in_place(along_stride(coeffs), [(step + k) % 4 for k in range(4)])
        partial_coef = dot(block, stacked, 1, 0)
        group_coef = lax.psum_scatter(
            partial_coef, "leaf", scatter_dimension=0, axis_index_groups=SQUARES, tiled=True
        )
        partial_proj = dot(local, top_basis, 0, 0) - dot(partial_coef, lifts, 0, 0)
        tiles = lax.all_to_all(partial_proj.reshape(16, 16, RANK), "leaf", 0, 0, tiled=True)
        share = jnp.sum(tiles, axis=0)
        gathered = from_everyone(share, "grp")
        wide = jnp.moveaxis(gathered, 0, 1).reshape(16, 16 * RANK)
        share_coef = dot(wide, top_capacitance, 1, 1)
        top_coef = from_everyone(share_coef, "leaf").reshape(CLASSES, RANK)
        inner = local - dot(leaf_solved, group_coef, 1, 0)
        solved = inner - dot(top_solved, top_coef, 1, 1)
        moved = scaled_dual + label_sign * solved
        dual_box = jnp.clip(moved, 0.0, 1.0)
        scaled_dual = moved - dual_box
    return (dual_box, scaled_dual)


def solution(mesh):
    split = P(("grp", "leaf"), None)
    return jax.shard_map(
        shards,
        mesh=mesh,
        in_specs=(P(("grp", "leaf")), split, split, split, split, split, split, P("grp", None)),
        out_specs=(split, split),
        check_vma=False,
    )
```

time: 214 us -> 190 us (0.89)
  blocking collectives: 185 us -> 54.6 us
  local copies, waits for them, and re-layouts: 4.79 us -> 37 us
  waiting for transfers between devices: 0 us -> 30.9 us
  starting transfers between devices: 0 us -> 27.6 us
  between operations: 0.85 us -> 14.6 us
    all_to_all x6 -> x2, blocking collectives: 159 us -> 25.5 us  [from_everyone(): lax.all_to_all(jnp.broadcast_to(shard[None], (devices, *shard.shape)), ax...]
    unnamed x16 -> x78, local copies, waits for them, and re-layouts: 3.24 us -> 29.7 us
    ppermute x0 -> x9, waiting for transfers between devices: none -> 19 us  [the longest x6 11.8 us: along_stride(): found.append(lax.ppermute(block, 'leaf', pairs))]
    ppermute x0 -> x9, starting transfers between devices: none -> 17.8 us  [the longest x6 14.2 us: along_stride(): found.append(lax.ppermute(block, 'leaf', pairs))]
    all_to_all x0 -> x2, waiting for transfers between devices: none -> 11.8 us  [from_everyone(): lax.all_to_all(jnp.broadcast_to(shard[None], (devices, *shard.shape)), ax...]
    all_to_all x0 -> x2, starting transfers between devices: none -> 9.78 us  [from_everyone(): lax.all_to_all(jnp.broadcast_to(shard[None], (devices, *shard.shape)), ax...]
    dynamic_update_slice x0 -> x10, local copies, waits for them, and re-layouts: none -> 4.86 us  [in_place(): stack = lax.dynamic_update_slice(stack, block, (position * height, 0))]
    all_to_all x2, blocking collectives: 26 us -> 29 us  [shards(): lax.all_to_all(partial_proj.reshape(16, 16, RANK), 'leaf', 0, 0, tiled=True)]
  transfers between devices with their start and end apart: 0 -> 13, of which waited for: 0 -> 8; matrix products, arithmetic and copies ran while one was open for 0% -> 25% of each run, Pallas kernels for 0% -> 0%
where the time goes in v1:
time: 190 us; the launch traced here: 189 us
  blocking collectives  54.6 us (29%)
  local copies, waits for them, and re-layouts  37 us (19%)
  waiting for transfers between devices  30.9 us (16%)
  starting transfers between devices  27.6 us (15%)
  matrix products  23.8 us (13%)
  between operations  14.6 us (8%)
    unnamed x78, local copies, waits for them, and re-layouts  29.7 us
    all_to_all x2, blocking collectives, shards(): lax.all_to_all(partial_proj.reshape(16, 16, RANK), 'leaf', 0, 0, tiled=True)  29 us
    all_to_all x2, blocking collectives, from_everyone(): lax.all_to_all(jnp.broadcast_to(shard[None], (devices, *shard.shape)), ax...  25.5 us
    dot_general x17, matrix products, dot(): lax.dot_general(left, right, (((left_dim,), (right_dim,)), ((), ())), pre...  23.8 us
    ppermute x6, starting transfers between devices, along_stride(): found.append(lax.ppermute(block, 'leaf', pairs))  14.2 us
    all_to_all x2, waiting for transfers between devices, from_everyone(): lax.all_to_all(jnp.broadcast_to(shard[None], (devices, *shard.shape)), ax...  11.8 us
    ppermute x6, waiting for transfers between devices, along_stride(): found.append(lax.ppermute(block, 'leaf', pairs))  11.8 us
    all_to_all x2, starting transfers between devices, from_everyone(): lax.all_to_all(jnp.broadcast_to(shard[None], (devices, *shard.shape)), ax...  9.78 us
  transfers between devices with their start and end apart: 13, of which 8 were waited for; matrix products, arithmetic and copies ran while one was open for 25% of the time, Pallas kernels for 0%

profile of v1, /device:TPU:32, one launch (start us, length us, event | category | flops | bytes accessed | tf_op | source)
XLA Modules:
  0.0 188.6 jit_solution(2580737355351762027)
XLA Ops:
  7.3 1.1 copy-done
  8.4 1.4 fusion.5
  9.9 1.1 constant_dynamic-update-slice_fusion.27
  10.9 5.4 %collective-permute-start.3 = (f32[128,256]{0,1:T(8,128)}, f32[128,256]{0,1:T(8,128)}, u32[]{:S(2)}, u32[]{:S(2)}) collective-permute-start(f32[128,256]{0,1:T(8,128)} %get-tuple-element.31), channel_id=1, source_target_pairs={{0,6},{1,7},{2,0},{3,1},{4,2},{5,3},{6,4},{7,5},{8,14},{9,15},{10,... | collective-permute-start | bytes 393224 | tf_op jit(solution)/shard_map/ppermute | solution.py:51
  16.3 1.4 collective-permute-start.4
  17.8 2.4 %collective-permute-start.5 = (f32[128,256]{0,1:T(8,128)}, f32[128,256]{0,1:T(8,128)}, u32[]{:S(2)}, u32[]{:S(2)}) collective-permute-start(f32[128,256]{0,1:T(8,128)} %get-tuple-element.31), channel_id=1, source_target_pairs={{0,2},{1,3},{2,4},{3,5},{4,6},{5,7},{6,0},{7,1},{8,10},{9,11},{10,... | collective-permute-start | bytes 393224 | tf_op jit(solution)/shard_map/ppermute | solution.py:51
  23.5 1.6 copy.72
  26.0 1.6 copy.67
  27.6 1.6 copy.68
  29.1 1.6 copy.69
  30.7 1.6 copy.73
  35.2 1.5 constant_dynamic-update-slice_fusion.14
  42.4 1.5 constant_dynamic-update-slice_fusion.13
  44.5 1.5 constant_dynamic-update-slice_fusion.1
  46.6 1.1 constant_dynamic-update-slice_fusion.15
  47.7 1.0 collective-permute-start
  48.7 1.5 collective-permute-start.1
  51.3 1.1 collective-permute-start.2
  55.1 3.5 %collective-permute-done = f32[128,640]{0,1:T(8,128)} collective-permute-done((f32[128,640]{0,1:T(8,128)}, f32[128,640]{0,1:T(8,128)}, u32[]{:S(2)}, u32[]{:S(2)}) %collective-permute-start) | collective-permute-done | bytes 327712 | tf_op jit(solution)/shard_map/ppermute | solution.py:43
  58.6 1.0 constant_dynamic-update-slice_fusion.30
  59.6 3.7 %collective-permute-done.1 = f32[128,640]{0,1:T(8,128)} collective-permute-done((f32[128,640]{0,1:T(8,128)}, f32[128,640]{0,1:T(8,128)}, u32[]{:S(2)}, u32[]{:S(2)}) %collective-permute-start.1) | collective-permute-done | bytes 327712 | tf_op jit(solution)/shard_map/ppermute | solution.py:43
  63.3 1.0 constant_dynamic-update-slice_fusion.29
  64.5 1.8 fusion.9
  66.3 1.4 fusion.34
  68.3 15.3 %all_to_all.32 = f32[16,16,128]{2,1,0:T(8,128)S(1)} all-to-all(f32[16,16,128]{2,1,0:T(8,128)S(1)} %bitcast.63), channel_id=1, replica_groups=mesh['grp'=16,'leaf'=16] {'leaf'}, dimensions={0} | all-to-all | bytes 262144 | tf_op jit(solution)/shard_map/all_to_all | solution.py:96
  83.6 14.7 %all_to_all.30 = f32[16,16,128]{2,1,0:T(8,128)S(1)} all-to-all(f32[16,16,128]{2,1,0:T(8,128)S(1)} %broadcast_in_dim.18), channel_id=1, replica_groups=mesh['grp'=16,'leaf'=16] {'grp'}, dimensions={0} | all-to-all | bytes 262144 | tf_op jit(solution)/shard_map/all_to_all | solution.py:26
  98.3 1.8 fusion.26
  100.8 4.5 %all-to-all-start.2 = ((f32[16,16,128]{2,1,0:T(8,128)}), f32[16,16,128]{2,1,0:T(8,128)S(1)}, u32[]{:S(2)}, u32[]{:S(2)}) async-start(f32[16,16,128]{2,1,0:T(8,128)} %broadcast_in_dim.19), calls=%async_computation.3 | async-start | bytes 262144 | tf_op jit(solution)/shard_map/all_to_all | solution.py:26
  105.4 2.1 %convolution_subtract_fusion.3 = f32[256,512]{1,0:T(8,128)} fusion(f32[256,512]{1,0:T(8,128)S(1)} %fusion.5, f32[128,256]{1,0:T(8,128)} %reduce-scatter.3.cloned.1.call-done, f32[512,128]{1,0:T(8,128)S(1)} %copy-done.4), kind=kOutput, calls=%fused_computation.8 | convolution fusion | flops 100794368 | bytes 1441792 | tf_op jit(solution)/shard_map/dot_general | solution.py:15
  107.5 5.9 %all-to-all-done.2 = f32[16,16,128]{2,1,0:T(8,128)S(1)} async-done(((f32[16,16,128]{2,1,0:T(8,128)}), f32[16,16,128]{2,1,0:T(8,128)S(1)}, u32[]{:S(2)}, u32[]{:S(2)}) %all-to-all-start.2) | async-done | bytes 131104 | tf_op jit(solution)/shard_map/all_to_all | solution.py:26
  113.4 1.4 fusion.4
  116.2 1.8 collective-permute-start.6
  118.0 2.7 %collective-permute-start.7 = (f32[128,256]{0,1:T(8,128)S(1)}, f32[128,256]{0,1:T(8,128)S(1)}, u32[]{:S(2)}, u32[]{:S(2)}) collective-permute-start(f32[128,256]{0,1:T(8,128)S(1)} %get-tuple-element.33), channel_id=1, source_target_pairs={{0,4},{1,5},{2,6},{3,7},{4,0},{5,1},{6,2},{7,3},{8,12},{9,13},{10,... | collective-permute-start | bytes 393224 | tf_op jit(solution)/shard_map/ppermute | solution.py:51
  121.2 4.5 %collective-permute-done.6 = f32[128,256]{0,1:T(8,128)S(1)} collective-permute-done((f32[128,256]{0,1:T(8,128)S(1)}, f32[128,256]{0,1:T(8,128)S(1)}, u32[]{:S(2)}, u32[]{:S(2)}) %collective-permute-start.6) | collective-permute-done | bytes 131104 | tf_op jit(solution)/shard_map/ppermute | solution.py:51
  125.7 4.4 %collective-permute-done.7 = f32[128,256]{0,1:T(8,128)S(1)} collective-permute-done((f32[128,256]{0,1:T(8,128)S(1)}, f32[128,256]{0,1:T(8,128)S(1)}, u32[]{:S(2)}, u32[]{:S(2)}) %collective-permute-start.7) | collective-permute-done | bytes 131104 | tf_op jit(solution)/shard_map/ppermute | solution.py:51
  130.1 2.9 %collective-permute-done.8 = f32[128,256]{0,1:T(8,128)S(1)} collective-permute-done((f32[128,256]{0,1:T(8,128)S(1)}, f32[128,256]{0,1:T(8,128)S(1)}, u32[]{:S(2)}, u32[]{:S(2)}) %collective-permute-start.8) | collective-permute-done | bytes 131104 | tf_op jit(solution)/shard_map/ppermute | solution.py:51
  133.0 1.8 fusion.7
  134.8 1.3 fusion.35
  136.2 1.6 convolution_subtract_fusion.4
  137.8 13.8 %all_to_all.33 = f32[16,16,128]{2,1,0:T(8,128)S(1)} all-to-all(f32[16,16,128]{2,1,0:T(8,128)S(1)} %bitcast.62), channel_id=1, replica_groups=mesh['grp'=16,'leaf'=16] {'leaf'}, dimensions={0} | all-to-all | bytes 262144 | tf_op jit(solution)/shard_map/all_to_all | solution.py:96
  151.6 10.8 %all_to_all.31 = f32[16,16,128]{2,1,0:T(8,128)S(1)} all-to-all(f32[16,16,128]{2,1,0:T(8,128)S(1)} %broadcast_in_dim.20), channel_id=1, replica_groups=mesh['grp'=16,'leaf'=16] {'grp'}, dimensions={0} | all-to-all | bytes 262144 | tf_op jit(solution)/shard_map/all_to_all | solution.py:26
  162.5 1.8 fusion.23
  164.9 5.3 %all-to-all-start.5 = ((f32[16,16,128]{2,1,0:T(8,128)}), f32[16,16,128]{2,1,0:T(8,128)S(1)}, u32[]{:S(2)}, u32[]{:S(2)}) async-start(f32[16,16,128]{2,1,0:T(8,128)} %broadcast_in_dim.21), calls=%async_computation.7 | async-start | bytes 262144 | tf_op jit(solution)/shard_map/all_to_all | solution.py:26
  170.2 2.1 %convolution_subtract_fusion.1 = f32[256,512]{1,0:T(8,128)} fusion(f32[256,512]{1,0:T(8,128)S(1)} %fusion.12, f32[128,256]{1,0:T(8,128)} %reduce-scatter.5.cloned.1.call-done, f32[512,128]{1,0:T(8,128)S(1)} %copy-done.5), kind=kOutput, calls=%fused_computation.4 | convolution fusion | flops 100794368 | bytes 1441792 | tf_op jit(solution)/shard_map/dot_general | solution.py:15
  172.3 5.9 %all-to-all-done.5 = f32[16,16,128]{2,1,0:T(8,128)S(1)} async-done(((f32[16,16,128]{2,1,0:T(8,128)}), f32[16,16,128]{2,1,0:T(8,128)S(1)}, u32[]{:S(2)}, u32[]{:S(2)}) %all-to-all-start.5) | async-done | bytes 131104 | tf_op jit(solution)/shard_map/all_to_all | solution.py:26
  178.3 1.5 fusion.22
  179.8 1.0 copy.64
  180.8 1.0 copy.65
  (99 shorter events, 22.1 us)
Async XLA Ops:
  7.2 1.2 copy-start
  7.2 2.7 %copy-start.7 = (f32[512,128]{1,0:T(8,128)S(1)}, f32[512,128]{1,0:T(8,128)}, u32[]{:S(2)}) copy-start(f32[512,128]{1,0:T(8,128)} %param.10) | copy-start | bytes 786436
  7.2 98.2 %reduce-scatter.3.cloned.1.call-start = ((), (), s32[]{:S(2)}) async-start(), calls=%async_computation.8 | async-start | bytes 655360 | tf_op jit(solution)/shard_map/reduce_scatter | solution.py:92
  8.4 11.7 %copy-start.6 = (f32[128,2048]{1,0:T(8,128)S(1)}, f32[128,2048]{1,0:T(8,128)}, u32[]{:S(2)}) copy-start(f32[128,2048]{1,0:T(8,128)} %param.12) | copy-start | bytes 3145732
  10.9 40.3 %collective-permute-start.3 = (f32[128,256]{0,1:T(8,128)}, f32[128,256]{0,1:T(8,128)}, u32[]{:S(2)}, u32[]{:S(2)}) collective-permute-start(f32[128,256]{0,1:T(8,128)} %get-tuple-element.31), channel_id=1, source_target_pairs={{0,6},{1,7},{2,0},{3,1},{4,2},{5,3},{6,4},{7,5},{8,14},{9,15},{10,... | collective-permute-start | bytes 393224 | tf_op jit(solution)/shard_map/ppermute | solution.py:51
  16.3 36.9 %collective-permute-start.4 = (f32[128,256]{0,1:T(8,128)}, f32[128,256]{0,1:T(8,128)}, u32[]{:S(2)}, u32[]{:S(2)}) collective-permute-start(f32[128,256]{0,1:T(8,128)} %get-tuple-element.31), channel_id=1, source_target_pairs={{0,4},{1,5},{2,6},{3,7},{4,0},{5,1},{6,2},{7,3},{8,12},{9,13},{10,... | collective-permute-start | bytes 393224 | tf_op jit(solution)/shard_map/ppermute | solution.py:51
  17.8 36.4 %collective-permute-start.5 = (f32[128,256]{0,1:T(8,128)}, f32[128,256]{0,1:T(8,128)}, u32[]{:S(2)}, u32[]{:S(2)}) collective-permute-start(f32[128,256]{0,1:T(8,128)} %get-tuple-element.31), channel_id=1, source_target_pairs={{0,2},{1,3},{2,4},{3,5},{4,6},{5,7},{6,0},{7,1},{8,10},{9,11},{10,... | collective-permute-start | bytes 393224 | tf_op jit(solution)/shard_map/ppermute | solution.py:51
  21.0 11.3 %copy-start.14 = (f32[128,128]{1,0:T(8,128)S(1)}, f32[128,128]{1,0:T(8,128)}, u32[]{:S(2)}) copy-start(f32[128,128]{1,0:T(8,128)} %get-tuple-element.11) | copy-start | bytes 196612
  21.0 12.0 %copy-start.13 = (f32[128,128]{1,0:T(8,128)S(1)}, f32[128,128]{1,0:T(8,128)}, u32[]{:S(2)}) copy-start(f32[128,128]{1,0:T(8,128)} %get-tuple-element.10) | copy-start | bytes 196612
  32.4 7.2 %copy-start.15 = (f32[128,128]{0,1:T(8,128)S(1)}, f32[128,128]{0,1:T(8,128)}, u32[]{:S(2)}) copy-start(f32[128,128]{0,1:T(8,128)} %copy.72) | copy-start | bytes 196612
  33.0 13.6 %copy-start.2 = (f32[512,128]{1,0:T(8,128)S(1)}, f32[512,128]{1,0:T(8,128)}, u32[]{:S(2)}) copy-start(f32[512,128]{1,0:T(8,128)} %param.13) | copy-start | bytes 786436
  33.0 13.6 %copy-start.3 = (f32[512,128]{1,0:T(8,128)S(1)}, f32[512,128]{1,0:T(8,128)}, u32[]{:S(2)}) copy-start(f32[512,128]{1,0:T(8,128)} %param.11) | copy-start | bytes 786436
  33.7 7.3 %copy-start.16 = (f32[128,128]{0,1:T(8,128)S(1)}, f32[128,128]{0,1:T(8,128)}, u32[]{:S(2)}) copy-start(f32[128,128]{0,1:T(8,128)} %copy.68) | copy-start | bytes 196612
  34.4 6.6 %copy-start.17 = (f32[128,128]{0,1:T(8,128)S(1)}, f32[128,128]{0,1:T(8,128)}, u32[]{:S(2)}) copy-start(f32[128,128]{0,1:T(8,128)} %copy.79) | copy-start | bytes 196612
  35.2 6.5 %copy-start.18 = (f32[128,128]{0,1:T(8,128)S(1)}, f32[128,128]{0,1:T(8,128)}, u32[]{:S(2)}) copy-start(f32[128,128]{0,1:T(8,128)} %copy.80) | copy-start | bytes 196612
  37.5 7.0 %copy-start.19 = (f32[128,128]{0,1:T(8,128)S(1)}, f32[128,128]{0,1:T(8,128)}, u32[]{:S(2)}) copy-start(f32[128,128]{0,1:T(8,128)} %copy.69) | copy-start | bytes 196612
  38.2 7.7 %copy-start.20 = (f32[128,128]{0,1:T(8,128)S(1)}, f32[128,128]{0,1:T(8,128)}, u32[]{:S(2)}) copy-start(f32[128,128]{0,1:T(8,128)} %copy.77) | copy-start | bytes 196612
  39.0 7.0 %copy-start.21 = (f32[128,128]{0,1:T(8,128)S(1)}, f32[128,128]{0,1:T(8,128)}, u32[]{:S(2)}) copy-start(f32[128,128]{0,1:T(8,128)} %copy.81) | copy-start | bytes 196612
  47.7 2.5 %copy-start.11 = (f32[128,640]{0,1:T(8,128)}, f32[128,640]{0,1:T(8,128)S(1)}, u32[]{:S(2)}) copy-start(f32[128,640]{0,1:T(8,128)S(1)} %get-tuple-element.29) | copy-start | bytes 983044
  47.7 11.0 %collective-permute-start = (f32[128,640]{0,1:T(8,128)}, f32[128,640]{0,1:T(8,128)}, u32[]{:S(2)}, u32[]{:S(2)}) collective-permute-start(f32[128,640]{0,1:T(8,128)} %get-tuple-element.28), channel_id=1, source_target_pairs={{0,1},{1,0},{2,3},{3,2},{4,5},{5,4},{6,7},{7,6},{8,9},{9,8},{10,11... | collective-permute-start | bytes 983048 | tf_op jit(solution)/shard_map/ppermute | solution.py:43
  48.7 14.7 %collective-permute-start.1 = (f32[128,640]{0,1:T(8,128)}, f32[128,640]{0,1:T(8,128)}, u32[]{:S(2)}, u32[]{:S(2)}) collective-permute-start(f32[128,640]{0,1:T(8,128)} %get-tuple-element.27), channel_id=1, source_target_pairs={{0,8},{1,9},{2,10},{3,11},{4,12},{5,13},{6,14},{7,15},{8,0},{9,1},... | collective-permute-start | bytes 983048 | tf_op jit(solution)/shard_map/ppermute | solution.py:43
  50.2 1.0 copy-start.12
  51.3 13.2 %collective-permute-start.2 = (f32[128,640]{0,1:T(8,128)}, f32[128,640]{0,1:T(8,128)S(1)}, u32[]{:S(2)}, u32[]{:S(2)}) collective-permute-start(f32[128,640]{0,1:T(8,128)} %get-tuple-element.26), channel_id=1, source_target_pairs={{0,9},{1,8},{2,11},{3,10},{4,13},{5,12},{6,15},{7,14},{8,1},{9,0},... | collective-permute-start | bytes 983048 | tf_op jit(solution)/shard_map/ppermute | solution.py:43
  66.3 1.4 copy-start.1
  68.3 37.1 %copy-start.4 = (f32[512,128]{1,0:T(8,128)S(1)}, f32[512,128]{1,0:T(8,128)}, u32[]{:S(2)}) copy-start(f32[512,128]{1,0:T(8,128)} %param.11) | copy-start | bytes 786436
  98.3 15.1 %copy-start.9 = (f32[512,128]{1,0:T(8,128)S(1)}, f32[512,128]{1,0:T(8,128)}, u32[]{:S(2)}) copy-start(f32[512,128]{1,0:T(8,128)} %param.14) | copy-start | bytes 786436
  98.3 15.1 %copy-start.22 = (s32[512]{0:T(512)S(1)}, s32[512]{0:T(512)}, u32[]{:S(2)}) copy-start(s32[512]{0:T(512)} %param.8) | copy-start | bytes 6148
  100.8 12.6 %all-to-all-start.2 = ((f32[16,16,128]{2,1,0:T(8,128)}), f32[16,16,128]{2,1,0:T(8,128)S(1)}, u32[]{:S(2)}, u32[]{:S(2)}) async-start(f32[16,16,128]{2,1,0:T(8,128)} %broadcast_in_dim.19), calls=%async_computation.3 | async-start | bytes 262144 | tf_op jit(solution)/shard_map/all_to_all | solution.py:26
  105.3 64.9 %reduce-scatter.5.cloned.1.call-start = ((), (), s32[]{:S(2)}) async-start(), calls=%async_computation.9 | async-start | bytes 655360 | tf_op jit(solution)/shard_map/reduce_scatter | solution.py:92
  114.9 1.0 copy-start.8
  116.2 9.5 %collective-permute-start.6 = (f32[128,256]{0,1:T(8,128)S(1)}, f32[128,256]{0,1:T(8,128)S(1)}, u32[]{:S(2)}, u32[]{:S(2)}) collective-permute-start(f32[128,256]{0,1:T(8,128)S(1)} %get-tuple-element.33), channel_id=1, source_target_pairs={{0,6},{1,7},{2,0},{3,1},{4,2},{5,3},{6,4},{7,5},{8,14},{9,15},{10,... | collective-permute-start | bytes 393224 | tf_op jit(solution)/shard_map/ppermute | solution.py:51
  118.0 12.1 %collective-permute-start.7 = (f32[128,256]{0,1:T(8,128)S(1)}, f32[128,256]{0,1:T(8,128)S(1)}, u32[]{:S(2)}, u32[]{:S(2)}) collective-permute-start(f32[128,256]{0,1:T(8,128)S(1)} %get-tuple-element.33), channel_id=1, source_target_pairs={{0,4},{1,5},{2,6},{3,7},{4,0},{5,1},{6,2},{7,3},{8,12},{9,13},{10,... | collective-permute-start | bytes 393224 | tf_op jit(solution)/shard_map/ppermute | solution.py:51
  120.7 12.3 %collective-permute-start.8 = (f32[128,256]{0,1:T(8,128)S(1)}, f32[128,256]{0,1:T(8,128)S(1)}, u32[]{:S(2)}, u32[]{:S(2)}) collective-permute-start(f32[128,256]{0,1:T(8,128)S(1)} %get-tuple-element.33), channel_id=1, source_target_pairs={{0,2},{1,3},{2,4},{3,5},{4,6},{5,7},{6,0},{7,1},{8,10},{9,11},{10,... | collective-permute-start | bytes 393224 | tf_op jit(solution)/shard_map/ppermute | solution.py:51
  137.8 32.4 %copy-start.5 = (f32[512,128]{1,0:T(8,128)S(1)}, f32[512,128]{1,0:T(8,128)}, u32[]{:S(2)}) copy-start(f32[512,128]{1,0:T(8,128)} %param.11) | copy-start | bytes 786436
  162.4 15.8 %copy-start.10 = (f32[512,128]{1,0:T(8,128)S(1)}, f32[512,128]{1,0:T(8,128)}, u32[]{:S(2)}) copy-start(f32[512,128]{1,0:T(8,128)} %param.14) | copy-start | bytes 786436
  164.9 13.4 %all-to-all-start.5 = ((f32[16,16,128]{2,1,0:T(8,128)}), f32[16,16,128]{2,1,0:T(8,128)S(1)}, u32[]{:S(2)}, u32[]{:S(2)}) async-start(f32[16,16,128]{2,1,0:T(8,128)} %broadcast_in_dim.21), calls=%async_computation.7 | async-start | bytes 262144 | tf_op jit(solution)/shard_map/all_to_all | solution.py:26
Sparse Core Ops, SparseCore 0:
  66.4 24.5 reduce-scatter.2
  135.0 21.0 reduce-scatter.4

commit v2 on v0

v2 whole, which is shorter than its diff:
```python
import functools

import jax
import jax.numpy as jnp
from jax import lax
from jax.experimental import pallas as pl
from jax.experimental.pallas import tpu as pltpu
from jax.sharding import PartitionSpec as P

CLASSES = 256
RANK = 128
LEAF = 512
BOTH = ("grp", "leaf")


def partner(core, z):
    return (((z + core) ^ 1) - core) % 8


def devices():
    return [(g, i // 8, i % 8) for g in range(16) for i in range(16)]


def index(g, x, z):
    return g * 16 + x * 8 + z


def square_pairs(q):
    pairs = []
    for g, x, z in devices():
        other = index(g, x ^ (q // 2), partner(g % 2, z) if q % 2 else z)
        pairs.append((index(g, x, z), other))
    return pairs


def stride_pairs(k):
    return [(index(g, x, z), index(g, x, (z - 2 * k) % 8)) for g, x, z in devices()]


def square_groups():
    groups = []
    for g in range(16):
        for low in range(g % 2, 8, 2):
            high = (low + 1) % 8
            groups.append([index(g, x, z) for x in range(2) for z in (low, high)])
    return groups


def stride_groups():
    return [
        [index(g, x, parity + 2 * j) for j in range(4)]
        for g in range(16)
        for x in range(2)
        for parity in range(2)
    ]


def split(value):
    high = value.astype(jnp.bfloat16)
    return high, (value - high.astype(jnp.float32)).astype(jnp.bfloat16)


def passes(left, right, right_dim=0):
    def one(a, b):
        return lax.dot_general(
            a, b, (((1,), (right_dim,)), ((), ())), preferred_element_type=jnp.float32
        )

    total = one(left[1], right[0])
    if right[1] is not None:
        total = total + one(left[0], right[1])
    return total + one(left[0], right[0])


def times(left, right, right_dim=0):
    return passes(split(left), split(right), right_dim)


def signs(labels):
    spread = jnp.broadcast_to(labels.astype(jnp.float32), (RANK, LEAF)).T
    lane = lax.broadcasted_iota(jnp.int32, (LEAF, RANK), 1).astype(jnp.float32)
    halves = [jnp.where(spread == lane + RANK * h, 1.0, -1.0) for h in range(2)]
    return jnp.concatenate(halves, axis=1).astype(jnp.float32)


def as_tiles(projection):
    return projection.T.reshape(16, 16, RANK)


def place_of():
    leaf, core = lax.axis_index("leaf"), lax.axis_index("grp") % 2
    x, z = leaf // 8, leaf % 8
    return x, z, (z + core) % 2


def cut_kernel(capacitance, solved, basis, *pieces):
    x, z, _ = place_of()
    lifted = times(solved[...].T, basis[...])
    for q in range(4):
        first = ((x + q // 2) % 2) * 8 + (z + q) % 2
        for j in range(4):
            start = pl.multiple_of((first + 2 * j) * RANK, RANK)
            pieces[q][:, j * RANK : (j + 1) * RANK] = capacitance[:, pl.ds(start, RANK)]
        pieces[q][:, 4 * RANK :] = lifted


def first_kernel(labels, inverse, basis, top, local, coeffs, projection):
    sign = signs(labels[...])
    found = passes(split(inverse[...]), (sign.astype(jnp.bfloat16), None))
    local[...] = found
    parts = split(found)
    coeffs[...] = passes(split(basis[...].T), parts)
    projection[...] = passes(split(top[...].T), parts)


def stack_coeffs(pieces, stacked):
    step = (lax.axis_index("leaf") % 8) // 2
    for k in range(4):
        start = pl.multiple_of(((step + k) % 4) * RANK, RANK)
        stacked[pl.ds(start, RANK), :] = pieces[k][...]


def row_start(q):
    x, _, low = place_of()
    return pl.multiple_of((((x + q // 2) % 2) * 2 + (low + q) % 2) * RANK, RANK)


def group_kernel(*refs):
    blocks, pieces, (projection, partial, tiles, stacked) = refs[:4], refs[4:8], refs[8:]
    stack_coeffs(pieces, stacked)
    right = split(stacked[...])
    total = projection[...]
    for q in range(4):
        rows = passes(split(blocks[q][:, : 4 * RANK]), right)
        partial[pl.ds(row_start(q), RANK), :] = rows
        total = total - times(blocks[q][:, 4 * RANK :].T, rows)
    tiles[...] = as_tiles(total)


def later_group_kernel(*refs):
    blocks, pieces, (partial, stacked) = refs[:4], refs[4:8], refs[8:]
    stack_coeffs(pieces, stacked)
    right = split(stacked[...])
    for q in range(4):
        partial[pl.ds(row_start(q), RANK), :] = passes(split(blocks[q][:, : 4 * RANK]), right)


def lift_kernel(*refs):
    blocks, out = refs[:4], refs[4]
    total = times(blocks[0][:, 4 * RANK :].T, blocks[0][:, : 4 * RANK])
    for q in range(1, 4):
        total = total + times(blocks[q][:, 4 * RANK :].T, blocks[q][:, : 4 * RANK])
    out[...] = total.T


def sum_kernel(tiles, out):
    out[...] = jnp.broadcast_to(jnp.sum(tiles[...], axis=0)[None], (16, 16, RANK))


def top_kernel(gathered, capacitance, out):
    wide = jnp.concatenate([gathered[g] for g in range(16)], axis=1)
    share = times(wide, capacitance[...], 1)
    out[...] = jnp.broadcast_to(share[None], (16, 16, RANK))


def inner_kernel(local, solved, coef, inner):
    inner[...] = local[...] - times(solved[...], coef[...])


def solved_of(inner, top_solved, top_coef):
    return inner[...] - times(top_solved[...], top_coef[...].reshape(CLASSES, RANK), 1)


def next_kernel(
    labels, inner, top_solved, top_coef, inverse, basis, top, lift, local, scaled, coeffs, tiles
):
    sign = signs(labels[...])
    moved = sign * solved_of(inner, top_solved, top_coef)
    box = jnp.clip(moved, 0.0, 1.0)
    rest = moved - box
    scaled[...] = rest
    found = times(inverse[...], sign * (1.0 + (box - rest)))
    local[...] = found
    parts = split(found)
    mine = passes(split(basis[...].T), parts)
    coeffs[...] = mine
    tiles[...] = as_tiles(passes(split(top[...].T), parts) - times(lift[...].T, mine))


def last_kernel(labels, inner, top_solved, top_coef, scaled, box_out, scaled_out):
    moved = scaled[...] + signs(labels[...]) * solved_of(inner, top_solved, top_coef)
    box = jnp.clip(moved, 0.0, 1.0)
    box_out[...] = box
    scaled_out[...] = moved - box


def call(kernel, outs, *args, scratch=(), flops=0):
    shapes = [jax.ShapeDtypeStruct(shape, jnp.float32) for shape in outs]
    moved = sum(4 * a.size for a in args) + sum(4 * s.size for s in shapes)
    return pl.pallas_call(
        kernel,
        out_shape=shapes,
        in_specs=[pl.BlockSpec(memory_space=pltpu.VMEM)] * len(args),
        out_specs=[pl.BlockSpec(memory_space=pltpu.VMEM)] * len(outs),
        scratch_shapes=[pltpu.VMEM(shape, jnp.float32) for shape in scratch],
        compiler_params=pltpu.CompilerParams(vmem_limit_bytes=24 * 1024 * 1024),
        cost_estimate=pl.CostEstimate(flops=flops, bytes_accessed=moved, transcendentals=0),
    )(*args)


STACK = (4 * RANK, CLASSES)
WIDE = (LEAF, CLASSES)
TILES = (16, 16, RANK)
COEFFS = (RANK, CLASSES)
UNIT = 6 * RANK * RANK * RANK


def exchange(tiles, axis):
    return lax.all_to_all(tiles, axis, 0, 0, tiled=True)


def scattered(value, groups):
    return lax.psum_scatter(
        value, BOTH, scatter_dimension=0, axis_index_groups=groups, tiled=True
    )


def along_stride(coeffs):
    return [coeffs] + [lax.ppermute(coeffs, BOTH, stride_pairs(k)) for k in range(1, 4)]


def top_solve(tiles, top_capacitance):
    (shares,) = call(sum_kernel, [TILES], exchange(tiles, "leaf"))
    (coefs,) = call(
        top_kernel, [TILES], exchange(shares, "grp"), top_capacitance, flops=16 * UNIT
    )
    return exchange(coefs, "leaf")


def shards(
    labels,
    leaf_inverse,
    leaf_basis,
    leaf_solved,
    group_capacitance,
    top_basis,
    top_solved,
    top_capacitance,
):
    labels = labels.reshape(1, LEAF)
    pieces = call(
        cut_kernel,
        [(RANK, 5 * RANK)] * 4,
        group_capacitance,
        leaf_solved,
        top_basis,
        flops=4 * UNIT,
    )
    blocks = [pieces[0]] + [lax.ppermute(pieces[q], BOTH, square_pairs(q)) for q in range(1, 4)]

    local, coeffs, projection = call(
        first_kernel,
        [WIDE, COEFFS, COEFFS],
        labels,
        leaf_inverse,
        leaf_basis,
        top_basis,
        flops=48 * UNIT,
    )
    partial, tiles = call(
        group_kernel,
        [STACK, TILES],
        *blocks,
        *along_stride(coeffs),
        projection,
        scratch=[STACK],
        flops=40 * UNIT,
    )
    group_coef = scattered(partial, square_groups())
    (lifts,) = call(lift_kernel, [(4 * RANK, RANK)], *blocks, flops=16 * UNIT)
    lift = scattered(lifts, stride_groups())
    top_coef = top_solve(tiles, top_capacitance)
    (inner,) = call(inner_kernel, [WIDE], local, leaf_solved, group_coef, flops=8 * UNIT)

    local, scaled, coeffs, tiles = call(
        next_kernel,
        [WIDE, WIDE, COEFFS, TILES],
        labels,
        inner,
        top_solved,
        top_coef,
        leaf_inverse,
        leaf_basis,
        top_basis,
        lift,
        flops=60 * UNIT,
    )
    (partial,) = call(
        later_group_kernel,
        [STACK],
        *blocks,
        *along_stride(coeffs),
        scratch=[STACK],
        flops=32 * UNIT,
    )
    group_coef = scattered(partial, square_groups())
    top_coef = top_solve(tiles, top_capacitance)
    (inner,) = call(inner_kernel, [WIDE], local, leaf_solved, group_coef, flops=8 * UNIT)
    return tuple(
        call(
            last_kernel,
            [WIDE, WIDE],
            labels,
            inner,
            top_solved,
            top_coef,
            scaled,
            flops=8 * UNIT,
        )
    )


def solution(mesh):
    rows = P(BOTH, None)
    return jax.shard_map(
        shards,
        mesh=mesh,
        in_specs=(P(BOTH), rows, rows, rows, rows, rows, rows, P("grp", None)),
        out_specs=(rows, rows),
        check_vma=False,
    )
```

time: 214 us -> 174 us (0.81)
  blocking collectives: 185 us -> 47.2 us
  starting transfers between devices: 0 us -> 43 us
  waiting for transfers between devices: 0 us -> 42.9 us
  matrix products: 22.5 us -> 0 us
  Pallas kernels: 0 us -> 13.5 us
  between operations: 0.85 us -> 13.9 us
  local copies, waits for them, and re-layouts: 4.79 us -> 13.1 us
    all_to_all x8 -> x3, blocking collectives: 185 us -> 47.2 us  [exchange(): return lax.all_to_all(tiles, axis, 0, 0, tiled=True)]
    dot_general x14 -> x0, matrix products: 22.5 us -> none  [the longest x10 18.6 us: matmul(): jnp.dot(left, right, precision=high, preferred_element_type=jnp.float32)]
    ppermute x0 -> x9, starting transfers between devices: none -> 21.7 us  [the longest x6 18.1 us: along_stride(): lax.ppermute(coeffs, BOTH, stride_pairs(k))]
    all_to_all x0 -> x3, starting transfers between devices: none -> 21.1 us  [exchange(): return lax.all_to_all(tiles, axis, 0, 0, tiled=True)]
    ppermute x0 -> x9, waiting for transfers between devices: none -> 14.5 us  [the longest x6 14.5 us: along_stride(): lax.ppermute(coeffs, BOTH, stride_pairs(k))]
    all_to_all x0 -> x3, waiting for transfers between devices: none -> 14.4 us  [exchange(): return lax.all_to_all(tiles, axis, 0, 0, tiled=True)]
    reduce_scatter x0 -> x3, waiting for transfers between devices: none -> 14 us  [scattered(): lax.psum_scatter(value, BOTH, scatter_dimension=0, axis_index_groups=grou...]
    pallas_call x0 -> x13, Pallas kernels: none -> 13.5 us  [call(): pl.pallas_call(kernel, out_shape=shapes, in_specs=[pl.BlockSpec(memory_sp...]
  transfers between devices with their start and end apart: 0 -> 15, of which waited for: 0 -> 9; matrix products, arithmetic and copies ran while one was open for 0% -> 0% of each run, Pallas kernels for 0% -> 3%
where the time goes in v2:
time: 174 us; the launch traced here: 173 us
  blocking collectives  47.2 us (27%)
  starting transfers between devices  43 us (25%)
  waiting for transfers between devices  42.9 us (25%)
  between operations  13.9 us (8%)
  Pallas kernels  13.5 us (8%)
  local copies, waits for them, and re-layouts  13.1 us (8%)
    all_to_all x3, blocking collectives, exchange(): return lax.all_to_all(tiles, axis, 0, 0, tiled=True)  47.2 us
    all_to_all x3, starting transfers between devices, exchange(): return lax.all_to_all(tiles, axis, 0, 0, tiled=True)  21.1 us
    ppermute x6, starting transfers between devices, along_stride(): lax.ppermute(coeffs, BOTH, stride_pairs(k))  18.1 us
    ppermute x6, waiting for transfers between devices, along_stride(): lax.ppermute(coeffs, BOTH, stride_pairs(k))  14.5 us
    all_to_all x3, waiting for transfers between devices, exchange(): return lax.all_to_all(tiles, axis, 0, 0, tiled=True)  14.4 us
    reduce_scatter x3, waiting for transfers between devices, scattered(): lax.psum_scatter(value, BOTH, scatter_dimension=0, axis_index_groups=grou...  14 us
    pallas_call x13, Pallas kernels, call(): pl.pallas_call(kernel, out_shape=shapes, in_specs=[pl.BlockSpec(memory_sp...  13.5 us
    unnamed x44, local copies, waits for them, and re-layouts  13.1 us
  transfers between devices with their start and end apart: 15, of which 9 were waited for; matrix products, arithmetic and copies ran while one was open for 0% of the time, Pallas kernels for 3%

profile of v2, /device:TPU:32, one launch (start us, length us, event | category | flops | bytes accessed | tf_op | source)
XLA Modules:
  0.0 173.5 jit_solution(13085275392029341246)
XLA Ops:
  7.2 0.9 copy-done.1
  8.2 1.2 copy-done.3
  9.4 0.9 copy-done.8
  10.3 0.4 shard_map.96
  10.7 1.9 %collective-permute-start = (f32[128,640]{1,0:T(8,128)S(1)}, f32[128,640]{1,0:T(8,128)S(1)}, u32[]{:S(2)}, u32[]{:S(2)}) collective-permute-start(f32[128,640]{1,0:T(8,128)S(1)} %get-tuple-element.17), channel_id=1, source_target_pairs={{0,1},{1,0},{2,3},{3,2},{4,5},{5,4},{6,7},{7,6},{8,9},{9,8},{10,11... | collective-permute-start | bytes 983048 | tf_op jit(solution)/shard_map/ppermute | solution.py:259
  12.7 1.6 collective-permute-start.2
  14.3 1.2 shard_map.95
  15.5 3.3 %collective-permute-start.5 = (f32[128,256]{1,0:T(8,128)S(1)}, f32[128,256]{1,0:T(8,128)S(1)}, u32[]{:S(2)}, u32[]{:S(2)}) collective-permute-start(f32[128,256]{1,0:T(8,128)S(1)} %get-tuple-element.20.refs_4_), channel_id=1, source_target_pairs={{0,2},{1,3},{2,4},{3,5},{4,6},{5,7},{6,0},{7,1},{8,10},{9,11},{10,... | collective-permute-start | bytes 393224 | tf_op jit(solution)/shard_map/ppermute | solution.py:229
  18.9 4.5 %collective-permute-start.4 = (f32[128,256]{1,0:T(8,128)S(1)}, f32[128,256]{1,0:T(8,128)S(1)}, u32[]{:S(2)}, u32[]{:S(2)}) collective-permute-start(f32[128,256]{1,0:T(8,128)S(1)} %get-tuple-element.20.refs_4_), channel_id=1, source_target_pairs={{0,4},{1,5},{2,6},{3,7},{4,0},{5,1},{6,2},{7,3},{8,12},{9,13},{10,... | collective-permute-start | bytes 393224 | tf_op jit(solution)/shard_map/ppermute | solution.py:229
  23.4 4.0 %collective-permute-done.5.refs_7_ = f32[128,256]{1,0:T(8,128)S(1)} collective-permute-done((f32[128,256]{1,0:T(8,128)S(1)}, f32[128,256]{1,0:T(8,128)S(1)}, u32[]{:S(2)}, u32[]{:S(2)}) %collective-permute-start.5) | collective-permute-done | bytes 131104 | tf_op jit(solution)/shard_map/ppermute | solution.py:229
  27.4 2.9 %collective-permute-start.3 = (f32[128,256]{1,0:T(8,128)S(1)}, f32[128,256]{1,0:T(8,128)S(1)}, u32[]{:S(2)}, u32[]{:S(2)}) collective-permute-start(f32[128,256]{1,0:T(8,128)S(1)} %get-tuple-element.20.refs_4_), channel_id=1, source_target_pairs={{0,6},{1,7},{2,0},{3,1},{4,2},{5,3},{6,4},{7,5},{8,14},{9,15},{10,... | collective-permute-start | bytes 393224 | tf_op jit(solution)/shard_map/ppermute | solution.py:229
  30.3 3.2 %collective-permute-done.4.refs_6_ = f32[128,256]{1,0:T(8,128)S(1)} collective-permute-done((f32[128,256]{1,0:T(8,128)S(1)}, f32[128,256]{1,0:T(8,128)S(1)}, u32[]{:S(2)}, u32[]{:S(2)}) %collective-permute-start.4) | collective-permute-done | bytes 131104 | tf_op jit(solution)/shard_map/ppermute | solution.py:229
  33.5 1.0 collective-permute-done.3.refs_5_
  34.6 2.4 %shard_map.97 = (f32[512,256]{1,0:T(8,128)}, f32[16,16,128]{2,1,0:T(8,128)}) custom-call(f32[128,640]{1,0:T(8,128)S(1)} %get-tuple-element.16.refs_0_, f32[128,640]{1,0:T(8,128)S(1)} %collective-permute-done.refs_1_, f32[128,640]{1,0:T(8,128)S(1)} %collective-permute-done.1.refs_2_, f32[128,640]{1,0:T(8,128)S(1)} %collective-permute-done.2.refs_3_, ...), custom_call_target="tpu_custom_call" | custom-call | flops 503316480 | bytes 2621440 | tf_op jit(solution)/shard_map/pallas_call | solution.py:200
  37.0 12.2 %all-to-all-start = ((f32[16,16,128]{2,1,0:T(8,128)}), f32[16,16,128]{2,1,0:T(8,128)S(1)}, u32[]{:S(2)}, u32[]{:S(2)}) async-start(f32[16,16,128]{2,1,0:T(8,128)} %get-tuple-element.23), calls=%async_computation.1 | async-start | bytes 262144 | tf_op jit(solution)/shard_map/all_to_all | solution.py:219
  49.2 1.4 shard_map.101
  50.7 7.4 %all-to-all-done.tiles = f32[16,16,128]{2,1,0:T(8,128)S(1)} async-done(((f32[16,16,128]{2,1,0:T(8,128)}), f32[16,16,128]{2,1,0:T(8,128)S(1)}, u32[]{:S(2)}, u32[]{:S(2)}) %all-to-all-start) | async-done | bytes 131104 | tf_op jit(solution)/shard_map/all_to_all | solution.py:219
  58.1 14.7 %all_to_all.30.gathered = f32[16,16,128]{2,1,0:T(8,128)S(1)} all-to-all(f32[16,16,128]{2,1,0:T(8,128)S(1)} %shard_map.99), channel_id=1, replica_groups=mesh['grp'=16,'leaf'=16] {'grp'}, dimensions={0} | all-to-all | bytes 262144 | tf_op jit(solution)/shard_map/all_to_all | solution.py:219
  72.9 1.2 shard_map.100
  74.0 4.7 %all-to-all-start.2 = ((f32[16,16,128]{2,1,0:T(8,128)}), f32[16,16,128]{2,1,0:T(8,128)S(1)}, u32[]{:S(2)}, u32[]{:S(2)}) async-start(f32[16,16,128]{2,1,0:T(8,128)} %shard_map.100), calls=%async_computation.3 | async-start | bytes 262144 | tf_op jit(solution)/shard_map/all_to_all | solution.py:219
  78.9 0.9 copy-done.14
  79.8 0.4 shard_map.98.inner
  80.2 0.8 copy-done.6
  80.9 13.9 %reduce-scatter.6.cloned.1.call-done.lift = f32[128,128]{1,0:T(8,128)} async-done(((f32[512,128]{1,0:T(8,128)}), f32[128,128]{1,0:T(8,128)}) %reduce-scatter.6.cloned.1.call-update) | async-done | bytes 65552 | tf_op jit(solution)/shard_map/reduce_scatter | solution.py:223
  94.9 0.7 copy-done.12
  95.5 1.0 copy-done.7
  96.6 0.9 copy-done.10
  97.5 0.9 copy-done.13
  98.4 1.2 copy-done.18
  99.7 0.9 copy-done.20
  100.6 0.8 copy-done.21
  101.5 2.1 %shard_map.102 = (f32[512,256]{1,0:T(8,128)S(1)}, f32[512,256]{1,0:T(8,128)S(1)}, f32[128,256]{1,0:T(8,128)S(1)}, f32[16,16,128]{2,1,0:T(8,128)S(1)}) custom-call(s32[1,512]{1,0:T(1,128)S(1)} %bitcast.2, f32[512,256]{1,0:T(8,128)S(1)} %copy-done.7, f32[512,128]{1,0:T(8,128)S(1)} %copy-done.10, f32[16,16,128]{2,1,0:T(8,128)S(1)} %copy-done.13, ...), custom_call_target="tpu_custom_call" | custom-call | flops 754974720 | bytes 3868672 | tf_op jit(solution)/shard_map/pallas_call | solution.py:200
  103.6 0.8 copy-done.4
  104.4 2.5 %collective-permute-start.8 = (f32[128,256]{1,0:T(8,128)S(1)}, f32[128,256]{1,0:T(8,128)S(1)}, u32[]{:S(2)}, u32[]{:S(2)}) collective-permute-start(f32[128,256]{1,0:T(8,128)S(1)} %get-tuple-element.25.refs_4_), channel_id=1, source_target_pairs={{0,2},{1,3},{2,4},{3,5},{4,6},{5,7},{6,0},{7,1},{8,10},{9,11},{10,... | collective-permute-start | bytes 393224 | tf_op jit(solution)/shard_map/ppermute | solution.py:229
  106.9 2.3 %collective-permute-start.7 = (f32[128,256]{1,0:T(8,128)S(1)}, f32[128,256]{1,0:T(8,128)S(1)}, u32[]{:S(2)}, u32[]{:S(2)}) collective-permute-start(f32[128,256]{1,0:T(8,128)S(1)} %get-tuple-element.25.refs_4_), channel_id=1, source_target_pairs={{0,4},{1,5},{2,6},{3,7},{4,0},{5,1},{6,2},{7,3},{8,12},{9,13},{10,... | collective-permute-start | bytes 393224 | tf_op jit(solution)/shard_map/ppermute | solution.py:229
  109.2 2.6 %collective-permute-start.6 = (f32[128,256]{1,0:T(8,128)S(1)}, f32[128,256]{1,0:T(8,128)S(1)}, u32[]{:S(2)}, u32[]{:S(2)}) collective-permute-start(f32[128,256]{1,0:T(8,128)S(1)} %get-tuple-element.25.refs_4_), channel_id=1, source_target_pairs={{0,6},{1,7},{2,0},{3,1},{4,2},{5,3},{6,4},{7,5},{8,14},{9,15},{10,... | collective-permute-start | bytes 393224 | tf_op jit(solution)/shard_map/ppermute | solution.py:229
  111.7 0.5 collective-permute-done.8.refs_7_
  112.2 5.6 %collective-permute-done.7.refs_6_ = f32[128,256]{1,0:T(8,128)S(1)} collective-permute-done((f32[128,256]{1,0:T(8,128)S(1)}, f32[128,256]{1,0:T(8,128)S(1)}, u32[]{:S(2)}, u32[]{:S(2)}) %collective-permute-start.7) | collective-permute-done | bytes 131104 | tf_op jit(solution)/shard_map/ppermute | solution.py:229
  117.8 0.2 collective-permute-done.6.refs_5_
  118.0 1.5 shard_map.103
  119.4 18.0 %all_to_all.31.tiles = f32[16,16,128]{2,1,0:T(8,128)S(1)} all-to-all(f32[16,16,128]{2,1,0:T(8,128)S(1)} %get-tuple-element.26), channel_id=1, replica_groups=mesh['grp'=16,'leaf'=16] {'leaf'}, dimensions={0} | all-to-all | bytes 262144 | tf_op jit(solution)/shard_map/all_to_all | solution.py:219
  137.5 14.4 %all_to_all.32.gathered = f32[16,16,128]{2,1,0:T(8,128)S(1)} all-to-all(f32[16,16,128]{2,1,0:T(8,128)S(1)} %shard_map.105), channel_id=1, replica_groups=mesh['grp'=16,'leaf'=16] {'grp'}, dimensions={0} | all-to-all | bytes 262144 | tf_op jit(solution)/shard_map/all_to_all | solution.py:219
  151.9 1.2 shard_map.106
  153.1 4.2 %all-to-all-start.5 = ((f32[16,16,128]{2,1,0:T(8,128)}), f32[16,16,128]{2,1,0:T(8,128)S(1)}, u32[]{:S(2)}, u32[]{:S(2)}) async-start(f32[16,16,128]{2,1,0:T(8,128)} %shard_map.106), calls=%async_computation.8 | async-start | bytes 262144 | tf_op jit(solution)/shard_map/all_to_all | solution.py:219
  157.4 0.9 copy-done.15
  158.3 0.4 shard_map.104.inner
  158.7 6.9 %all-to-all-done.5.top_coef = f32[16,16,128]{2,1,0:T(8,128)S(1)} async-done(((f32[16,16,128]{2,1,0:T(8,128)}), f32[16,16,128]{2,1,0:T(8,128)S(1)}, u32[]{:S(2)}, u32[]{:S(2)}) %all-to-all-start.5) | async-done | bytes 131104 | tf_op jit(solution)/shard_map/all_to_all | solution.py:219
  165.6 1.4 shard_map.107
  (45 shorter events, 0.3 us)
Async XLA Ops:
  7.2 71.7 %reduce-scatter.4.cloned.1.call-start = ((), (), s32[]{:S(2)}) async-start(), calls=%async_computation.9 | async-start | bytes 655360 | tf_op jit(solution)/shard_map/reduce_scatter | solution.py:223
  7.2 1.0 copy-start.1
  8.2 1.2 copy-start.3
  9.4 0.9 copy-start.8
  10.3 4.0 %copy-start.9 = (f32[512,128]{1,0:T(8,128)S(1)}, f32[512,128]{1,0:T(8,128)}, u32[]{:S(2)}) copy-start(f32[512,128]{1,0:T(8,128)} %top.3) | copy-start | bytes 786436
  10.3 4.0 %copy-start.17 = (f32[512,512]{1,0:T(8,128)S(1)}, f32[512,512]{1,0:T(8,128)}, u32[]{:S(2)}) copy-start(f32[512,512]{1,0:T(8,128)} %inverse.3) | copy-start | bytes 3145732
  10.3 4.0 %copy-start.19 = (f32[512,128]{1,0:T(8,128)S(1)}, f32[512,128]{1,0:T(8,128)}, u32[]{:S(2)}) copy-start(f32[512,128]{1,0:T(8,128)} %basis.5) | copy-start | bytes 786436
  10.7 23.8 %collective-permute-start = (f32[128,640]{1,0:T(8,128)S(1)}, f32[128,640]{1,0:T(8,128)S(1)}, u32[]{:S(2)}, u32[]{:S(2)}) collective-permute-start(f32[128,640]{1,0:T(8,128)S(1)} %get-tuple-element.17), channel_id=1, source_target_pairs={{0,1},{1,0},{2,3},{3,2},{4,5},{5,4},{6,7},{7,6},{8,9},{9,8},{10,11... | collective-permute-start | bytes 983048 | tf_op jit(solution)/shard_map/ppermute | solution.py:259
  12.7 1.7 copy-start.16
  12.7 21.9 %collective-permute-start.1 = (f32[128,640]{1,0:T(8,128)S(1)}, f32[128,640]{1,0:T(8,128)S(1)}, u32[]{:S(2)}, u32[]{:S(2)}) collective-permute-start(f32[128,640]{1,0:T(8,128)S(1)} %get-tuple-element.18), channel_id=1, source_target_pairs={{0,8},{1,9},{2,10},{3,11},{4,12},{5,13},{6,14},{7,15},{8,0},{9,1},... | collective-permute-start | bytes 983048 | tf_op jit(solution)/shard_map/ppermute | solution.py:259
  12.7 21.9 %collective-permute-start.2 = (f32[128,640]{1,0:T(8,128)S(1)}, f32[128,640]{1,0:T(8,128)S(1)}, u32[]{:S(2)}, u32[]{:S(2)}) collective-permute-start(f32[128,640]{1,0:T(8,128)S(1)} %get-tuple-element.19), channel_id=1, source_target_pairs={{0,9},{1,8},{2,11},{3,10},{4,13},{5,12},{6,15},{7,14},{8,1},{9,0},... | collective-permute-start | bytes 983048 | tf_op jit(solution)/shard_map/ppermute | solution.py:259
  15.5 11.9 %collective-permute-start.5 = (f32[128,256]{1,0:T(8,128)S(1)}, f32[128,256]{1,0:T(8,128)S(1)}, u32[]{:S(2)}, u32[]{:S(2)}) collective-permute-start(f32[128,256]{1,0:T(8,128)S(1)} %get-tuple-element.20.refs_4_), channel_id=1, source_target_pairs={{0,2},{1,3},{2,4},{3,5},{4,6},{5,7},{6,0},{7,1},{8,10},{9,11},{10,... | collective-permute-start | bytes 393224 | tf_op jit(solution)/shard_map/ppermute | solution.py:229
  18.9 14.6 %collective-permute-start.4 = (f32[128,256]{1,0:T(8,128)S(1)}, f32[128,256]{1,0:T(8,128)S(1)}, u32[]{:S(2)}, u32[]{:S(2)}) collective-permute-start(f32[128,256]{1,0:T(8,128)S(1)} %get-tuple-element.20.refs_4_), channel_id=1, source_target_pairs={{0,4},{1,5},{2,6},{3,7},{4,0},{5,1},{6,2},{7,3},{8,12},{9,13},{10,... | collective-permute-start | bytes 393224 | tf_op jit(solution)/shard_map/ppermute | solution.py:229
  27.4 7.2 %collective-permute-start.3 = (f32[128,256]{1,0:T(8,128)S(1)}, f32[128,256]{1,0:T(8,128)S(1)}, u32[]{:S(2)}, u32[]{:S(2)}) collective-permute-start(f32[128,256]{1,0:T(8,128)S(1)} %get-tuple-element.20.refs_4_), channel_id=1, source_target_pairs={{0,6},{1,7},{2,0},{3,1},{4,2},{5,3},{6,4},{7,5},{8,14},{9,15},{10,... | collective-permute-start | bytes 393224 | tf_op jit(solution)/shard_map/ppermute | solution.py:229
  37.0 21.1 %all-to-all-start = ((f32[16,16,128]{2,1,0:T(8,128)}), f32[16,16,128]{2,1,0:T(8,128)S(1)}, u32[]{:S(2)}, u32[]{:S(2)}) async-start(f32[16,16,128]{2,1,0:T(8,128)} %get-tuple-element.23), calls=%async_computation.1 | async-start | bytes 262144 | tf_op jit(solution)/shard_map/all_to_all | solution.py:219
  49.2 23.7 %copy-start = (f32[128,2048]{1,0:T(8,128)S(1)}, f32[128,2048]{1,0:T(8,128)}, u32[]{:S(2)}) copy-start(f32[128,2048]{1,0:T(8,128)} %capacitance.5) | copy-start | bytes 3145732
  49.2 45.7 %reduce-scatter.6.cloned.1.call-start = ((), (), s32[]{:S(2)}) async-start(), calls=%async_computation.10 | async-start | bytes 327680 | tf_op jit(solution)/shard_map/reduce_scatter | solution.py:223
  74.0 4.8 %copy-start.2 = (f32[512,128]{1,0:T(8,128)S(1)}, f32[512,128]{1,0:T(8,128)}, u32[]{:S(2)}) copy-start(f32[512,128]{1,0:T(8,128)} %solved.5) | copy-start | bytes 786436
  74.0 20.8 %all-to-all-start.2 = ((f32[16,16,128]{2,1,0:T(8,128)}), f32[16,16,128]{2,1,0:T(8,128)S(1)}, u32[]{:S(2)}, u32[]{:S(2)}) async-start(f32[16,16,128]{2,1,0:T(8,128)} %shard_map.100), calls=%async_computation.3 | async-start | bytes 262144 | tf_op jit(solution)/shard_map/all_to_all | solution.py:219
  78.8 78.6 %reduce-scatter.8.cloned.1.call-start = ((), (), s32[]{:S(2)}) async-start(), calls=%async_computation.11 | async-start | bytes 655360 | tf_op jit(solution)/shard_map/reduce_scatter | solution.py:223
  78.9 0.9 copy-start.14
  80.1 0.8 copy-start.6
  94.9 0.7 copy-start.12
  95.5 1.0 copy-start.7
  96.6 0.9 copy-start.10
  97.5 0.9 copy-start.13
  98.4 1.2 copy-start.18
  99.7 0.9 copy-start.20
  100.6 0.8 copy-start.21
  103.6 0.8 copy-start.4
  104.4 7.9 %collective-permute-start.8 = (f32[128,256]{1,0:T(8,128)S(1)}, f32[128,256]{1,0:T(8,128)S(1)}, u32[]{:S(2)}, u32[]{:S(2)}) collective-permute-start(f32[128,256]{1,0:T(8,128)S(1)} %get-tuple-element.25.refs_4_), channel_id=1, source_target_pairs={{0,2},{1,3},{2,4},{3,5},{4,6},{5,7},{6,0},{7,1},{8,10},{9,11},{10,... | collective-permute-start | bytes 393224 | tf_op jit(solution)/shard_map/ppermute | solution.py:229
  106.9 10.9 %collective-permute-start.7 = (f32[128,256]{1,0:T(8,128)S(1)}, f32[128,256]{1,0:T(8,128)S(1)}, u32[]{:S(2)}, u32[]{:S(2)}) collective-permute-start(f32[128,256]{1,0:T(8,128)S(1)} %get-tuple-element.25.refs_4_), channel_id=1, source_target_pairs={{0,4},{1,5},{2,6},{3,7},{4,0},{5,1},{6,2},{7,3},{8,12},{9,13},{10,... | collective-permute-start | bytes 393224 | tf_op jit(solution)/shard_map/ppermute | solution.py:229
  109.2 8.8 %collective-permute-start.6 = (f32[128,256]{1,0:T(8,128)S(1)}, f32[128,256]{1,0:T(8,128)S(1)}, u32[]{:S(2)}, u32[]{:S(2)}) collective-permute-start(f32[128,256]{1,0:T(8,128)S(1)} %get-tuple-element.25.refs_4_), channel_id=1, source_target_pairs={{0,6},{1,7},{2,0},{3,1},{4,2},{5,3},{6,4},{7,5},{8,14},{9,15},{10,... | collective-permute-start | bytes 393224 | tf_op jit(solution)/shard_map/ppermute | solution.py:229
  151.9 5.5 %copy-start.5 = (f32[512,256]{1,0:T(8,128)S(1)}, f32[512,256]{1,0:T(8,128)}, u32[]{:S(2)}) copy-start(f32[512,256]{1,0:T(8,128)} %copy-done.4) | copy-start | bytes 1572868
  153.1 12.5 %all-to-all-start.5 = ((f32[16,16,128]{2,1,0:T(8,128)}), f32[16,16,128]{2,1,0:T(8,128)S(1)}, u32[]{:S(2)}, u32[]{:S(2)}) async-start(f32[16,16,128]{2,1,0:T(8,128)} %shard_map.106), calls=%async_computation.8 | async-start | bytes 262144 | tf_op jit(solution)/shard_map/all_to_all | solution.py:219
  157.4 0.9 copy-start.15
  158.3 7.3 %copy-start.11 = (f32[512,128]{1,0:T(8,128)S(1)}, f32[512,128]{1,0:T(8,128)}, u32[]{:S(2)}) copy-start(f32[512,128]{1,0:T(8,128)} %top_solved.3) | copy-start | bytes 786436
Sparse Core Ops, SparseCore 0:
  37.1 29.0 reduce-scatter.3
  69.3 25.5 reduce-scatter.5
  119.6 25.6 reduce-scatter.7

commit v3 on v2

v3 whole, which is shorter than its diff:
```python
import functools

import jax
import jax.numpy as jnp
from jax import lax
from jax.experimental import pallas as pl
from jax.experimental.pallas import tpu as pltpu
from jax.sharding import PartitionSpec as P

CLASSES = 256
RANK = 128
LEAF = 512
BOTH = ("grp", "leaf")


def partner(core, z):
    return (((z + core) ^ 1) - core) % 8


def devices():
    return [(g, i // 8, i % 8) for g in range(16) for i in range(16)]


def index(g, x, z):
    return g * 16 + x * 8 + z


def square_pairs(q):
    pairs = []
    for g, x, z in devices():
        other = index(g, x ^ (q // 2), partner(g % 2, z) if q % 2 else z)
        pairs.append((index(g, x, z), other))
    return pairs


def mirrored_pairs(k):
    sign = (1, -1)
    return [
        (index(g, x, z), index(g, x, (z + 2 * k * sign[g % 2]) % 8)) for g, x, z in devices()
    ]


def split(value):
    high = value.astype(jnp.bfloat16)
    return high, (value - high.astype(jnp.float32)).astype(jnp.bfloat16)


def passes(left, right, right_dim=0):
    def one(a, b):
        return lax.dot_general(
            a, b, (((1,), (right_dim,)), ((), ())), preferred_element_type=jnp.float32
        )

    total = one(left[1], right[0])
    if right[1] is not None:
        total = total + one(left[0], right[1])
    return total + one(left[0], right[0])


def times(left, right, right_dim=0):
    return passes(split(left), split(right), right_dim)


def signs(labels):
    spread = jnp.broadcast_to(labels.astype(jnp.float32), (RANK, LEAF)).T
    lane = lax.broadcasted_iota(jnp.int32, (LEAF, RANK), 1).astype(jnp.float32)
    halves = [jnp.where(spread == lane + RANK * h, 1.0, -1.0) for h in range(2)]
    return jnp.concatenate(halves, axis=1).astype(jnp.float32)


def cut_kernel(capacitance, *refs):
    pieces, done = refs[:4], refs[4]
    leaf = lax.axis_index("leaf")
    x, z = leaf // 8, leaf % 8
    copies = []
    for q in (3, 2, 1, 0):
        first = ((x + q // 2) % 2) * 8 + (z + q) % 2
        for j in range(4):
            start = pl.multiple_of((first + 2 * j) * RANK, RANK)
            copies.append(
                pltpu.make_async_copy(
                    capacitance.at[:, pl.ds(start, RANK)],
                    pieces[q].at[:, j * RANK : (j + 1) * RANK],
                    done.at[4 * q + j],
                )
            )
            copies[-1].start()
    for copy in copies:
        copy.wait()


def first_kernel(labels, inverse, basis, local, coeffs):
    sign = signs(labels[...])
    found = passes(split(inverse[...]), (sign.astype(jnp.bfloat16), None))
    local[...] = found
    coeffs[...] = times(basis[...].T, found)


def row_of(k):
    sign = 1 - 2 * (lax.axis_index("grp") % 2)
    step = (lax.axis_index("leaf") % 8) // 2
    return pl.ds(pl.multiple_of(((step + k * sign + 4) % 4) * RANK, RANK), RANK)


def group_kernel(*refs):
    blocks, pieces, partials, stacked = refs[:4], refs[4:8], refs[8:12], refs[12]
    for piece, k in zip(pieces, (0, -1, 1, 2)):
        stacked[row_of(k), :] = piece[...]
    right = split(stacked[...])
    for q in range(4):
        partials[q][...] = passes(split(blocks[q][...]), right)


def inner_kernel(local, solved, top, *refs):
    parts, inner, tiles = refs[:4], refs[4], refs[5]
    coef = (parts[0][...] + parts[1][...]) + (parts[2][...] + parts[3][...])
    found = local[...] - times(solved[...], coef)
    inner[...] = found
    tiles[...] = times(top[...].T, found).T.reshape(16, 16, RANK)


def sum_kernel(tiles, out):
    out[...] = jnp.broadcast_to(jnp.sum(tiles[...], axis=0)[None], (16, 16, RANK))


def top_kernel(gathered, capacitance, out):
    wide = jnp.concatenate([gathered[g] for g in range(16)], axis=1)
    share = times(wide, capacitance[...], 1)
    out[...] = jnp.broadcast_to(share[None], (16, 16, RANK))


def solved_of(inner, top_solved, top_coef):
    return inner[...] - times(top_solved[...], top_coef[...].reshape(CLASSES, RANK), 1)


def next_kernel(
    inner, top_coef, labels, top_solved, inverse, basis, local, scaled, coeffs
):
    sign = signs(labels[...])
    moved = sign * solved_of(inner, top_solved, top_coef)
    box = jnp.clip(moved, 0.0, 1.0)
    rest = moved - box
    scaled[...] = rest
    found = times(inverse[...], sign * (1.0 + (box - rest)))
    local[...] = found
    coeffs[...] = times(basis[...].T, found)


def last_kernel(inner, top_coef, scaled, labels, top_solved, box_out, scaled_out):
    moved = scaled[...] + signs(labels[...]) * solved_of(inner, top_solved, top_coef)
    box = jnp.clip(moved, 0.0, 1.0)
    box_out[...] = box
    scaled_out[...] = moved - box


def call(kernel, outs, args, scratch=(), flops=0):
    shapes = [jax.ShapeDtypeStruct(shape, jnp.float32) for shape in outs]
    moved = sum(4 * a.size for a in args) + sum(4 * s.size for s in shapes)
    return pl.pallas_call(
        kernel,
        out_shape=shapes,
        in_specs=[pl.BlockSpec(memory_space=pltpu.VMEM)] * len(args),
        out_specs=[pl.BlockSpec(memory_space=pltpu.VMEM)] * len(outs),
        scratch_shapes=[pltpu.VMEM(shape, jnp.float32) for shape in scratch],
        compiler_params=pltpu.CompilerParams(vmem_limit_bytes=16 * 1024 * 1024),
        cost_estimate=pl.CostEstimate(flops=flops, bytes_accessed=moved, transcendentals=0),
    )(*args)


STACK = (4 * RANK, CLASSES)
WIDE = (LEAF, CLASSES)
TILES = (16, 16, RANK)
COEFFS = (RANK, CLASSES)
UNIT = 6 * RANK * RANK * RANK


def exchange(tiles, axis):
    return lax.all_to_all(tiles, axis, 0, 0, tiled=True)


def across_square(pieces):
    return [pieces[0]] + [lax.ppermute(pieces[q], BOTH, square_pairs(q)) for q in range(1, 4)]


def relayed(coeffs):
    before = lax.ppermute(coeffs, BOTH, mirrored_pairs(1))
    after = lax.ppermute(coeffs, BOTH, mirrored_pairs(-1))
    opposite = lax.ppermute(before, BOTH, mirrored_pairs(1))
    return [coeffs, before, after, opposite]


def iteration(local, coeffs, blocks, leaf_solved, top_basis, top_capacitance):
    partials = call(
        group_kernel,
        [COEFFS] * 4,
        [*blocks, *relayed(coeffs)],
        scratch=[STACK],
        flops=32 * UNIT,
    )
    inner, tiles = call(
        inner_kernel,
        [WIDE, TILES],
        [local, leaf_solved, top_basis, *across_square(partials)],
        flops=16 * UNIT,
    )
    (shares,) = call(sum_kernel, [TILES], [exchange(tiles, "leaf")])
    (coefs,) = call(
        top_kernel, [TILES], [exchange(shares, "grp"), top_capacitance], flops=16 * UNIT
    )
    return inner, exchange(coefs, "leaf")


def shards(
    labels,
    leaf_inverse,
    leaf_basis,
    leaf_solved,
    group_capacitance,
    top_basis,
    top_solved,
    top_capacitance,
):
    labels = labels.reshape(1, LEAF)
    pieces = pl.pallas_call(
        cut_kernel,
        out_shape=[jax.ShapeDtypeStruct((RANK, 4 * RANK), jnp.float32)] * 4,
        in_specs=[pl.BlockSpec(memory_space=pl.ANY)],
        out_specs=[pl.BlockSpec(memory_space=pl.ANY)] * 4,
        scratch_shapes=[pltpu.SemaphoreType.DMA((16,))],
        compiler_params=pltpu.CompilerParams(vmem_limit_bytes=16 * 1024 * 1024),
    )(group_capacitance)
    blocks = across_square(pieces)
    local, coeffs = call(
        first_kernel,
        [WIDE, COEFFS],
        [labels, leaf_inverse, leaf_basis],
        flops=40 * UNIT,
    )
    shared = (blocks, leaf_solved, top_basis, top_capacitance)
    inner, top_coef = iteration(local, coeffs, *shared)
    local, scaled, coeffs = call(
        next_kernel,
        [WIDE, WIDE, COEFFS],
        [inner, top_coef, labels, top_solved, leaf_inverse, leaf_basis],
        flops=56 * UNIT,
    )
    inner, top_coef = iteration(local, coeffs, *shared)
    return tuple(
        call(
            last_kernel, [WIDE, WIDE], [inner, top_coef, scaled, labels, top_solved], flops=8 * UNIT
        )
    )


def solution(mesh):
    rows = P(BOTH, None)
    return jax.shard_map(
        shards,
        mesh=mesh,
        in_specs=(P(BOTH), rows, rows, rows, rows, rows, rows, P("grp", None)),
        out_specs=(rows, rows),
        check_vma=False,
    )
```

time: 174 us -> 146 us (0.84)
  blocking collectives: 47.2 us -> 77.4 us
  starting transfers between devices: 43 us -> 22.8 us
  between operations: 13.9 us -> 0.82 us
  local copies, waits for them, and re-layouts: 13.1 us -> 2.98 us
  waiting for transfers between devices: 42.9 us -> 32.9 us
  Pallas kernels: 13.5 us -> 8.5 us
    all_to_all x3 -> x6, blocking collectives: 47.2 us -> 77.4 us  [exchange(): return lax.all_to_all(tiles, axis, 0, 0, tiled=True)]
    all_to_all x3 -> x0, starting transfers between devices: 21.1 us -> none  [exchange(): return lax.all_to_all(tiles, axis, 0, 0, tiled=True)]
    ppermute x9 -> x15, waiting for transfers between devices: 14.5 us -> 32.9 us  [the longest x2 9.59 us: relayed(): opposite = lax.ppermute(before, BOTH, mirrored_pairs(1))]
    all_to_all x3 -> x0, waiting for transfers between devices: 14.4 us -> none  [exchange(): return lax.all_to_all(tiles, axis, 0, 0, tiled=True)]
    reduce_scatter x3 -> x0, waiting for transfers between devices: 14 us -> none  [scattered(): lax.psum_scatter(value, BOTH, scatter_dimension=0, axis_index_groups=grou...]
    unnamed x44 -> x22, local copies, waits for them, and re-layouts: 13.1 us -> 2.98 us
    pallas_call x13 -> x11, Pallas kernels: 13.5 us -> 8.14 us  [call(): pl.pallas_call(kernel, out_shape=shapes, in_specs=[pl.BlockSpec(memory_sp...]
    ppermute x9 -> x15, starting transfers between devices: 21.7 us -> 22.8 us  [the longest x9 10.7 us: across_square(): lax.ppermute(pieces[q], BOTH, square_pairs(q))]
  transfers between devices with their start and end apart: 15 -> 15, of which waited for: 9 -> 10; matrix products, arithmetic and copies ran while one was open for 0% -> 0% of each run, Pallas kernels for 3% -> 0%
where the time goes in v3:
time: 146 us; the launch traced here: 145 us
  blocking collectives  77.4 us (53%)
  waiting for transfers between devices  32.9 us (23%)
  starting transfers between devices  22.8 us (16%)
  Pallas kernels  8.5 us (6%)
  local copies, waits for them, and re-layouts  2.98 us (2%)
    all_to_all x6, blocking collectives, exchange(): return lax.all_to_all(tiles, axis, 0, 0, tiled=True)  77.4 us
    ppermute x9, starting transfers between devices, across_square(): lax.ppermute(pieces[q], BOTH, square_pairs(q))  10.7 us
    ppermute x2, waiting for transfers between devices, relayed(): opposite = lax.ppermute(before, BOTH, mirrored_pairs(1))  9.59 us
    ppermute x2, waiting for transfers between devices, relayed(): after = lax.ppermute(coeffs, BOTH, mirrored_pairs(-1))  9.03 us
    pallas_call x11, Pallas kernels, call(): pl.pallas_call(kernel, out_shape=shapes, in_specs=[pl.BlockSpec(memory_sp...  8.14 us
    ppermute x9, waiting for transfers between devices, across_square(): lax.ppermute(pieces[q], BOTH, square_pairs(q))  7.77 us
    ppermute x2, waiting for transfers between devices, relayed(): before = lax.ppermute(coeffs, BOTH, mirrored_pairs(1))  6.51 us
    ppermute x2, starting transfers between devices, relayed(): after = lax.ppermute(coeffs, BOTH, mirrored_pairs(-1))  5.66 us
  transfers between devices with their start and end apart: 15, of which 10 were waited for; matrix products, arithmetic and copies ran while one was open for 0% of the time, Pallas kernels for 0%

profile of v3, /device:TPU:32, one launch (start us, length us, event | category | flops | bytes accessed | tf_op | source)
XLA Modules:
  0.0 145.4 jit_solution(390151896066002192)
XLA Ops:
  0.6 0.0 copy-start.5
  0.7 0.8 copy-done.5
  1.4 1.2 copy-done.7
  2.6 0.9 copy-done.9
  3.6 0.9 shard_map.95
  4.5 3.4 %collective-permute-start.3 = (f32[128,256]{1,0:T(8,128)S(1)}, f32[128,256]{1,0:T(8,128)S(1)}, u32[]{:S(2)}, u32[]{:S(2)}) collective-permute-start(f32[128,256]{1,0:T(8,128)S(1)} %get-tuple-element.28.refs_4_), channel_id=1, source_target_pairs={{0,2},{1,3},{2,4},{3,5},{4,6},{5,7},{6,0},{7,1},{8,10},{9,11},{10,... | collective-permute-start | bytes 393224 | tf_op jit(solution)/shard_map/ppermute | solution.py:186
  7.9 0.4 shard_map.96
  8.3 0.2 collective-permute-start
  8.4 1.5 %collective-permute-start.1 = (f32[128,512]{1,0:T(8,128)S(1)}, f32[128,512]{1,0:T(8,128)S(1)}, u32[]{:S(2)}, u32[]{:S(2)}) collective-permute-start(f32[128,512]{1,0:T(8,128)S(1)} %get-tuple-element.26), channel_id=1, source_target_pairs={{0,8},{1,9},{2,10},{3,11},{4,12},{5,13},{6,14},{7,15},{8,0},{9,1},... | collective-permute-start | bytes 786440 | tf_op jit(solution)/shard_map/ppermute | solution.py:182
  9.9 1.9 %collective-permute-start.2 = (f32[128,512]{1,0:T(8,128)S(1)}, f32[128,512]{1,0:T(8,128)S(1)}, u32[]{:S(2)}, u32[]{:S(2)}) collective-permute-start(f32[128,512]{1,0:T(8,128)S(1)} %get-tuple-element.27), channel_id=1, source_target_pairs={{0,9},{1,8},{2,11},{3,10},{4,13},{5,12},{6,15},{7,14},{8,1},{9,0},... | collective-permute-start | bytes 786440 | tf_op jit(solution)/shard_map/ppermute | solution.py:182
  11.8 2.2 %collective-permute-start.4 = (f32[128,256]{1,0:T(8,128)S(1)}, f32[128,256]{1,0:T(8,128)S(1)}, u32[]{:S(2)}, u32[]{:S(2)}) collective-permute-start(f32[128,256]{1,0:T(8,128)S(1)} %get-tuple-element.28.refs_4_), channel_id=1, source_target_pairs={{0,6},{1,7},{2,0},{3,1},{4,2},{5,3},{6,4},{7,5},{8,14},{9,15},{10,... | collective-permute-start | bytes 393224 | tf_op jit(solution)/shard_map/ppermute | solution.py:187
  14.0 0.5 collective-permute-done.3.refs_5_
  14.5 2.3 %collective-permute-start.5 = (f32[128,256]{1,0:T(8,128)S(1)}, f32[128,256]{1,0:T(8,128)S(1)}, u32[]{:S(2)}, u32[]{:S(2)}) collective-permute-start(f32[128,256]{1,0:T(8,128)S(1)} %collective-permute-done.3.refs_5_), channel_id=1, source_target_pairs={{0,2},{1,3},{2,4},{3,5},{4,6},{5,7},{6,0},{7,1},{8,10},{9,11},{10,... | collective-permute-start | bytes 393224 | tf_op jit(solution)/shard_map/ppermute | solution.py:188
  16.8 8.9 %collective-permute-done.4.refs_6_ = f32[128,256]{1,0:T(8,128)S(1)} collective-permute-done((f32[128,256]{1,0:T(8,128)S(1)}, f32[128,256]{1,0:T(8,128)S(1)}, u32[]{:S(2)}, u32[]{:S(2)}) %collective-permute-start.4) | collective-permute-done | bytes 131104 | tf_op jit(solution)/shard_map/ppermute | solution.py:187
  25.7 0.0 copy-start.2
  25.7 0.0 copy-start.3
  25.7 0.7 shard_map.97
  26.4 0.1 collective-permute-start.6
  26.5 1.6 %collective-permute-start.7 = (f32[128,256]{1,0:T(8,128)S(1)}, f32[128,256]{1,0:T(8,128)S(1)}, u32[]{:S(2)}, u32[]{:S(2)}) collective-permute-start(f32[128,256]{1,0:T(8,128)S(1)} %get-tuple-element.31), channel_id=1, source_target_pairs={{0,8},{1,9},{2,10},{3,11},{4,12},{5,13},{6,14},{7,15},{8,0},{9,1},... | collective-permute-start | bytes 393224 | tf_op jit(solution)/shard_map/ppermute | solution.py:182
  28.1 1.9 %collective-permute-start.8 = (f32[128,256]{1,0:T(8,128)S(1)}, f32[128,256]{1,0:T(8,128)S(1)}, u32[]{:S(2)}, u32[]{:S(2)}) collective-permute-start(f32[128,256]{1,0:T(8,128)S(1)} %get-tuple-element.32), channel_id=1, source_target_pairs={{0,9},{1,8},{2,11},{3,10},{4,13},{5,12},{6,15},{7,14},{8,1},{9,0},... | collective-permute-start | bytes 393224 | tf_op jit(solution)/shard_map/ppermute | solution.py:182
  30.0 1.5 %collective-permute-done.6.refs_1_ = f32[128,256]{1,0:T(8,128)S(1)} collective-permute-done((f32[128,256]{1,0:T(8,128)S(1)}, f32[128,256]{1,0:T(8,128)S(1)}, u32[]{:S(2)}, u32[]{:S(2)}) %collective-permute-start.6) | collective-permute-done | bytes 131104 | tf_op jit(solution)/shard_map/ppermute | solution.py:182
  31.5 3.2 %collective-permute-done.7.refs_2_ = f32[128,256]{1,0:T(8,128)S(1)} collective-permute-done((f32[128,256]{1,0:T(8,128)S(1)}, f32[128,256]{1,0:T(8,128)S(1)}, u32[]{:S(2)}, u32[]{:S(2)}) %collective-permute-start.7) | collective-permute-done | bytes 131104 | tf_op jit(solution)/shard_map/ppermute | solution.py:182
  34.7 0.0 copy-start
  34.7 0.8 shard_map.98
  35.6 15.0 %all_to_all.30.tiles = f32[16,16,128]{2,1,0:T(8,128)S(1)} all-to-all(f32[16,16,128]{2,1,0:T(8,128)S(1)} %get-tuple-element.34), channel_id=1, replica_groups=mesh['grp'=16,'leaf'=16] {'leaf'}, dimensions={0} | all-to-all | bytes 262144 | tf_op jit(solution)/shard_map/all_to_all | solution.py:178
  50.6 14.8 %all_to_all.31.gathered = f32[16,16,128]{2,1,0:T(8,128)S(1)} all-to-all(f32[16,16,128]{2,1,0:T(8,128)S(1)} %shard_map.99), channel_id=1, replica_groups=mesh['grp'=16,'leaf'=16] {'grp'}, dimensions={0} | all-to-all | bytes 262144 | tf_op jit(solution)/shard_map/all_to_all | solution.py:178
  65.4 0.5 shard_map.100
  65.9 11.8 %all_to_all.32.top_coef = f32[16,16,128]{2,1,0:T(8,128)S(1)} all-to-all(f32[16,16,128]{2,1,0:T(8,128)S(1)} %shard_map.100), channel_id=1, replica_groups=mesh['grp'=16,'leaf'=16] {'leaf'}, dimensions={0} | all-to-all | bytes 262144 | tf_op jit(solution)/shard_map/all_to_all | solution.py:178
  77.8 1.7 %shard_map.101 = (f32[512,256]{1,0:T(8,128)S(1)}, f32[512,256]{1,0:T(8,128)S(1)}, f32[128,256]{1,0:T(8,128)S(1)}) custom-call(f32[512,256]{1,0:T(8,128)S(1)} %get-tuple-element.33.inner, f32[16,16,128]{2,1,0:T(8,128)S(1)} %all_to_all.32.top_coef, s32[1,512]{1,0:T(1,128)S(1)} %bitcast.2, f32[512,128]{1,0:T(8,128)S(1)} %copy-done.4, f32[512,512]{1,0:T(8,128)S(1)} %copy-done.8, ...), custom_call_target="tpu_custom_call" | custom-call | flops 704643072 | bytes 3409920 | tf_op jit(solution)/shard_map/pallas_call | solution.py:159
  79.5 0.7 collective-permute-start.9
  80.2 3.5 %collective-permute-start.10 = (f32[128,256]{1,0:T(8,128)S(1)}, f32[128,256]{1,0:T(8,128)S(1)}, u32[]{:S(2)}, u32[]{:S(2)}) collective-permute-start(f32[128,256]{1,0:T(8,128)S(1)} %get-tuple-element.36.refs_4_), channel_id=1, source_target_pairs={{0,6},{1,7},{2,0},{3,1},{4,2},{5,3},{6,4},{7,5},{8,14},{9,15},{10,... | collective-permute-start | bytes 393224 | tf_op jit(solution)/shard_map/ppermute | solution.py:187
  83.7 6.1 %collective-permute-done.9.refs_5_ = f32[128,256]{1,0:T(8,128)S(1)} collective-permute-done((f32[128,256]{1,0:T(8,128)S(1)}, f32[128,256]{1,0:T(8,128)S(1)}, u32[]{:S(2)}, u32[]{:S(2)}) %collective-permute-start.9) | collective-permute-done | bytes 131104 | tf_op jit(solution)/shard_map/ppermute | solution.py:186
  89.8 0.0 collective-permute-start.11
  89.8 0.1 collective-permute-done.10.refs_6_
  89.9 9.6 %collective-permute-done.11.refs_7_ = f32[128,256]{1,0:T(8,128)S(1)} collective-permute-done((f32[128,256]{1,0:T(8,128)S(1)}, f32[128,256]{1,0:T(8,128)S(1)}, u32[]{:S(2)}, u32[]{:S(2)}) %collective-permute-start.11) | collective-permute-done | bytes 131104 | tf_op jit(solution)/shard_map/ppermute | solution.py:188
  99.5 0.7 shard_map.102
  100.1 0.1 collective-permute-start.12
  100.2 0.7 collective-permute-start.13
  100.9 2.8 %collective-permute-start.14 = (f32[128,256]{1,0:T(8,128)S(1)}, f32[128,256]{1,0:T(8,128)S(1)}, u32[]{:S(2)}, u32[]{:S(2)}) collective-permute-start(f32[128,256]{1,0:T(8,128)S(1)} %get-tuple-element.40), channel_id=1, source_target_pairs={{0,9},{1,8},{2,11},{3,10},{4,13},{5,12},{6,15},{7,14},{8,1},{9,0},... | collective-permute-start | bytes 393224 | tf_op jit(solution)/shard_map/ppermute | solution.py:182
  103.7 1.5 %collective-permute-done.12.refs_1_ = f32[128,256]{1,0:T(8,128)S(1)} collective-permute-done((f32[128,256]{1,0:T(8,128)S(1)}, f32[128,256]{1,0:T(8,128)S(1)}, u32[]{:S(2)}, u32[]{:S(2)}) %collective-permute-start.12) | collective-permute-done | bytes 131104 | tf_op jit(solution)/shard_map/ppermute | solution.py:182
  105.2 0.1 collective-permute-done.13.refs_2_
  105.3 1.5 %collective-permute-done.14.refs_3_ = f32[128,256]{1,0:T(8,128)S(1)} collective-permute-done((f32[128,256]{1,0:T(8,128)S(1)}, f32[128,256]{1,0:T(8,128)S(1)}, u32[]{:S(2)}, u32[]{:S(2)}) %collective-permute-start.14) | collective-permute-done | bytes 131104 | tf_op jit(solution)/shard_map/ppermute | solution.py:182
  106.8 0.8 shard_map.103
  107.6 13.3 %all_to_all.33.tiles = f32[16,16,128]{2,1,0:T(8,128)S(1)} all-to-all(f32[16,16,128]{2,1,0:T(8,128)S(1)} %get-tuple-element.42), channel_id=1, replica_groups=mesh['grp'=16,'leaf'=16] {'leaf'}, dimensions={0} | all-to-all | bytes 262144 | tf_op jit(solution)/shard_map/all_to_all | solution.py:178
  120.9 10.8 %all_to_all.34.gathered = f32[16,16,128]{2,1,0:T(8,128)S(1)} all-to-all(f32[16,16,128]{2,1,0:T(8,128)S(1)} %shard_map.104), channel_id=1, replica_groups=mesh['grp'=16,'leaf'=16] {'grp'}, dimensions={0} | all-to-all | bytes 262144 | tf_op jit(solution)/shard_map/all_to_all | solution.py:178
  131.8 0.5 shard_map.105
  132.3 11.7 %all_to_all.35.top_coef = f32[16,16,128]{2,1,0:T(8,128)S(1)} all-to-all(f32[16,16,128]{2,1,0:T(8,128)S(1)} %shard_map.105), channel_id=1, replica_groups=mesh['grp'=16,'leaf'=16] {'leaf'}, dimensions={0} | all-to-all | bytes 262144 | tf_op jit(solution)/shard_map/all_to_all | solution.py:178
  144.0 1.4 shard_map.106
  (22 shorter events, 0.1 us)
Async XLA Ops:
  0.6 7.3 %copy-start.1 = (f32[128,2048]{1,0:T(8,128)S(1)}, f32[128,2048]{1,0:T(8,128)}, u32[]{:S(2)}) copy-start(f32[128,2048]{1,0:T(8,128)} %capacitance.3) | copy-start | bytes 3145732
  0.6 0.8 copy-start.5
  1.4 1.2 copy-start.7
  2.6 0.9 copy-start.9
  4.5 9.9 %collective-permute-start.3 = (f32[128,256]{1,0:T(8,128)S(1)}, f32[128,256]{1,0:T(8,128)S(1)}, u32[]{:S(2)}, u32[]{:S(2)}) collective-permute-start(f32[128,256]{1,0:T(8,128)S(1)} %get-tuple-element.28.refs_4_), channel_id=1, source_target_pairs={{0,2},{1,3},{2,4},{3,5},{4,6},{5,7},{6,0},{7,1},{8,10},{9,11},{10,... | collective-permute-start | bytes 393224 | tf_op jit(solution)/shard_map/ppermute | solution.py:186
  8.3 17.4 %collective-permute-start = (f32[128,512]{1,0:T(8,128)S(1)}, f32[128,512]{1,0:T(8,128)S(1)}, u32[]{:S(2)}, u32[]{:S(2)}) collective-permute-start(f32[128,512]{1,0:T(8,128)S(1)} %get-tuple-element.25), channel_id=1, source_target_pairs={{0,1},{1,0},{2,3},{3,2},{4,5},{5,4},{6,7},{7,6},{8,9},{9,8},{10,11... | collective-permute-start | bytes 786440 | tf_op jit(solution)/shard_map/ppermute | solution.py:182
  8.4 17.3 %collective-permute-start.1 = (f32[128,512]{1,0:T(8,128)S(1)}, f32[128,512]{1,0:T(8,128)S(1)}, u32[]{:S(2)}, u32[]{:S(2)}) collective-permute-start(f32[128,512]{1,0:T(8,128)S(1)} %get-tuple-element.26), channel_id=1, source_target_pairs={{0,8},{1,9},{2,10},{3,11},{4,12},{5,13},{6,14},{7,15},{8,0},{9,1},... | collective-permute-start | bytes 786440 | tf_op jit(solution)/shard_map/ppermute | solution.py:182
  9.9 15.8 %collective-permute-start.2 = (f32[128,512]{1,0:T(8,128)S(1)}, f32[128,512]{1,0:T(8,128)S(1)}, u32[]{:S(2)}, u32[]{:S(2)}) collective-permute-start(f32[128,512]{1,0:T(8,128)S(1)} %get-tuple-element.27), channel_id=1, source_target_pairs={{0,9},{1,8},{2,11},{3,10},{4,13},{5,12},{6,15},{7,14},{8,1},{9,0},... | collective-permute-start | bytes 786440 | tf_op jit(solution)/shard_map/ppermute | solution.py:182
  11.8 13.9 %collective-permute-start.4 = (f32[128,256]{1,0:T(8,128)S(1)}, f32[128,256]{1,0:T(8,128)S(1)}, u32[]{:S(2)}, u32[]{:S(2)}) collective-permute-start(f32[128,256]{1,0:T(8,128)S(1)} %get-tuple-element.28.refs_4_), channel_id=1, source_target_pairs={{0,6},{1,7},{2,0},{3,1},{4,2},{5,3},{6,4},{7,5},{8,14},{9,15},{10,... | collective-permute-start | bytes 393224 | tf_op jit(solution)/shard_map/ppermute | solution.py:187
  14.5 11.2 %collective-permute-start.5 = (f32[128,256]{1,0:T(8,128)S(1)}, f32[128,256]{1,0:T(8,128)S(1)}, u32[]{:S(2)}, u32[]{:S(2)}) collective-permute-start(f32[128,256]{1,0:T(8,128)S(1)} %collective-permute-done.3.refs_5_), channel_id=1, source_target_pairs={{0,2},{1,3},{2,4},{3,5},{4,6},{5,7},{6,0},{7,1},{8,10},{9,11},{10,... | collective-permute-start | bytes 393224 | tf_op jit(solution)/shard_map/ppermute | solution.py:188
  25.7 9.0 %copy-start.2 = (f32[512,128]{1,0:T(8,128)S(1)}, f32[512,128]{1,0:T(8,128)}, u32[]{:S(2)}) copy-start(f32[512,128]{1,0:T(8,128)} %solved.3) | copy-start | bytes 786436
  25.7 9.0 %copy-start.3 = (f32[512,128]{1,0:T(8,128)S(1)}, f32[512,128]{1,0:T(8,128)}, u32[]{:S(2)}) copy-start(f32[512,128]{1,0:T(8,128)} %top.3) | copy-start | bytes 786436
  26.4 5.1 %collective-permute-start.6 = (f32[128,256]{1,0:T(8,128)S(1)}, f32[128,256]{1,0:T(8,128)S(1)}, u32[]{:S(2)}, u32[]{:S(2)}) collective-permute-start(f32[128,256]{1,0:T(8,128)S(1)} %get-tuple-element.30), channel_id=1, source_target_pairs={{0,1},{1,0},{2,3},{3,2},{4,5},{5,4},{6,7},{7,6},{8,9},{9,8},{10,11... | collective-permute-start | bytes 393224 | tf_op jit(solution)/shard_map/ppermute | solution.py:182
  26.5 8.2 %collective-permute-start.7 = (f32[128,256]{1,0:T(8,128)S(1)}, f32[128,256]{1,0:T(8,128)S(1)}, u32[]{:S(2)}, u32[]{:S(2)}) collective-permute-start(f32[128,256]{1,0:T(8,128)S(1)} %get-tuple-element.31), channel_id=1, source_target_pairs={{0,8},{1,9},{2,10},{3,11},{4,12},{5,13},{6,14},{7,15},{8,0},{9,1},... | collective-permute-start | bytes 393224 | tf_op jit(solution)/shard_map/ppermute | solution.py:182
  28.1 6.6 %collective-permute-start.8 = (f32[128,256]{1,0:T(8,128)S(1)}, f32[128,256]{1,0:T(8,128)S(1)}, u32[]{:S(2)}, u32[]{:S(2)}) collective-permute-start(f32[128,256]{1,0:T(8,128)S(1)} %get-tuple-element.32), channel_id=1, source_target_pairs={{0,9},{1,8},{2,11},{3,10},{4,13},{5,12},{6,15},{7,14},{8,1},{9,0},... | collective-permute-start | bytes 393224 | tf_op jit(solution)/shard_map/ppermute | solution.py:182
  34.7 30.6 %copy-start = (f32[128,2048]{1,0:T(8,128)S(1)}, f32[128,2048]{1,0:T(8,128)}, u32[]{:S(2)}) copy-start(f32[128,2048]{1,0:T(8,128)} %capacitance.5) | copy-start | bytes 3145732
  50.6 27.2 %copy-start.8 = (f32[512,512]{1,0:T(8,128)S(1)}, f32[512,512]{1,0:T(8,128)}, u32[]{:S(2)}) copy-start(f32[512,512]{1,0:T(8,128)} %inverse.3) | copy-start | bytes 3145732
  65.4 12.4 %copy-start.6 = (s32[512]{0:T(512)S(1)}, s32[512]{0:T(512)}, u32[]{:S(2)}) copy-start(s32[512]{0:T(512)} %param.8) | copy-start | bytes 6148
  65.4 12.4 %copy-start.10 = (f32[512,128]{1,0:T(8,128)S(1)}, f32[512,128]{1,0:T(8,128)}, u32[]{:S(2)}) copy-start(f32[512,128]{1,0:T(8,128)} %basis.3) | copy-start | bytes 786436
  65.9 11.9 %copy-start.4 = (f32[512,128]{1,0:T(8,128)S(1)}, f32[512,128]{1,0:T(8,128)}, u32[]{:S(2)}) copy-start(f32[512,128]{1,0:T(8,128)} %top_solved.3) | copy-start | bytes 786436
  79.5 10.3 %collective-permute-start.9 = (f32[128,256]{1,0:T(8,128)S(1)}, f32[128,256]{1,0:T(8,128)S(1)}, u32[]{:S(2)}, u32[]{:S(2)}) collective-permute-start(f32[128,256]{1,0:T(8,128)S(1)} %get-tuple-element.36.refs_4_), channel_id=1, source_target_pairs={{0,2},{1,3},{2,4},{3,5},{4,6},{5,7},{6,0},{7,1},{8,10},{9,11},{10,... | collective-permute-start | bytes 393224 | tf_op jit(solution)/shard_map/ppermute | solution.py:186
  80.2 9.6 %collective-permute-start.10 = (f32[128,256]{1,0:T(8,128)S(1)}, f32[128,256]{1,0:T(8,128)S(1)}, u32[]{:S(2)}, u32[]{:S(2)}) collective-permute-start(f32[128,256]{1,0:T(8,128)S(1)} %get-tuple-element.36.refs_4_), channel_id=1, source_target_pairs={{0,6},{1,7},{2,0},{3,1},{4,2},{5,3},{6,4},{7,5},{8,14},{9,15},{10,... | collective-permute-start | bytes 393224 | tf_op jit(solution)/shard_map/ppermute | solution.py:187
  89.8 9.7 %collective-permute-start.11 = (f32[128,256]{1,0:T(8,128)S(1)}, f32[128,256]{1,0:T(8,128)S(1)}, u32[]{:S(2)}, u32[]{:S(2)}) collective-permute-start(f32[128,256]{1,0:T(8,128)S(1)} %collective-permute-done.9.refs_5_), channel_id=1, source_target_pairs={{0,2},{1,3},{2,4},{3,5},{4,6},{5,7},{6,0},{7,1},{8,10},{9,11},{10,... | collective-permute-start | bytes 393224 | tf_op jit(solution)/shard_map/ppermute | solution.py:188
  100.1 5.1 %collective-permute-start.12 = (f32[128,256]{1,0:T(8,128)S(1)}, f32[128,256]{1,0:T(8,128)S(1)}, u32[]{:S(2)}, u32[]{:S(2)}) collective-permute-start(f32[128,256]{1,0:T(8,128)S(1)} %get-tuple-element.38), channel_id=1, source_target_pairs={{0,1},{1,0},{2,3},{3,2},{4,5},{5,4},{6,7},{7,6},{8,9},{9,8},{10,11... | collective-permute-start | bytes 393224 | tf_op jit(solution)/shard_map/ppermute | solution.py:182
  100.2 5.1 %collective-permute-start.13 = (f32[128,256]{1,0:T(8,128)S(1)}, f32[128,256]{1,0:T(8,128)S(1)}, u32[]{:S(2)}, u32[]{:S(2)}) collective-permute-start(f32[128,256]{1,0:T(8,128)S(1)} %get-tuple-element.39), channel_id=1, source_target_pairs={{0,8},{1,9},{2,10},{3,11},{4,12},{5,13},{6,14},{7,15},{8,0},{9,1},... | collective-permute-start | bytes 393224 | tf_op jit(solution)/shard_map/ppermute | solution.py:182
  100.9 5.9 %collective-permute-start.14 = (f32[128,256]{1,0:T(8,128)S(1)}, f32[128,256]{1,0:T(8,128)S(1)}, u32[]{:S(2)}, u32[]{:S(2)}) collective-permute-start(f32[128,256]{1,0:T(8,128)S(1)} %get-tuple-element.40), channel_id=1, source_target_pairs={{0,9},{1,8},{2,11},{3,10},{4,13},{5,12},{6,15},{7,14},{8,1},{9,0},... | collective-permute-start | bytes 393224 | tf_op jit(solution)/shard_map/ppermute | solution.py:182

commit v4 on v3

--- a/solution.py
+++ b/solution.py
@@ -96,27 +96,56 @@
     coeffs[...] = times(basis[...].T, found)
 
 
+def lift_kernel(solved, top, lift):
+    found = times(top[...].T, solved[...])
+    lift[...] = jnp.concatenate([found[: RANK // 2], found[RANK // 2 :]], axis=1)
+
+
 def row_of(k):
     sign = 1 - 2 * (lax.axis_index("grp") % 2)
     step = (lax.axis_index("leaf") % 8) // 2
     return pl.ds(pl.multiple_of(((step + k * sign + 4) % 4) * RANK, RANK), RANK)
 
 
-def group_kernel(*refs):
-    blocks, pieces, partials, stacked = refs[:4], refs[4:8], refs[8:12], refs[12]
+def partial_coefs(blocks, pieces, stacked):
     for piece, k in zip(pieces, (0, -1, 1, 2)):
         stacked[row_of(k), :] = piece[...]
-    right = split(stacked[...])
+    block = jnp.concatenate([part[...] for part in blocks], axis=0)
+    return passes(split(block), split(stacked[...]))
+
+
+def group_kernel(lift, *refs):
+    rows = partial_coefs(refs[:4], refs[4:8], refs[12])
     for q in range(4):
-        partials[q][...] = passes(split(blocks[q][...]), right)
+        refs[8 + q][:RANK, :] = rows[q * RANK : (q + 1) * RANK]
+        refs[8 + q][RANK:, :] = lift[...]
 
 
 def inner_kernel(local, solved, top, *refs):
     parts, inner, tiles = refs[:4], refs[4], refs[5]
-    coef = (parts[0][...] + parts[1][...]) + (parts[2][...] + parts[3][...])
+    coef = (parts[0][:RANK] + parts[1][:RANK]) + (parts[2][:RANK] + parts[3][:RANK])
     found = local[...] - times(solved[...], coef)
     inner[...] = found
     tiles[...] = times(top[...].T, found).T.reshape(16, 16, RANK)
+
+
+def later_group_kernel(projection, *refs):
+    sent, partials, tiles = refs[8:12], refs[12:16], refs[16]
+    rows = partial_coefs(refs[:4], refs[4:8], refs[17])
+    lifts = []
+    for q in range(4):
+        partials[q][...] = rows[q * RANK : (q + 1) * RANK]
+        lift = sent[q][RANK:, :]
+        lifts.append(jnp.concatenate([lift[:, :RANK], lift[:, RANK:]], axis=0))
+    total = projection[...] - times(jnp.concatenate(lifts, axis=1), rows)
+    tiles[...] = total.T.reshape(16, 16, RANK)
+
+
+def sum_inner_kernel(tiles, local, solved, *refs):
+    parts, out, inner = refs[:4], refs[4], refs[5]
+    out[...] = jnp.broadcast_to(jnp.sum(tiles[...], axis=0)[None], (16, 16, RANK))
+    coef = (parts[0][...] + parts[1][...]) + (parts[2][...] + parts[3][...])
+    inner[...] = local[...] - times(solved[...], coef)
 
 
 def sum_kernel(tiles, out):
@@ -134,7 +163,7 @@
 
 
 def next_kernel(
-    inner, top_coef, labels, top_solved, inverse, basis, local, scaled, coeffs
+    inner, top_coef, labels, top_solved, inverse, basis, top, local, scaled, coeffs, projection
 ):
     sign = signs(labels[...])
     moved = sign * solved_of(inner, top_solved, top_coef)
@@ -143,7 +172,9 @@
     scaled[...] = rest
     found = times(inverse[...], sign * (1.0 + (box - rest)))
     local[...] = found
-    coeffs[...] = times(basis[...].T, found)
+    parts = split(found)
+    coeffs[...] = passes(split(basis[...].T), parts)
+    projection[...] = passes(split(top[...].T), parts)
 
 
 def last_kernel(inner, top_coef, scaled, labels, top_solved, box_out, scaled_out):
@@ -189,25 +220,11 @@
     return [coeffs, before, after, opposite]
 
 
-def iteration(local, coeffs, blocks, leaf_solved, top_basis, top_capacitance):
-    partials = call(
-        group_kernel,
-        [COEFFS] * 4,
-        [*blocks, *relayed(coeffs)],
-        scratch=[STACK],
-        flops=32 * UNIT,
-    )
-    inner, tiles = call(
-        inner_kernel,
-        [WIDE, TILES],
-        [local, leaf_solved, top_basis, *across_square(partials)],
-        flops=16 * UNIT,
-    )
-    (shares,) = call(sum_kernel, [TILES], [exchange(tiles, "leaf")])
+def top_solve(shares, top_capacitance):
     (coefs,) = call(
         top_kernel, [TILES], [exchange(shares, "grp"), top_capacitance], flops=16 * UNIT
     )
-    return inner, exchange(coefs, "leaf")
+    return exchange(coefs, "leaf")
 
 
 def shards(
@@ -236,15 +253,45 @@
         [labels, leaf_inverse, leaf_basis],
         flops=40 * UNIT,
     )
-    shared = (blocks, leaf_solved, top_basis, top_capacitance)
-    inner, top_coef = iteration(local, coeffs, *shared)
-    local, scaled, coeffs = call(
+    (lift,) = call(lift_kernel, [(RANK // 2, CLASSES)], [leaf_solved, top_basis], flops=4 * UNIT)
+    sent = across_square(
+        call(
+            group_kernel,
+            [(RANK + RANK // 2, CLASSES)] * 4,
+            [lift, *blocks, *relayed(coeffs)],
+            scratch=[STACK],
+            flops=32 * UNIT,
+        )
+    )
+    inner, tiles = call(
+        inner_kernel,
+        [WIDE, TILES],
+        [local, leaf_solved, top_basis, *sent],
+        flops=16 * UNIT,
+    )
+    (shares,) = call(sum_kernel, [TILES], [exchange(tiles, "leaf")])
+    top_coef = top_solve(shares, top_capacitance)
+
+    local, scaled, coeffs, projection = call(
         next_kernel,
-        [WIDE, WIDE, COEFFS],
-        [inner, top_coef, labels, top_solved, leaf_inverse, leaf_basis],
+        [WIDE, WIDE, COEFFS, COEFFS],
+        [inner, top_coef, labels, top_solved, leaf_inverse, leaf_basis, top_basis],
         flops=56 * UNIT,
     )
-    inner, top_coef = iteration(local, coeffs, *shared)
+    *partials, tiles = call(
+        later_group_kernel,
+        [COEFFS] * 4 + [TILES],
+        [projection, *blocks, *relayed(coeffs), *sent],
+        scratch=[STACK],
+        flops=40 * UNIT,
+    )
+    shares, inner = call(
+        sum_inner_kernel,
+        [TILES, WIDE],
+        [exchange(tiles, "leaf"), local, leaf_solved, *across_square(partials)],
+        flops=8 * UNIT,
+    )
+    top_coef = top_solve(shares, top_capacitance)
     return tuple(
         call(
             last_kernel, [WIDE, WIDE], [inner, top_coef, scaled, labels, top_solved], flops=8 * UNIT

time: 146 us -> 143 us (0.979)
  blocking collectives: 77.4 us -> 67 us
  starting transfers between devices: 22.8 us -> 26.2 us
  waiting for transfers between devices: 32.9 us -> 35.9 us
    all_to_all x6 -> x5, blocking collectives: 77.4 us -> 67 us  [exchange(): return lax.all_to_all(tiles, axis, 0, 0, tiled=True)]
    ppermute x9, waiting for transfers between devices: 7.77 us -> 12.4 us  [across_square(): lax.ppermute(pieces[q], BOTH, square_pairs(q))]
    all_to_all x0 -> x1, starting transfers between devices: none -> 3.5 us  [exchange(): return lax.all_to_all(tiles, axis, 0, 0, tiled=True)]
  transfers between devices with their start and end apart: 15 -> 16, of which waited for: 10 -> 9; matrix products, arithmetic and copies ran while one was open for 0% -> 0% of each run, Pallas kernels for 0% -> 0%
where the time goes in v4:
time: 143 us
  blocking collectives  67 us (47%)
  waiting for transfers between devices  35.9 us (25%)
  starting transfers between devices  26.2 us (18%)
  Pallas kernels  9.7 us (7%)
  local copies, waits for them, and re-layouts  2.98 us (2%)
    all_to_all x5, blocking collectives, exchange(): return lax.all_to_all(tiles, axis, 0, 0, tiled=True)  67 us
    ppermute x9, waiting for transfers between devices, across_square(): lax.ppermute(pieces[q], BOTH, square_pairs(q))  12.4 us
    ppermute x9, starting transfers between devices, across_square(): lax.ppermute(pieces[q], BOTH, square_pairs(q))  10.7 us
    pallas_call x11, Pallas kernels, call(): pl.pallas_call(kernel, out_shape=shapes, in_specs=[pl.BlockSpec(memory_sp...  9.33 us
    ppermute x2, waiting for transfers between devices, relayed(): after = lax.ppermute(coeffs, BOTH, mirrored_pairs(-1))  8.68 us
    ppermute x2, waiting for transfers between devices, relayed(): opposite = lax.ppermute(before, BOTH, mirrored_pairs(1))  8.33 us
    ppermute x2, waiting for transfers between devices, relayed(): before = lax.ppermute(coeffs, BOTH, mirrored_pairs(1))  6.51 us
    ppermute x2, starting transfers between devices, relayed(): after = lax.ppermute(coeffs, BOTH, mirrored_pairs(-1))  5.65 us
  transfers between devices with their start and end apart: 16, of which 9 were waited for; matrix products, arithmetic and copies ran while one was open for 0% of the time, Pallas kernels for 0%

profile of v4, /device:TPU:32, one launch (start us, length us, event | category | flops | bytes accessed | tf_op | source)
XLA Modules:
  0.0 142.6 jit_solution(16559467422332305461)
XLA Ops:
  0.6 0.0 copy-start.5
  0.7 0.8 copy-done.5
  1.4 1.2 copy-done.7
  2.6 0.9 copy-done.9
  3.6 0.9 shard_map.95
  4.5 0.0 copy-start.1
  4.5 0.0 copy-start.2
  4.5 3.4 %collective-permute-start.3 = (f32[128,256]{1,0:T(8,128)S(1)}, f32[128,256]{1,0:T(8,128)S(1)}, u32[]{:S(2)}, u32[]{:S(2)}) collective-permute-start(f32[128,256]{1,0:T(8,128)S(1)} %get-tuple-element.30.refs_4_), channel_id=1, source_target_pairs={{0,2},{1,3},{2,4},{3,5},{4,6},{5,7},{6,0},{7,1},{8,10},{9,11},{10,... | collective-permute-start | bytes 393224 | tf_op jit(solution)/shard_map/ppermute | solution.py:217
  7.9 0.4 shard_map.97
  8.3 0.2 collective-permute-start
  8.5 1.5 %collective-permute-start.1 = (f32[128,512]{1,0:T(8,128)S(1)}, f32[128,512]{1,0:T(8,128)S(1)}, u32[]{:S(2)}, u32[]{:S(2)}) collective-permute-start(f32[128,512]{1,0:T(8,128)S(1)} %get-tuple-element.28), channel_id=1, source_target_pairs={{0,8},{1,9},{2,10},{3,11},{4,12},{5,13},{6,14},{7,15},{8,0},{9,1},... | collective-permute-start | bytes 786440 | tf_op jit(solution)/shard_map/ppermute | solution.py:213
  10.0 1.9 %collective-permute-start.2 = (f32[128,512]{1,0:T(8,128)S(1)}, f32[128,512]{1,0:T(8,128)S(1)}, u32[]{:S(2)}, u32[]{:S(2)}) collective-permute-start(f32[128,512]{1,0:T(8,128)S(1)} %get-tuple-element.29), channel_id=1, source_target_pairs={{0,9},{1,8},{2,11},{3,10},{4,13},{5,12},{6,15},{7,14},{8,1},{9,0},... | collective-permute-start | bytes 786440 | tf_op jit(solution)/shard_map/ppermute | solution.py:213
  11.9 2.2 %collective-permute-start.4 = (f32[128,256]{1,0:T(8,128)S(1)}, f32[128,256]{1,0:T(8,128)S(1)}, u32[]{:S(2)}, u32[]{:S(2)}) collective-permute-start(f32[128,256]{1,0:T(8,128)S(1)} %get-tuple-element.30.refs_4_), channel_id=1, source_target_pairs={{0,6},{1,7},{2,0},{3,1},{4,2},{5,3},{6,4},{7,5},{8,14},{9,15},{10,... | collective-permute-start | bytes 393224 | tf_op jit(solution)/shard_map/ppermute | solution.py:218
  14.0 0.5 collective-permute-done.3.refs_5_
  14.5 2.3 %collective-permute-start.5 = (f32[128,256]{1,0:T(8,128)S(1)}, f32[128,256]{1,0:T(8,128)S(1)}, u32[]{:S(2)}, u32[]{:S(2)}) collective-permute-start(f32[128,256]{1,0:T(8,128)S(1)} %collective-permute-done.3.refs_5_), channel_id=1, source_target_pairs={{0,2},{1,3},{2,4},{3,5},{4,6},{5,7},{6,0},{7,1},{8,10},{9,11},{10,... | collective-permute-start | bytes 393224 | tf_op jit(solution)/shard_map/ppermute | solution.py:219
  16.8 0.3 shard_map.96.lift
  17.1 8.6 %collective-permute-done.4.refs_6_ = f32[128,256]{1,0:T(8,128)S(1)} collective-permute-done((f32[128,256]{1,0:T(8,128)S(1)}, f32[128,256]{1,0:T(8,128)S(1)}, u32[]{:S(2)}, u32[]{:S(2)}) %collective-permute-start.4) | collective-permute-done | bytes 131104 | tf_op jit(solution)/shard_map/ppermute | solution.py:218
  25.7 0.7 shard_map.98
  26.4 0.1 collective-permute-start.6
  26.5 1.6 %collective-permute-start.7 = (f32[192,256]{1,0:T(8,128)S(1)}, f32[192,256]{1,0:T(8,128)S(1)}, u32[]{:S(2)}, u32[]{:S(2)}) collective-permute-start(f32[192,256]{1,0:T(8,128)S(1)} %get-tuple-element.33), channel_id=1, source_target_pairs={{0,8},{1,9},{2,10},{3,11},{4,12},{5,13},{6,14},{7,15},{8,0},{9,1},... | collective-permute-start | bytes 589832 | tf_op jit(solution)/shard_map/ppermute | solution.py:213
  28.1 1.9 %collective-permute-start.8 = (f32[192,256]{1,0:T(8,128)S(1)}, f32[192,256]{1,0:T(8,128)S(1)}, u32[]{:S(2)}, u32[]{:S(2)}) collective-permute-start(f32[192,256]{1,0:T(8,128)S(1)} %get-tuple-element.34), channel_id=1, source_target_pairs={{0,9},{1,8},{2,11},{3,10},{4,13},{5,12},{6,15},{7,14},{8,1},{9,0},... | collective-permute-start | bytes 589832 | tf_op jit(solution)/shard_map/ppermute | solution.py:213
  30.0 2.2 %collective-permute-done.6.refs_1_.refs_9_ = f32[192,256]{1,0:T(8,128)S(1)} collective-permute-done((f32[192,256]{1,0:T(8,128)S(1)}, f32[192,256]{1,0:T(8,128)S(1)}, u32[]{:S(2)}, u32[]{:S(2)}) %collective-permute-start.6) | collective-permute-done | bytes 196640 | tf_op jit(solution)/shard_map/ppermute | solution.py:213
  32.2 5.3 %collective-permute-done.7.refs_2_.refs_10_ = f32[192,256]{1,0:T(8,128)S(1)} collective-permute-done((f32[192,256]{1,0:T(8,128)S(1)}, f32[192,256]{1,0:T(8,128)S(1)}, u32[]{:S(2)}, u32[]{:S(2)}) %collective-permute-start.7) | collective-permute-done | bytes 196640 | tf_op jit(solution)/shard_map/ppermute | solution.py:213
  37.5 0.8 shard_map.99
  38.4 14.9 %all_to_all.30.tiles = f32[16,16,128]{2,1,0:T(8,128)S(1)} all-to-all(f32[16,16,128]{2,1,0:T(8,128)S(1)} %get-tuple-element.36), channel_id=1, replica_groups=mesh['grp'=16,'leaf'=16] {'leaf'}, dimensions={0} | all-to-all | bytes 262144 | tf_op jit(solution)/shard_map/all_to_all | solution.py:209
  53.3 14.8 %all_to_all.31.gathered = f32[16,16,128]{2,1,0:T(8,128)S(1)} all-to-all(f32[16,16,128]{2,1,0:T(8,128)S(1)} %shard_map.100), channel_id=1, replica_groups=mesh['grp'=16,'leaf'=16] {'grp'}, dimensions={0} | all-to-all | bytes 262144 | tf_op jit(solution)/shard_map/all_to_all | solution.py:209
  68.1 0.5 shard_map.101
  68.6 0.0 copy-start.4
  68.6 11.8 %all_to_all.32.top_coef = f32[16,16,128]{2,1,0:T(8,128)S(1)} all-to-all(f32[16,16,128]{2,1,0:T(8,128)S(1)} %shard_map.101), channel_id=1, replica_groups=mesh['grp'=16,'leaf'=16] {'leaf'}, dimensions={0} | all-to-all | bytes 262144 | tf_op jit(solution)/shard_map/all_to_all | solution.py:209
  80.5 2.0 %shard_map.102 = (f32[512,256]{1,0:T(8,128)S(1)}, f32[512,256]{1,0:T(8,128)S(1)}, f32[128,256]{1,0:T(8,128)S(1)}, f32[128,256]{1,0:T(8,128)S(1)}) custom-call(f32[512,256]{1,0:T(8,128)S(1)} %get-tuple-element.35.inner, f32[16,16,128]{2,1,0:T(8,128)S(1)} %all_to_all.32.top_coef, s32[1,512]{1,0:T(1,128)S(1)} %bitcast.2, f32[512,128]{1,0:T(8,128)S(1)} %copy-done.4, ...), custom_call_target="tpu_custom_call" | custom-call | flops 704643072 | bytes 3803136 | tf_op jit(solution)/shard_map/pallas_call | solution.py:190
  82.5 0.7 collective-permute-start.9
  83.2 3.5 %collective-permute-start.10 = (f32[128,256]{1,0:T(8,128)S(1)}, f32[128,256]{1,0:T(8,128)S(1)}, u32[]{:S(2)}, u32[]{:S(2)}) collective-permute-start(f32[128,256]{1,0:T(8,128)S(1)} %get-tuple-element.38.refs_4_), channel_id=1, source_target_pairs={{0,6},{1,7},{2,0},{3,1},{4,2},{5,3},{6,4},{7,5},{8,14},{9,15},{10,... | collective-permute-start | bytes 393224 | tf_op jit(solution)/shard_map/ppermute | solution.py:218
  86.7 6.1 %collective-permute-done.9.refs_5_ = f32[128,256]{1,0:T(8,128)S(1)} collective-permute-done((f32[128,256]{1,0:T(8,128)S(1)}, f32[128,256]{1,0:T(8,128)S(1)}, u32[]{:S(2)}, u32[]{:S(2)}) %collective-permute-start.9) | collective-permute-done | bytes 131104 | tf_op jit(solution)/shard_map/ppermute | solution.py:217
  92.8 0.0 collective-permute-start.11
  92.8 0.1 collective-permute-done.10.refs_6_
  92.9 8.3 %collective-permute-done.11.refs_7_ = f32[128,256]{1,0:T(8,128)S(1)} collective-permute-done((f32[128,256]{1,0:T(8,128)S(1)}, f32[128,256]{1,0:T(8,128)S(1)}, u32[]{:S(2)}, u32[]{:S(2)}) %collective-permute-start.11) | collective-permute-done | bytes 131104 | tf_op jit(solution)/shard_map/ppermute | solution.py:219
  101.2 1.8 %shard_map.103 = (f32[128,256]{1,0:T(8,128)S(1)}, f32[128,256]{1,0:T(8,128)}, f32[128,256]{1,0:T(8,128)S(1)}, f32[128,256]{1,0:T(8,128)S(1)}, f32[16,16,128]{2,1,0:T(8,128)}) custom-call(f32[128,256]{1,0:T(8,128)S(1)} %get-tuple-element.37.projection, f32[128,512]{1,0:T(8,128)S(1)} %get-tuple-element.26.refs_0_, ...), custom_call_target="tpu_custom_call" | custom-call | flops 503316480 | bytes 3145728 | tf_op jit(solution)/shard_map/pallas_call | solution.py:190
  103.0 3.5 %all-to-all-start.3 = ((f32[16,16,128]{2,1,0:T(8,128)}), f32[16,16,128]{2,1,0:T(8,128)S(1)}, u32[]{:S(2)}, u32[]{:S(2)}) async-start(f32[16,16,128]{2,1,0:T(8,128)} %get-tuple-element.39), calls=%async_computation.3 | async-start | bytes 262144 | tf_op jit(solution)/shard_map/all_to_all | solution.py:209
  106.5 0.2 collective-permute-start.12
  106.6 1.8 %collective-permute-start.13 = (f32[128,256]{1,0:T(8,128)S(1)}, f32[128,256]{1,0:T(8,128)S(1)}, u32[]{:S(2)}, u32[]{:S(2)}) collective-permute-start(f32[128,256]{1,0:T(8,128)S(1)} %get-tuple-element.43), channel_id=1, source_target_pairs={{0,8},{1,9},{2,10},{3,11},{4,12},{5,13},{6,14},{7,15},{8,0},{9,1},... | collective-permute-start | bytes 393224 | tf_op jit(solution)/shard_map/ppermute | solution.py:213
  108.5 1.5 %collective-permute-start.14 = (f32[128,256]{1,0:T(8,128)S(1)}, f32[128,256]{1,0:T(8,128)S(1)}, u32[]{:S(2)}, u32[]{:S(2)}) collective-permute-start(f32[128,256]{1,0:T(8,128)S(1)} %get-tuple-element.44), channel_id=1, source_target_pairs={{0,9},{1,8},{2,11},{3,10},{4,13},{5,12},{6,15},{7,14},{8,1},{9,0},... | collective-permute-start | bytes 393224 | tf_op jit(solution)/shard_map/ppermute | solution.py:213
  110.0 2.4 %collective-permute-done.12.refs_1_ = f32[128,256]{1,0:T(8,128)S(1)} collective-permute-done((f32[128,256]{1,0:T(8,128)}, f32[128,256]{1,0:T(8,128)S(1)}, u32[]{:S(2)}, u32[]{:S(2)}) %collective-permute-start.12) | collective-permute-done | bytes 131104 | tf_op jit(solution)/shard_map/ppermute | solution.py:213
  112.4 2.4 %collective-permute-done.14.refs_3_ = f32[128,256]{1,0:T(8,128)S(1)} collective-permute-done((f32[128,256]{1,0:T(8,128)S(1)}, f32[128,256]{1,0:T(8,128)S(1)}, u32[]{:S(2)}, u32[]{:S(2)}) %collective-permute-start.14) | collective-permute-done | bytes 131104 | tf_op jit(solution)/shard_map/ppermute | solution.py:213
  114.8 0.4 shard_map.104
  115.2 10.8 %all_to_all.33.gathered = f32[16,16,128]{2,1,0:T(8,128)S(1)} all-to-all(f32[16,16,128]{2,1,0:T(8,128)S(1)} %get-tuple-element.46), channel_id=1, replica_groups=mesh['grp'=16,'leaf'=16] {'grp'}, dimensions={0} | all-to-all | bytes 262144 | tf_op jit(solution)/shard_map/all_to_all | solution.py:209
  126.0 0.5 shard_map.105
  126.6 14.6 %all_to_all.34.top_coef = f32[16,16,128]{2,1,0:T(8,128)S(1)} all-to-all(f32[16,16,128]{2,1,0:T(8,128)S(1)} %shard_map.105), channel_id=1, replica_groups=mesh['grp'=16,'leaf'=16] {'leaf'}, dimensions={0} | all-to-all | bytes 262144 | tf_op jit(solution)/shard_map/all_to_all | solution.py:209
  141.2 1.4 shard_map.106
  (23 shorter events, 0.1 us)
Async XLA Ops:
  0.6 7.3 %copy-start.3 = (f32[128,2048]{1,0:T(8,128)S(1)}, f32[128,2048]{1,0:T(8,128)}, u32[]{:S(2)}) copy-start(f32[128,2048]{1,0:T(8,128)} %capacitance.3) | copy-start | bytes 3145732
  0.6 0.8 copy-start.5
  1.4 1.2 copy-start.7
  2.6 0.9 copy-start.9
  4.5 12.3 %copy-start.1 = (f32[512,128]{1,0:T(8,128)S(1)}, f32[512,128]{1,0:T(8,128)}, u32[]{:S(2)}) copy-start(f32[512,128]{1,0:T(8,128)} %solved.5) | copy-start | bytes 786436
  4.5 12.2 %copy-start.2 = (f32[512,128]{1,0:T(8,128)S(1)}, f32[512,128]{1,0:T(8,128)}, u32[]{:S(2)}) copy-start(f32[512,128]{1,0:T(8,128)} %top.5) | copy-start | bytes 786436
  4.5 9.9 %collective-permute-start.3 = (f32[128,256]{1,0:T(8,128)S(1)}, f32[128,256]{1,0:T(8,128)S(1)}, u32[]{:S(2)}, u32[]{:S(2)}) collective-permute-start(f32[128,256]{1,0:T(8,128)S(1)} %get-tuple-element.30.refs_4_), channel_id=1, source_target_pairs={{0,2},{1,3},{2,4},{3,5},{4,6},{5,7},{6,0},{7,1},{8,10},{9,11},{10,... | collective-permute-start | bytes 393224 | tf_op jit(solution)/shard_map/ppermute | solution.py:217
  8.3 17.4 %collective-permute-start = (f32[128,512]{1,0:T(8,128)S(1)}, f32[128,512]{1,0:T(8,128)S(1)}, u32[]{:S(2)}, u32[]{:S(2)}) collective-permute-start(f32[128,512]{1,0:T(8,128)S(1)} %get-tuple-element.27), channel_id=1, source_target_pairs={{0,1},{1,0},{2,3},{3,2},{4,5},{5,4},{6,7},{7,6},{8,9},{9,8},{10,11... | collective-permute-start | bytes 786440 | tf_op jit(solution)/shard_map/ppermute | solution.py:213
  8.5 17.3 %collective-permute-start.1 = (f32[128,512]{1,0:T(8,128)S(1)}, f32[128,512]{1,0:T(8,128)S(1)}, u32[]{:S(2)}, u32[]{:S(2)}) collective-permute-start(f32[128,512]{1,0:T(8,128)S(1)} %get-tuple-element.28), channel_id=1, source_target_pairs={{0,8},{1,9},{2,10},{3,11},{4,12},{5,13},{6,14},{7,15},{8,0},{9,1},... | collective-permute-start | bytes 786440 | tf_op jit(solution)/shard_map/ppermute | solution.py:213
  10.0 15.8 %collective-permute-start.2 = (f32[128,512]{1,0:T(8,128)S(1)}, f32[128,512]{1,0:T(8,128)S(1)}, u32[]{:S(2)}, u32[]{:S(2)}) collective-permute-start(f32[128,512]{1,0:T(8,128)S(1)} %get-tuple-element.29), channel_id=1, source_target_pairs={{0,9},{1,8},{2,11},{3,10},{4,13},{5,12},{6,15},{7,14},{8,1},{9,0},... | collective-permute-start | bytes 786440 | tf_op jit(solution)/shard_map/ppermute | solution.py:213
  11.9 13.9 %collective-permute-start.4 = (f32[128,256]{1,0:T(8,128)S(1)}, f32[128,256]{1,0:T(8,128)S(1)}, u32[]{:S(2)}, u32[]{:S(2)}) collective-permute-start(f32[128,256]{1,0:T(8,128)S(1)} %get-tuple-element.30.refs_4_), channel_id=1, source_target_pairs={{0,6},{1,7},{2,0},{3,1},{4,2},{5,3},{6,4},{7,5},{8,14},{9,15},{10,... | collective-permute-start | bytes 393224 | tf_op jit(solution)/shard_map/ppermute | solution.py:218
  14.5 11.2 %collective-permute-start.5 = (f32[128,256]{1,0:T(8,128)S(1)}, f32[128,256]{1,0:T(8,128)S(1)}, u32[]{:S(2)}, u32[]{:S(2)}) collective-permute-start(f32[128,256]{1,0:T(8,128)S(1)} %collective-permute-done.3.refs_5_), channel_id=1, source_target_pairs={{0,2},{1,3},{2,4},{3,5},{4,6},{5,7},{6,0},{7,1},{8,10},{9,11},{10,... | collective-permute-start | bytes 393224 | tf_op jit(solution)/shard_map/ppermute | solution.py:219
  26.4 5.8 %collective-permute-start.6 = (f32[192,256]{1,0:T(8,128)S(1)}, f32[192,256]{1,0:T(8,128)S(1)}, u32[]{:S(2)}, u32[]{:S(2)}) collective-permute-start(f32[192,256]{1,0:T(8,128)S(1)} %get-tuple-element.32), channel_id=1, source_target_pairs={{0,1},{1,0},{2,3},{3,2},{4,5},{5,4},{6,7},{7,6},{8,9},{9,8},{10,11... | collective-permute-start | bytes 589832 | tf_op jit(solution)/shard_map/ppermute | solution.py:213
  26.5 11.0 %collective-permute-start.7 = (f32[192,256]{1,0:T(8,128)S(1)}, f32[192,256]{1,0:T(8,128)S(1)}, u32[]{:S(2)}, u32[]{:S(2)}) collective-permute-start(f32[192,256]{1,0:T(8,128)S(1)} %get-tuple-element.33), channel_id=1, source_target_pairs={{0,8},{1,9},{2,10},{3,11},{4,12},{5,13},{6,14},{7,15},{8,0},{9,1},... | collective-permute-start | bytes 589832 | tf_op jit(solution)/shard_map/ppermute | solution.py:213
  28.1 9.4 %collective-permute-start.8 = (f32[192,256]{1,0:T(8,128)S(1)}, f32[192,256]{1,0:T(8,128)S(1)}, u32[]{:S(2)}, u32[]{:S(2)}) collective-permute-start(f32[192,256]{1,0:T(8,128)S(1)} %get-tuple-element.34), channel_id=1, source_target_pairs={{0,9},{1,8},{2,11},{3,10},{4,13},{5,12},{6,15},{7,14},{8,1},{9,0},... | collective-permute-start | bytes 589832 | tf_op jit(solution)/shard_map/ppermute | solution.py:213
  37.5 30.6 %copy-start = (f32[128,2048]{1,0:T(8,128)S(1)}, f32[128,2048]{1,0:T(8,128)}, u32[]{:S(2)}) copy-start(f32[128,2048]{1,0:T(8,128)} %capacitance.5) | copy-start | bytes 3145732
  53.3 27.2 %copy-start.8 = (f32[512,512]{1,0:T(8,128)S(1)}, f32[512,512]{1,0:T(8,128)}, u32[]{:S(2)}) copy-start(f32[512,512]{1,0:T(8,128)} %inverse.3) | copy-start | bytes 3145732
  68.1 12.4 %copy-start.6 = (s32[512]{0:T(512)S(1)}, s32[512]{0:T(512)}, u32[]{:S(2)}) copy-start(s32[512]{0:T(512)} %param.8) | copy-start | bytes 6148
  68.1 12.4 %copy-start.10 = (f32[512,128]{1,0:T(8,128)S(1)}, f32[512,128]{1,0:T(8,128)}, u32[]{:S(2)}) copy-start(f32[512,128]{1,0:T(8,128)} %basis.3) | copy-start | bytes 786436
  68.6 11.9 %copy-start.4 = (f32[512,128]{1,0:T(8,128)S(1)}, f32[512,128]{1,0:T(8,128)}, u32[]{:S(2)}) copy-start(f32[512,128]{1,0:T(8,128)} %top_solved.3) | copy-start | bytes 786436
  82.5 10.3 %collective-permute-start.9 = (f32[128,256]{1,0:T(8,128)S(1)}, f32[128,256]{1,0:T(8,128)S(1)}, u32[]{:S(2)}, u32[]{:S(2)}) collective-permute-start(f32[128,256]{1,0:T(8,128)S(1)} %get-tuple-element.38.refs_4_), channel_id=1, source_target_pairs={{0,2},{1,3},{2,4},{3,5},{4,6},{5,7},{6,0},{7,1},{8,10},{9,11},{10,... | collective-permute-start | bytes 393224 | tf_op jit(solution)/shard_map/ppermute | solution.py:217
  83.2 9.6 %collective-permute-start.10 = (f32[128,256]{1,0:T(8,128)S(1)}, f32[128,256]{1,0:T(8,128)S(1)}, u32[]{:S(2)}, u32[]{:S(2)}) collective-permute-start(f32[128,256]{1,0:T(8,128)S(1)} %get-tuple-element.38.refs_4_), channel_id=1, source_target_pairs={{0,6},{1,7},{2,0},{3,1},{4,2},{5,3},{6,4},{7,5},{8,14},{9,15},{10,... | collective-permute-start | bytes 393224 | tf_op jit(solution)/shard_map/ppermute | solution.py:218
  92.8 8.4 %collective-permute-start.11 = (f32[128,256]{1,0:T(8,128)S(1)}, f32[128,256]{1,0:T(8,128)S(1)}, u32[]{:S(2)}, u32[]{:S(2)}) collective-permute-start(f32[128,256]{1,0:T(8,128)S(1)} %collective-permute-done.9.refs_5_), channel_id=1, source_target_pairs={{0,2},{1,3},{2,4},{3,5},{4,6},{5,7},{6,0},{7,1},{8,10},{9,11},{10,... | collective-permute-start | bytes 393224 | tf_op jit(solution)/shard_map/ppermute | solution.py:219
  103.0 11.9 %all-to-all-start.3 = ((f32[16,16,128]{2,1,0:T(8,128)}), f32[16,16,128]{2,1,0:T(8,128)S(1)}, u32[]{:S(2)}, u32[]{:S(2)}) async-start(f32[16,16,128]{2,1,0:T(8,128)} %get-tuple-element.39), calls=%async_computation.3 | async-start | bytes 262144 | tf_op jit(solution)/shard_map/all_to_all | solution.py:209
  106.5 5.9 %collective-permute-start.12 = (f32[128,256]{1,0:T(8,128)}, f32[128,256]{1,0:T(8,128)S(1)}, u32[]{:S(2)}, u32[]{:S(2)}) collective-permute-start(f32[128,256]{1,0:T(8,128)} %get-tuple-element.42), channel_id=1, source_target_pairs={{0,1},{1,0},{2,3},{3,2},{4,5},{5,4},{6,7},{7,6},{8,9},{9,8},{10,11... | collective-permute-start | bytes 393224 | tf_op jit(solution)/shard_map/ppermute | solution.py:213
  106.6 5.8 %collective-permute-start.13 = (f32[128,256]{1,0:T(8,128)S(1)}, f32[128,256]{1,0:T(8,128)S(1)}, u32[]{:S(2)}, u32[]{:S(2)}) collective-permute-start(f32[128,256]{1,0:T(8,128)S(1)} %get-tuple-element.43), channel_id=1, source_target_pairs={{0,8},{1,9},{2,10},{3,11},{4,12},{5,13},{6,14},{7,15},{8,0},{9,1},... | collective-permute-start | bytes 393224 | tf_op jit(solution)/shard_map/ppermute | solution.py:213
  108.5 6.3 %collective-permute-start.14 = (f32[128,256]{1,0:T(8,128)S(1)}, f32[128,256]{1,0:T(8,128)S(1)}, u32[]{:S(2)}, u32[]{:S(2)}) collective-permute-start(f32[128,256]{1,0:T(8,128)S(1)} %get-tuple-element.44), channel_id=1, source_target_pairs={{0,9},{1,8},{2,11},{3,10},{4,13},{5,12},{6,15},{7,14},{8,1},{9,0},... | collective-permute-start | bytes 393224 | tf_op jit(solution)/shard_map/ppermute | solution.py:213

commit v5 on v4

--- a/solution.py
+++ b/solution.py
@@ -96,9 +96,29 @@
     coeffs[...] = times(basis[...].T, found)
 
 
-def lift_kernel(solved, top, lift):
+def lift_kernel(solved, top, lift, folded):
     found = times(top[...].T, solved[...])
-    lift[...] = jnp.concatenate([found[: RANK // 2], found[RANK // 2 :]], axis=1)
+    lift[...] = found
+    folded[...] = jnp.concatenate([found[: RANK // 2], found[RANK // 2 :]], axis=1)
+
+
+def project_kernel(local, top, projection):
+    projection[...] = times(top[...].T, local[...])
+
+
+def reach_kernel(inverse, basis, top, reach):
+    both = jnp.concatenate([basis[...].T, top[...].T], axis=0)
+    reach[...] = times(both, inverse[...])
+
+
+def block_lift_kernel(*refs):
+    blocks, sent, out = refs[:4], refs[4:8], refs[8]
+    lifts = []
+    for q in range(4):
+        lift = sent[q][RANK:, :]
+        lifts.append(jnp.concatenate([lift[:, :RANK], lift[:, RANK:]], axis=0))
+    block = jnp.concatenate([part[...] for part in blocks], axis=0)
+    out[...] = times(jnp.concatenate(lifts, axis=1), block)
 
 
 def row_of(k):
@@ -121,24 +141,20 @@
         refs[8 + q][RANK:, :] = lift[...]
 
 
-def inner_kernel(local, solved, top, *refs):
+def inner_kernel(local, solved, lift, projection, reach, *refs):
     parts, inner, tiles = refs[:4], refs[4], refs[5]
     coef = (parts[0][:RANK] + parts[1][:RANK]) + (parts[2][:RANK] + parts[3][:RANK])
-    found = local[...] - times(solved[...], coef)
-    inner[...] = found
-    tiles[...] = times(top[...].T, found).T.reshape(16, 16, RANK)
-
-
-def later_group_kernel(projection, *refs):
-    sent, partials, tiles = refs[8:12], refs[12:16], refs[16]
-    rows = partial_coefs(refs[:4], refs[4:8], refs[17])
-    lifts = []
+    both = times(jnp.concatenate([solved[...], lift[...]], axis=0), coef)
+    inner[...] = local[...] - both[:LEAF]
+    tiles[...] = (projection[...] - both[LEAF:]).T.reshape(16, 16, RANK)
+
+
+def later_group_kernel(projection, block_lift, *refs):
+    partials, tiles = refs[8:12], refs[12]
+    rows = partial_coefs([*refs[:4], block_lift], refs[4:8], refs[13])
     for q in range(4):
         partials[q][...] = rows[q * RANK : (q + 1) * RANK]
-        lift = sent[q][RANK:, :]
-        lifts.append(jnp.concatenate([lift[:, :RANK], lift[:, RANK:]], axis=0))
-    total = projection[...] - times(jnp.concatenate(lifts, axis=1), rows)
-    tiles[...] = total.T.reshape(16, 16, RANK)
+    tiles[...] = (projection[...] - rows[4 * RANK :]).T.reshape(16, 16, RANK)
 
 
 def sum_inner_kernel(tiles, local, solved, *refs):
@@ -163,25 +179,38 @@
 
 
 def next_kernel(
-    inner, top_coef, labels, top_solved, inverse, basis, top, local, scaled, coeffs, projection
+    inner, top_coef, labels, top_solved, inverse, reach, local, scaled, coeffs, projection
 ):
     sign = signs(labels[...])
     moved = sign * solved_of(inner, top_solved, top_coef)
     box = jnp.clip(moved, 0.0, 1.0)
     rest = moved - box
     scaled[...] = rest
-    found = times(inverse[...], sign * (1.0 + (box - rest)))
-    local[...] = found
-    parts = split(found)
-    coeffs[...] = passes(split(basis[...].T), parts)
-    projection[...] = passes(split(top[...].T), parts)
-
-
-def last_kernel(inner, top_coef, scaled, labels, top_solved, box_out, scaled_out):
-    moved = scaled[...] + signs(labels[...]) * solved_of(inner, top_solved, top_coef)
-    box = jnp.clip(moved, 0.0, 1.0)
-    box_out[...] = box
-    scaled_out[...] = moved - box
+    both = jnp.concatenate([inverse[...], reach[...]], axis=0)
+    found = times(both, sign * (1.0 + (box - rest)))
+    local[...] = found[:LEAF]
+    coeffs[...] = found[LEAF : LEAF + RANK]
+    projection[...] = found[LEAF + RANK :]
+
+
+def last_kernel(inner, top_coef, scaled, labels, top_solved, box_out, scaled_out, near, done):
+    right = split(top_coef[...].reshape(CLASSES, RANK))
+    sign = signs(labels[...])
+    half = LEAF // 2
+    copies = []
+    for part in range(2):
+        rows = slice(part * half, (part + 1) * half)
+        solved = inner[rows] - passes(split(top_solved[rows]), right, 1)
+        moved = scaled[rows] + sign[rows] * solved
+        box = jnp.clip(moved, 0.0, 1.0)
+        near[0, rows] = box
+        near[1, rows] = moved - box
+        for i, out in enumerate((box_out, scaled_out)):
+            copy = pltpu.make_async_copy(near.at[i, rows], out.at[rows], done.at[2 * part + i])
+            copy.start()
+            copies.append(copy)
+    for copy in copies:
+        copy.wait()
 
 
 def call(kernel, outs, args, scratch=(), flops=0):
@@ -253,12 +282,24 @@
         [labels, leaf_inverse, leaf_basis],
         flops=40 * UNIT,
     )
-    (lift,) = call(lift_kernel, [(RANK // 2, CLASSES)], [leaf_solved, top_basis], flops=4 * UNIT)
+    lift, folded = call(
+        lift_kernel,
+        [(RANK, RANK), (RANK // 2, CLASSES)],
+        [leaf_solved, top_basis],
+        flops=4 * UNIT,
+    )
+    (projection,) = call(project_kernel, [COEFFS], [local, top_basis], flops=8 * UNIT)
+    (reach,) = call(
+        reach_kernel,
+        [(2 * RANK, LEAF)],
+        [leaf_inverse, leaf_basis, top_basis],
+        flops=32 * UNIT,
+    )
     sent = across_square(
         call(
             group_kernel,
             [(RANK + RANK // 2, CLASSES)] * 4,
-            [lift, *blocks, *relayed(coeffs)],
+            [folded, *blocks, *relayed(coeffs)],
             scratch=[STACK],
             flops=32 * UNIT,
         )
@@ -266,8 +307,8 @@
     inner, tiles = call(
         inner_kernel,
         [WIDE, TILES],
-        [local, leaf_solved, top_basis, *sent],
-        flops=16 * UNIT,
+        [local, leaf_solved, lift, projection, reach, *sent],
+        flops=10 * UNIT,
     )
     (shares,) = call(sum_kernel, [TILES], [exchange(tiles, "leaf")])
     top_coef = top_solve(shares, top_capacitance)
@@ -275,13 +316,16 @@
     local, scaled, coeffs, projection = call(
         next_kernel,
         [WIDE, WIDE, COEFFS, COEFFS],
-        [inner, top_coef, labels, top_solved, leaf_inverse, leaf_basis, top_basis],
+        [inner, top_coef, labels, top_solved, leaf_inverse, reach],
         flops=56 * UNIT,
+    )
+    (block_lift,) = call(
+        block_lift_kernel, [(RANK, 4 * RANK)], [*blocks, *sent], flops=16 * UNIT
     )
     *partials, tiles = call(
         later_group_kernel,
         [COEFFS] * 4 + [TILES],
-        [projection, *blocks, *relayed(coeffs), *sent],
+        [projection, block_lift, *blocks, *relayed(coeffs)],
         scratch=[STACK],
         flops=40 * UNIT,
     )
@@ -293,9 +337,17 @@
     )
     top_coef = top_solve(shares, top_capacitance)
     return tuple(
-        call(
-            last_kernel, [WIDE, WIDE], [inner, top_coef, scaled, labels, top_solved], flops=8 * UNIT
-        )
+        pl.pallas_call(
+            last_kernel,
+            out_shape=[jax.ShapeDtypeStruct(WIDE, jnp.float32)] * 2,
+            in_specs=[pl.BlockSpec(memory_space=pltpu.VMEM)] * 5,
+            out_specs=[pl.BlockSpec(memory_space=pl.ANY)] * 2,
+            scratch_shapes=[
+                pltpu.VMEM((2, *WIDE), jnp.float32),
+                pltpu.SemaphoreType.DMA((4,)),
+            ],
+            compiler_params=pltpu.CompilerParams(vmem_limit_bytes=16 * 1024 * 1024),
+        )(inner, top_coef, scaled, labels, top_solved)
     )
 
 

time: 143 us -> 142 us (level)
  waiting for transfers between devices: 35.9 us -> 34.4 us
    pallas_call x11 -> x13, Pallas kernels: 9.33 us -> 8.26 us  [call(): pl.pallas_call(kernel, out_shape=shapes, in_specs=[pl.BlockSpec(memory_sp...]
    unnamed x22 -> x20, local copies, waits for them, and re-layouts: 2.98 us -> 2.97 us
  transfers between devices with their start and end apart: 16 -> 16, of which waited for: 9 -> 8; matrix products, arithmetic and copies ran while one was open for 0% -> 0% of each run, Pallas kernels for 0% -> 1%
where the time goes in v5:
time: 142 us
  blocking collectives  66.9 us (47%)
  waiting for transfers between devices  34.4 us (24%)
  starting transfers between devices  26.2 us (18%)
  Pallas kernels  10 us (7%)
  local copies, waits for them, and re-layouts  2.97 us (2%)
    all_to_all x5, blocking collectives, exchange(): return lax.all_to_all(tiles, axis, 0, 0, tiled=True)  66.9 us
    ppermute x9, waiting for transfers between devices, across_square(): lax.ppermute(pieces[q], BOTH, square_pairs(q))  11.3 us
    ppermute x9, starting transfers between devices, across_square(): lax.ppermute(pieces[q], BOTH, square_pairs(q))  10.7 us
    ppermute x2, waiting for transfers between devices, relayed(): after = lax.ppermute(coeffs, BOTH, mirrored_pairs(-1))  8.61 us
    pallas_call x13, Pallas kernels, call(): pl.pallas_call(kernel, out_shape=shapes, in_specs=[pl.BlockSpec(memory_sp...  8.26 us
    ppermute x2, waiting for transfers between devices, relayed(): opposite = lax.ppermute(before, BOTH, mirrored_pairs(1))  7.98 us
    ppermute x2, waiting for transfers between devices, relayed(): before = lax.ppermute(coeffs, BOTH, mirrored_pairs(1))  6.51 us
    ppermute x2, starting transfers between devices, relayed(): after = lax.ppermute(coeffs, BOTH, mirrored_pairs(-1))  5.65 us
  transfers between devices with their start and end apart: 16, of which 8 were waited for; matrix products, arithmetic and copies ran while one was open for 0% of the time, Pallas kernels for 1%

profile of v5, /device:TPU:32, one launch (start us, length us, event | category | flops | bytes accessed | tf_op | source)
XLA Modules:
  0.0 141.6 jit_solution(7744392582028002487)
XLA Ops:
  0.6 0.0 copy-start.4
  0.7 1.3 copy-done.4
  2.0 0.9 copy-done.7
  2.9 0.7 copy-done.8
  3.6 0.9 shard_map.95
  4.5 0.0 copy-start.2
  4.5 3.4 %collective-permute-start.3 = (f32[128,256]{1,0:T(8,128)S(1)}, f32[128,256]{1,0:T(8,128)S(1)}, u32[]{:S(2)}, u32[]{:S(2)}) collective-permute-start(f32[128,256]{1,0:T(8,128)S(1)} %get-tuple-element.34.refs_4_), channel_id=1, source_target_pairs={{0,2},{1,3},{2,4},{3,5},{4,6},{5,7},{6,0},{7,1},{8,10},{9,11},{10,... | collective-permute-start | bytes 393224 | tf_op jit(solution)/shard_map/ppermute | solution.py:246
  7.9 0.4 shard_map.99
  8.3 0.2 collective-permute-start
  8.5 1.5 %collective-permute-start.1 = (f32[128,512]{1,0:T(8,128)S(1)}, f32[128,512]{1,0:T(8,128)S(1)}, u32[]{:S(2)}, u32[]{:S(2)}) collective-permute-start(f32[128,512]{1,0:T(8,128)S(1)} %get-tuple-element.32), channel_id=1, source_target_pairs={{0,8},{1,9},{2,10},{3,11},{4,12},{5,13},{6,14},{7,15},{8,0},{9,1},... | collective-permute-start | bytes 786440 | tf_op jit(solution)/shard_map/ppermute | solution.py:242
  10.0 1.9 %collective-permute-start.2 = (f32[128,512]{1,0:T(8,128)S(1)}, f32[128,512]{1,0:T(8,128)S(1)}, u32[]{:S(2)}, u32[]{:S(2)}) collective-permute-start(f32[128,512]{1,0:T(8,128)S(1)} %get-tuple-element.33), channel_id=1, source_target_pairs={{0,9},{1,8},{2,11},{3,10},{4,13},{5,12},{6,15},{7,14},{8,1},{9,0},... | collective-permute-start | bytes 786440 | tf_op jit(solution)/shard_map/ppermute | solution.py:242
  11.9 2.2 %collective-permute-start.4 = (f32[128,256]{1,0:T(8,128)S(1)}, f32[128,256]{1,0:T(8,128)S(1)}, u32[]{:S(2)}, u32[]{:S(2)}) collective-permute-start(f32[128,256]{1,0:T(8,128)S(1)} %get-tuple-element.34.refs_4_), channel_id=1, source_target_pairs={{0,6},{1,7},{2,0},{3,1},{4,2},{5,3},{6,4},{7,5},{8,14},{9,15},{10,... | collective-permute-start | bytes 393224 | tf_op jit(solution)/shard_map/ppermute | solution.py:247
  14.0 0.5 collective-permute-done.3.refs_5_
  14.5 2.3 %collective-permute-start.5 = (f32[128,256]{1,0:T(8,128)S(1)}, f32[128,256]{1,0:T(8,128)S(1)}, u32[]{:S(2)}, u32[]{:S(2)}) collective-permute-start(f32[128,256]{1,0:T(8,128)S(1)} %collective-permute-done.3.refs_5_), channel_id=1, source_target_pairs={{0,2},{1,3},{2,4},{3,5},{4,6},{5,7},{6,0},{7,1},{8,10},{9,11},{10,... | collective-permute-start | bytes 393224 | tf_op jit(solution)/shard_map/ppermute | solution.py:248
  16.8 0.3 shard_map.96
  17.1 8.6 %collective-permute-done.4.refs_6_ = f32[128,256]{1,0:T(8,128)S(1)} collective-permute-done((f32[128,256]{1,0:T(8,128)S(1)}, f32[128,256]{1,0:T(8,128)S(1)}, u32[]{:S(2)}, u32[]{:S(2)}) %collective-permute-start.4) | collective-permute-done | bytes 131104 | tf_op jit(solution)/shard_map/ppermute | solution.py:247
  25.8 0.7 shard_map.100
  26.4 0.1 collective-permute-start.6
  26.5 1.6 %collective-permute-start.7 = (f32[192,256]{1,0:T(8,128)S(1)}, f32[192,256]{1,0:T(8,128)S(1)}, u32[]{:S(2)}, u32[]{:S(2)}) collective-permute-start(f32[192,256]{1,0:T(8,128)S(1)} %get-tuple-element.37), channel_id=1, source_target_pairs={{0,8},{1,9},{2,10},{3,11},{4,12},{5,13},{6,14},{7,15},{8,0},{9,1},... | collective-permute-start | bytes 589832 | tf_op jit(solution)/shard_map/ppermute | solution.py:242
  28.1 1.9 %collective-permute-start.8 = (f32[192,256]{1,0:T(8,128)S(1)}, f32[192,256]{1,0:T(8,128)S(1)}, u32[]{:S(2)}, u32[]{:S(2)}) collective-permute-start(f32[192,256]{1,0:T(8,128)S(1)} %get-tuple-element.38), channel_id=1, source_target_pairs={{0,9},{1,8},{2,11},{3,10},{4,13},{5,12},{6,15},{7,14},{8,1},{9,0},... | collective-permute-start | bytes 589832 | tf_op jit(solution)/shard_map/ppermute | solution.py:242
  30.0 0.3 shard_map.97.projection
  30.4 0.6 shard_map.98.reach
  31.0 1.2 collective-permute-done.6.refs_1_.refs_5_
  32.2 5.3 %collective-permute-done.7.refs_2_.refs_6_ = f32[192,256]{1,0:T(8,128)S(1)} collective-permute-done((f32[192,256]{1,0:T(8,128)S(1)}, f32[192,256]{1,0:T(8,128)S(1)}, u32[]{:S(2)}, u32[]{:S(2)}) %collective-permute-start.7) | collective-permute-done | bytes 196640 | tf_op jit(solution)/shard_map/ppermute | solution.py:242
  37.5 0.5 shard_map.101
  38.0 14.9 %all_to_all.30.tiles = f32[16,16,128]{2,1,0:T(8,128)S(1)} all-to-all(f32[16,16,128]{2,1,0:T(8,128)S(1)} %get-tuple-element.40), channel_id=1, replica_groups=mesh['grp'=16,'leaf'=16] {'leaf'}, dimensions={0} | all-to-all | bytes 262144 | tf_op jit(solution)/shard_map/all_to_all | solution.py:238
  53.0 14.7 %all_to_all.31.gathered = f32[16,16,128]{2,1,0:T(8,128)S(1)} all-to-all(f32[16,16,128]{2,1,0:T(8,128)S(1)} %shard_map.102), channel_id=1, replica_groups=mesh['grp'=16,'leaf'=16] {'grp'}, dimensions={0} | all-to-all | bytes 262144 | tf_op jit(solution)/shard_map/all_to_all | solution.py:238
  67.6 0.5 shard_map.103
  68.2 11.8 %all_to_all.32.top_coef = f32[16,16,128]{2,1,0:T(8,128)S(1)} all-to-all(f32[16,16,128]{2,1,0:T(8,128)S(1)} %shard_map.103), channel_id=1, replica_groups=mesh['grp'=16,'leaf'=16] {'leaf'}, dimensions={0} | all-to-all | bytes 262144 | tf_op jit(solution)/shard_map/all_to_all | solution.py:238
  80.1 1.5 %shard_map.104 = (f32[512,256]{1,0:T(8,128)S(1)}, f32[512,256]{1,0:T(8,128)S(1)}, f32[128,256]{1,0:T(8,128)S(1)}, f32[128,256]{1,0:T(8,128)S(1)}) custom-call(f32[512,256]{1,0:T(8,128)S(1)} %get-tuple-element.39.inner, f32[16,16,128]{2,1,0:T(8,128)S(1)} %all_to_all.32.top_coef, s32[1,512]{1,0:T(1,128)S(1)} %bitcast.2, f32[512,128]{1,0:T(8,128)S(1)} %copy-done.6, ...), custom_call_target="tpu_custom_call" | custom-call | flops 704643072 | bytes 3803136 | tf_op jit(solution)/shard_map/pallas_call | solution.py:219
  81.6 0.7 collective-permute-start.9
  82.3 3.5 %collective-permute-start.10 = (f32[128,256]{1,0:T(8,128)S(1)}, f32[128,256]{1,0:T(8,128)S(1)}, u32[]{:S(2)}, u32[]{:S(2)}) collective-permute-start(f32[128,256]{1,0:T(8,128)S(1)} %get-tuple-element.42.refs_4_), channel_id=1, source_target_pairs={{0,6},{1,7},{2,0},{3,1},{4,2},{5,3},{6,4},{7,5},{8,14},{9,15},{10,... | collective-permute-start | bytes 393224 | tf_op jit(solution)/shard_map/ppermute | solution.py:247
  85.8 6.1 %collective-permute-done.9.refs_5_ = f32[128,256]{1,0:T(8,128)S(1)} collective-permute-done((f32[128,256]{1,0:T(8,128)S(1)}, f32[128,256]{1,0:T(8,128)S(1)}, u32[]{:S(2)}, u32[]{:S(2)}) %collective-permute-start.9) | collective-permute-done | bytes 131104 | tf_op jit(solution)/shard_map/ppermute | solution.py:246
  91.8 0.0 collective-permute-start.11
  91.9 0.4 shard_map.105.block_lift
  92.3 8.0 %collective-permute-done.11.refs_7_ = f32[128,256]{1,0:T(8,128)S(1)} collective-permute-done((f32[128,256]{1,0:T(8,128)S(1)}, f32[128,256]{1,0:T(8,128)S(1)}, u32[]{:S(2)}, u32[]{:S(2)}) %collective-permute-start.11) | collective-permute-done | bytes 131104 | tf_op jit(solution)/shard_map/ppermute | solution.py:248
  100.3 1.5 %shard_map.106 = (f32[128,256]{1,0:T(8,128)S(1)}, f32[128,256]{1,0:T(8,128)}, f32[128,256]{1,0:T(8,128)S(1)}, f32[128,256]{1,0:T(8,128)S(1)}, f32[16,16,128]{2,1,0:T(8,128)}) custom-call(f32[128,256]{1,0:T(8,128)S(1)} %get-tuple-element.41.projection, f32[128,512]{1,0:T(8,128)S(1)} %shard_map.105.block_lift, f32[128,512]{1,0:T(8,128)S(1)} %get-tuple-element.30.refs_0_, ...), custom_call_target="tpu_custom_call" | custom-call | flops 503316480 | bytes 2621440 | tf_op jit(solution)/shard_map/pallas_call | solution.py:219
  101.8 3.5 %all-to-all-start.3 = ((f32[16,16,128]{2,1,0:T(8,128)}), f32[16,16,128]{2,1,0:T(8,128)S(1)}, u32[]{:S(2)}, u32[]{:S(2)}) async-start(f32[16,16,128]{2,1,0:T(8,128)} %get-tuple-element.43), calls=%async_computation.3 | async-start | bytes 262144 | tf_op jit(solution)/shard_map/all_to_all | solution.py:238
  105.3 0.2 collective-permute-start.12
  105.4 1.8 %collective-permute-start.13 = (f32[128,256]{1,0:T(8,128)S(1)}, f32[128,256]{1,0:T(8,128)S(1)}, u32[]{:S(2)}, u32[]{:S(2)}) collective-permute-start(f32[128,256]{1,0:T(8,128)S(1)} %get-tuple-element.47), channel_id=1, source_target_pairs={{0,8},{1,9},{2,10},{3,11},{4,12},{5,13},{6,14},{7,15},{8,0},{9,1},... | collective-permute-start | bytes 393224 | tf_op jit(solution)/shard_map/ppermute | solution.py:242
  107.3 1.5 %collective-permute-start.14 = (f32[128,256]{1,0:T(8,128)S(1)}, f32[128,256]{1,0:T(8,128)S(1)}, u32[]{:S(2)}, u32[]{:S(2)}) collective-permute-start(f32[128,256]{1,0:T(8,128)S(1)} %get-tuple-element.48), channel_id=1, source_target_pairs={{0,9},{1,8},{2,11},{3,10},{4,13},{5,12},{6,15},{7,14},{8,1},{9,0},... | collective-permute-start | bytes 393224 | tf_op jit(solution)/shard_map/ppermute | solution.py:242
  108.8 2.4 %collective-permute-done.12.refs_1_ = f32[128,256]{1,0:T(8,128)S(1)} collective-permute-done((f32[128,256]{1,0:T(8,128)}, f32[128,256]{1,0:T(8,128)S(1)}, u32[]{:S(2)}, u32[]{:S(2)}) %collective-permute-start.12) | collective-permute-done | bytes 131104 | tf_op jit(solution)/shard_map/ppermute | solution.py:242
  111.2 2.4 %collective-permute-done.14.refs_3_ = f32[128,256]{1,0:T(8,128)S(1)} collective-permute-done((f32[128,256]{1,0:T(8,128)S(1)}, f32[128,256]{1,0:T(8,128)S(1)}, u32[]{:S(2)}, u32[]{:S(2)}) %collective-permute-start.14) | collective-permute-done | bytes 131104 | tf_op jit(solution)/shard_map/ppermute | solution.py:242
  113.6 0.4 shard_map.107
  114.0 10.8 %all_to_all.33.gathered = f32[16,16,128]{2,1,0:T(8,128)S(1)} all-to-all(f32[16,16,128]{2,1,0:T(8,128)S(1)} %get-tuple-element.50), channel_id=1, replica_groups=mesh['grp'=16,'leaf'=16] {'grp'}, dimensions={0} | all-to-all | bytes 262144 | tf_op jit(solution)/shard_map/all_to_all | solution.py:238
  124.8 0.5 shard_map.108
  125.4 14.6 %all_to_all.34.top_coef = f32[16,16,128]{2,1,0:T(8,128)S(1)} all-to-all(f32[16,16,128]{2,1,0:T(8,128)S(1)} %shard_map.108), channel_id=1, replica_groups=mesh['grp'=16,'leaf'=16] {'leaf'}, dimensions={0} | all-to-all | bytes 262144 | tf_op jit(solution)/shard_map/all_to_all | solution.py:238
  140.0 1.4 shard_map.109
  (24 shorter events, 0.1 us)
Async XLA Ops:
  0.6 7.3 %copy-start.3 = (f32[128,2048]{1,0:T(8,128)S(1)}, f32[128,2048]{1,0:T(8,128)}, u32[]{:S(2)}) copy-start(f32[128,2048]{1,0:T(8,128)} %capacitance.3) | copy-start | bytes 3145732
  0.6 1.3 copy-start.4
  2.0 0.9 copy-start.7
  2.9 0.7 copy-start.8
  4.5 12.2 %copy-start.1 = (f32[512,128]{1,0:T(8,128)S(1)}, f32[512,128]{1,0:T(8,128)}, u32[]{:S(2)}) copy-start(f32[512,128]{1,0:T(8,128)} %solved.5) | copy-start | bytes 786436
  4.5 12.2 %copy-start.2 = (f32[512,128]{1,0:T(8,128)S(1)}, f32[512,128]{1,0:T(8,128)}, u32[]{:S(2)}) copy-start(f32[512,128]{1,0:T(8,128)} %top.5) | copy-start | bytes 786436
  4.5 9.9 %collective-permute-start.3 = (f32[128,256]{1,0:T(8,128)S(1)}, f32[128,256]{1,0:T(8,128)S(1)}, u32[]{:S(2)}, u32[]{:S(2)}) collective-permute-start(f32[128,256]{1,0:T(8,128)S(1)} %get-tuple-element.34.refs_4_), channel_id=1, source_target_pairs={{0,2},{1,3},{2,4},{3,5},{4,6},{5,7},{6,0},{7,1},{8,10},{9,11},{10,... | collective-permute-start | bytes 393224 | tf_op jit(solution)/shard_map/ppermute | solution.py:246
  8.3 17.4 %collective-permute-start = (f32[128,512]{1,0:T(8,128)S(1)}, f32[128,512]{1,0:T(8,128)S(1)}, u32[]{:S(2)}, u32[]{:S(2)}) collective-permute-start(f32[128,512]{1,0:T(8,128)S(1)} %get-tuple-element.31), channel_id=1, source_target_pairs={{0,1},{1,0},{2,3},{3,2},{4,5},{5,4},{6,7},{7,6},{8,9},{9,8},{10,11... | collective-permute-start | bytes 786440 | tf_op jit(solution)/shard_map/ppermute | solution.py:242
  8.5 17.3 %collective-permute-start.1 = (f32[128,512]{1,0:T(8,128)S(1)}, f32[128,512]{1,0:T(8,128)S(1)}, u32[]{:S(2)}, u32[]{:S(2)}) collective-permute-start(f32[128,512]{1,0:T(8,128)S(1)} %get-tuple-element.32), channel_id=1, source_target_pairs={{0,8},{1,9},{2,10},{3,11},{4,12},{5,13},{6,14},{7,15},{8,0},{9,1},... | collective-permute-start | bytes 786440 | tf_op jit(solution)/shard_map/ppermute | solution.py:242
  10.0 15.8 %collective-permute-start.2 = (f32[128,512]{1,0:T(8,128)S(1)}, f32[128,512]{1,0:T(8,128)S(1)}, u32[]{:S(2)}, u32[]{:S(2)}) collective-permute-start(f32[128,512]{1,0:T(8,128)S(1)} %get-tuple-element.33), channel_id=1, source_target_pairs={{0,9},{1,8},{2,11},{3,10},{4,13},{5,12},{6,15},{7,14},{8,1},{9,0},... | collective-permute-start | bytes 786440 | tf_op jit(solution)/shard_map/ppermute | solution.py:242
  11.9 13.9 %collective-permute-start.4 = (f32[128,256]{1,0:T(8,128)S(1)}, f32[128,256]{1,0:T(8,128)S(1)}, u32[]{:S(2)}, u32[]{:S(2)}) collective-permute-start(f32[128,256]{1,0:T(8,128)S(1)} %get-tuple-element.34.refs_4_), channel_id=1, source_target_pairs={{0,6},{1,7},{2,0},{3,1},{4,2},{5,3},{6,4},{7,5},{8,14},{9,15},{10,... | collective-permute-start | bytes 393224 | tf_op jit(solution)/shard_map/ppermute | solution.py:247
  14.5 11.2 %collective-permute-start.5 = (f32[128,256]{1,0:T(8,128)S(1)}, f32[128,256]{1,0:T(8,128)S(1)}, u32[]{:S(2)}, u32[]{:S(2)}) collective-permute-start(f32[128,256]{1,0:T(8,128)S(1)} %collective-permute-done.3.refs_5_), channel_id=1, source_target_pairs={{0,2},{1,3},{2,4},{3,5},{4,6},{5,7},{6,0},{7,1},{8,10},{9,11},{10,... | collective-permute-start | bytes 393224 | tf_op jit(solution)/shard_map/ppermute | solution.py:248
  25.7 4.6 %copy-start.5 = (f32[512,512]{1,0:T(8,128)S(1)}, f32[512,512]{1,0:T(8,128)}, u32[]{:S(2)}) copy-start(f32[512,512]{1,0:T(8,128)} %inverse.5) | copy-start | bytes 3145732
  26.4 5.8 %collective-permute-start.6 = (f32[192,256]{1,0:T(8,128)S(1)}, f32[192,256]{1,0:T(8,128)S(1)}, u32[]{:S(2)}, u32[]{:S(2)}) collective-permute-start(f32[192,256]{1,0:T(8,128)S(1)} %get-tuple-element.36), channel_id=1, source_target_pairs={{0,1},{1,0},{2,3},{3,2},{4,5},{5,4},{6,7},{7,6},{8,9},{9,8},{10,11... | collective-permute-start | bytes 589832 | tf_op jit(solution)/shard_map/ppermute | solution.py:242
  26.5 11.0 %collective-permute-start.7 = (f32[192,256]{1,0:T(8,128)S(1)}, f32[192,256]{1,0:T(8,128)S(1)}, u32[]{:S(2)}, u32[]{:S(2)}) collective-permute-start(f32[192,256]{1,0:T(8,128)S(1)} %get-tuple-element.37), channel_id=1, source_target_pairs={{0,8},{1,9},{2,10},{3,11},{4,12},{5,13},{6,14},{7,15},{8,0},{9,1},... | collective-permute-start | bytes 589832 | tf_op jit(solution)/shard_map/ppermute | solution.py:242
  28.1 9.4 %collective-permute-start.8 = (f32[192,256]{1,0:T(8,128)S(1)}, f32[192,256]{1,0:T(8,128)S(1)}, u32[]{:S(2)}, u32[]{:S(2)}) collective-permute-start(f32[192,256]{1,0:T(8,128)S(1)} %get-tuple-element.38), channel_id=1, source_target_pairs={{0,9},{1,8},{2,11},{3,10},{4,13},{5,12},{6,15},{7,14},{8,1},{9,0},... | collective-permute-start | bytes 589832 | tf_op jit(solution)/shard_map/ppermute | solution.py:242
  37.5 30.1 %copy-start = (f32[128,2048]{1,0:T(8,128)S(1)}, f32[128,2048]{1,0:T(8,128)}, u32[]{:S(2)}) copy-start(f32[128,2048]{1,0:T(8,128)} %capacitance.5) | copy-start | bytes 3145732
  67.6 12.4 %copy-start.9 = (s32[512]{0:T(512)S(1)}, s32[512]{0:T(512)}, u32[]{:S(2)}) copy-start(s32[512]{0:T(512)} %param.8) | copy-start | bytes 6148
  68.2 11.9 %copy-start.6 = (f32[512,128]{1,0:T(8,128)S(1)}, f32[512,128]{1,0:T(8,128)}, u32[]{:S(2)}) copy-start(f32[512,128]{1,0:T(8,128)} %top_solved.3) | copy-start | bytes 786436
  81.6 10.3 %collective-permute-start.9 = (f32[128,256]{1,0:T(8,128)S(1)}, f32[128,256]{1,0:T(8,128)S(1)}, u32[]{:S(2)}, u32[]{:S(2)}) collective-permute-start(f32[128,256]{1,0:T(8,128)S(1)} %get-tuple-element.42.refs_4_), channel_id=1, source_target_pairs={{0,2},{1,3},{2,4},{3,5},{4,6},{5,7},{6,0},{7,1},{8,10},{9,11},{10,... | collective-permute-start | bytes 393224 | tf_op jit(solution)/shard_map/ppermute | solution.py:246
  82.3 10.0 %collective-permute-start.10 = (f32[128,256]{1,0:T(8,128)S(1)}, f32[128,256]{1,0:T(8,128)S(1)}, u32[]{:S(2)}, u32[]{:S(2)}) collective-permute-start(f32[128,256]{1,0:T(8,128)S(1)} %get-tuple-element.42.refs_4_), channel_id=1, source_target_pairs={{0,6},{1,7},{2,0},{3,1},{4,2},{5,3},{6,4},{7,5},{8,14},{9,15},{10,... | collective-permute-start | bytes 393224 | tf_op jit(solution)/shard_map/ppermute | solution.py:247
  91.8 8.4 %collective-permute-start.11 = (f32[128,256]{1,0:T(8,128)S(1)}, f32[128,256]{1,0:T(8,128)S(1)}, u32[]{:S(2)}, u32[]{:S(2)}) collective-permute-start(f32[128,256]{1,0:T(8,128)S(1)} %collective-permute-done.9.refs_5_), channel_id=1, source_target_pairs={{0,2},{1,3},{2,4},{3,5},{4,6},{5,7},{6,0},{7,1},{8,10},{9,11},{10,... | collective-permute-start | bytes 393224 | tf_op jit(solution)/shard_map/ppermute | solution.py:248
  101.8 11.9 %all-to-all-start.3 = ((f32[16,16,128]{2,1,0:T(8,128)}), f32[16,16,128]{2,1,0:T(8,128)S(1)}, u32[]{:S(2)}, u32[]{:S(2)}) async-start(f32[16,16,128]{2,1,0:T(8,128)} %get-tuple-element.43), calls=%async_computation.3 | async-start | bytes 262144 | tf_op jit(solution)/shard_map/all_to_all | solution.py:238
  105.3 5.9 %collective-permute-start.12 = (f32[128,256]{1,0:T(8,128)}, f32[128,256]{1,0:T(8,128)S(1)}, u32[]{:S(2)}, u32[]{:S(2)}) collective-permute-start(f32[128,256]{1,0:T(8,128)} %get-tuple-element.46), channel_id=1, source_target_pairs={{0,1},{1,0},{2,3},{3,2},{4,5},{5,4},{6,7},{7,6},{8,9},{9,8},{10,11... | collective-permute-start | bytes 393224 | tf_op jit(solution)/shard_map/ppermute | solution.py:242
  105.4 5.8 %collective-permute-start.13 = (f32[128,256]{1,0:T(8,128)S(1)}, f32[128,256]{1,0:T(8,128)S(1)}, u32[]{:S(2)}, u32[]{:S(2)}) collective-permute-start(f32[128,256]{1,0:T(8,128)S(1)} %get-tuple-element.47), channel_id=1, source_target_pairs={{0,8},{1,9},{2,10},{3,11},{4,12},{5,13},{6,14},{7,15},{8,0},{9,1},... | collective-permute-start | bytes 393224 | tf_op jit(solution)/shard_map/ppermute | solution.py:242
  107.3 6.3 %collective-permute-start.14 = (f32[128,256]{1,0:T(8,128)S(1)}, f32[128,256]{1,0:T(8,128)S(1)}, u32[]{:S(2)}, u32[]{:S(2)}) collective-permute-start(f32[128,256]{1,0:T(8,128)S(1)} %get-tuple-element.48), channel_id=1, source_target_pairs={{0,9},{1,8},{2,11},{3,10},{4,13},{5,12},{6,15},{7,14},{8,1},{9,0},... | collective-permute-start | bytes 393224 | tf_op jit(solution)/shard_map/ppermute | solution.py:242

commit v6 on v5

--- a/solution.py
+++ b/solution.py
@@ -89,11 +89,29 @@
         copy.wait()
 
 
-def first_kernel(labels, inverse, basis, local, coeffs):
-    sign = signs(labels[...])
-    found = passes(split(inverse[...]), (sign.astype(jnp.bfloat16), None))
-    local[...] = found
-    coeffs[...] = times(basis[...].T, found)
+def first_kernel(labels, inverse, basis, *refs):
+    local_out, coeffs_out, near_labels, near, near_basis, local, coeffs, done = refs
+    quarter = LEAF // 4
+    parts = [slice(k * quarter, (k + 1) * quarter) for k in range(4)]
+    copies = [pltpu.make_async_copy(labels, near_labels, done.at[0])]
+    for k, rows in enumerate(parts):
+        copies.append(pltpu.make_async_copy(inverse.at[rows], near.at[rows], done.at[k + 1]))
+    copies.append(pltpu.make_async_copy(basis, near_basis, done.at[5]))
+    for copy in copies:
+        copy.start()
+    copies[0].wait()
+    sign = (signs(near_labels[...]).astype(jnp.bfloat16), None)
+    for k, rows in enumerate(parts):
+        copies[k + 1].wait()
+        local[rows] = passes(split(near[rows]), sign)
+    leaving = pltpu.make_async_copy(local, local_out, done.at[6])
+    leaving.start()
+    copies[5].wait()
+    coeffs[...] = times(near_basis[...].T, local[...])
+    last = pltpu.make_async_copy(coeffs, coeffs_out, done.at[7])
+    last.start()
+    leaving.wait()
+    last.wait()
 
 
 def lift_kernel(solved, top, lift, folded):
@@ -276,12 +294,24 @@
         compiler_params=pltpu.CompilerParams(vmem_limit_bytes=16 * 1024 * 1024),
     )(group_capacitance)
     blocks = across_square(pieces)
-    local, coeffs = call(
+    local, coeffs = pl.pallas_call(
         first_kernel,
-        [WIDE, COEFFS],
-        [labels, leaf_inverse, leaf_basis],
-        flops=40 * UNIT,
-    )
+        out_shape=[
+            jax.ShapeDtypeStruct(WIDE, jnp.float32),
+            jax.ShapeDtypeStruct(COEFFS, jnp.float32),
+        ],
+        in_specs=[pl.BlockSpec(memory_space=pl.ANY)] * 3,
+        out_specs=[pl.BlockSpec(memory_space=pl.ANY)] * 2,
+        scratch_shapes=[
+            pltpu.VMEM(labels.shape, labels.dtype),
+            pltpu.VMEM(leaf_inverse.shape, jnp.float32),
+            pltpu.VMEM(leaf_basis.shape, jnp.float32),
+            pltpu.VMEM(WIDE, jnp.float32),
+            pltpu.VMEM(COEFFS, jnp.float32),
+            pltpu.SemaphoreType.DMA((8,)),
+        ],
+        compiler_params=pltpu.CompilerParams(vmem_limit_bytes=62900000),
+    )(labels, leaf_inverse, leaf_basis)
     lift, folded = call(
         lift_kernel,
         [(RANK, RANK), (RANK // 2, CLASSES)],

time: 142 us -> 142 us (level)
  Pallas kernels: 10 us -> 12.4 us
  local copies, waits for them, and re-layouts: 2.97 us -> 0.65 us
    pallas_call x0 -> x1, Pallas kernels: none -> 3.29 us  [shards(): pl.pallas_call(first_kernel, out_shape=[jax.ShapeDtypeStruct(WIDE, jnp.fl...]
    unnamed x20, local copies, waits for them, and re-layouts: 2.97 us -> 0.65 us
    pallas_call x13 -> x12, Pallas kernels: 8.26 us -> 7.31 us  [call(): pl.pallas_call(kernel, out_shape=shapes, in_specs=[pl.BlockSpec(memory_sp...]
where the time goes in v6:
time: 142 us; the launch traced here: 141 us
  blocking collectives  66.9 us (47%)
  waiting for transfers between devices  33.8 us (24%)
  starting transfers between devices  26.5 us (19%)
  Pallas kernels  12.4 us (9%)
    all_to_all x5, blocking collectives, exchange(): return lax.all_to_all(tiles, axis, 0, 0, tiled=True)  66.9 us
    ppermute x9, waiting for transfers between devices, across_square(): lax.ppermute(pieces[q], BOTH, square_pairs(q))  11 us
    ppermute x9, starting transfers between devices, across_square(): lax.ppermute(pieces[q], BOTH, square_pairs(q))  10.7 us
    ppermute x2, waiting for transfers between devices, relayed(): after = lax.ppermute(coeffs, BOTH, mirrored_pairs(-1))  8.03 us
    ppermute x2, waiting for transfers between devices, relayed(): opposite = lax.ppermute(before, BOTH, mirrored_pairs(1))  7.99 us
    pallas_call x12, Pallas kernels, call(): pl.pallas_call(kernel, out_shape=shapes, in_specs=[pl.BlockSpec(memory_sp...  7.31 us
    ppermute x2, waiting for transfers between devices, relayed(): before = lax.ppermute(coeffs, BOTH, mirrored_pairs(1))  6.83 us
    ppermute x2, starting transfers between devices, relayed(): after = lax.ppermute(coeffs, BOTH, mirrored_pairs(-1))  5.66 us
  transfers between devices with their start and end apart: 16, of which 8 were waited for; matrix products, arithmetic and copies ran while one was open for 0% of the time, Pallas kernels for 1%

profile of v6, /device:TPU:32, one launch (start us, length us, event | category | flops | bytes accessed | tf_op | source)
XLA Modules:
  0.0 141.2 jit_solution(10974632380009083541)
XLA Ops:
  0.6 3.3 %shard_map.95 = (f32[512,256]{1,0:T(8,128)}, f32[128,256]{1,0:T(8,128)}) custom-call(s32[1,512]{1,0:T(1,128)} %bitcast.1, f32[512,512]{1,0:T(8,128)} %inverse.5, f32[512,128]{1,0:T(8,128)} %basis.3), custom_call_target="tpu_custom_call" | custom-call | tf_op jit(solution)/shard_map/pallas_call | solution.py:297
  3.9 0.0 copy-start.8
  4.0 0.0 copy-start.3
  4.0 3.3 %collective-permute-start.3 = (f32[128,256]{1,0:T(8,128)}, f32[128,256]{1,0:T(8,128)S(1)}, u32[]{:S(2)}, u32[]{:S(2)}) collective-permute-start(f32[128,256]{1,0:T(8,128)} %get-tuple-element.34.refs_4_), channel_id=1, source_target_pairs={{0,2},{1,3},{2,4},{3,5},{4,6},{5,7},{6,0},{7,1},{8,10},{9,11},{10,... | collective-permute-start | bytes 393224 | tf_op jit(solution)/shard_map/ppermute | solution.py:264
  7.3 0.4 shard_map.99
  7.7 0.2 collective-permute-start
  7.9 1.5 %collective-permute-start.1 = (f32[128,512]{1,0:T(8,128)S(1)}, f32[128,512]{1,0:T(8,128)S(1)}, u32[]{:S(2)}, u32[]{:S(2)}) collective-permute-start(f32[128,512]{1,0:T(8,128)S(1)} %get-tuple-element.32), channel_id=1, source_target_pairs={{0,8},{1,9},{2,10},{3,11},{4,12},{5,13},{6,14},{7,15},{8,0},{9,1},... | collective-permute-start | bytes 786440 | tf_op jit(solution)/shard_map/ppermute | solution.py:260
  9.4 1.9 %collective-permute-start.2 = (f32[128,512]{1,0:T(8,128)S(1)}, f32[128,512]{1,0:T(8,128)S(1)}, u32[]{:S(2)}, u32[]{:S(2)}) collective-permute-start(f32[128,512]{1,0:T(8,128)S(1)} %get-tuple-element.33), channel_id=1, source_target_pairs={{0,9},{1,8},{2,11},{3,10},{4,13},{5,12},{6,15},{7,14},{8,1},{9,0},... | collective-permute-start | bytes 786440 | tf_op jit(solution)/shard_map/ppermute | solution.py:260
  11.3 2.2 %collective-permute-start.4 = (f32[128,256]{1,0:T(8,128)S(1)}, f32[128,256]{1,0:T(8,128)S(1)}, u32[]{:S(2)}, u32[]{:S(2)}) collective-permute-start(f32[128,256]{1,0:T(8,128)S(1)} %copy-done.8), channel_id=1, source_target_pairs={{0,6},{1,7},{2,0},{3,1},{4,2},{5,3},{6,4},{7,5},{8,14},{9,15},{10,... | collective-permute-start | bytes 393224 | tf_op jit(solution)/shard_map/ppermute | solution.py:265
  13.5 0.8 collective-permute-done.3.refs_5_
  14.2 2.5 %collective-permute-start.5 = (f32[128,256]{1,0:T(8,128)S(1)}, f32[128,256]{1,0:T(8,128)S(1)}, u32[]{:S(2)}, u32[]{:S(2)}) collective-permute-start(f32[128,256]{1,0:T(8,128)S(1)} %collective-permute-done.3.refs_5_), channel_id=1, source_target_pairs={{0,2},{1,3},{2,4},{3,5},{4,6},{5,7},{6,0},{7,1},{8,10},{9,11},{10,... | collective-permute-start | bytes 393224 | tf_op jit(solution)/shard_map/ppermute | solution.py:266
  16.8 0.3 shard_map.96
  17.1 8.0 %collective-permute-done.4.refs_6_ = f32[128,256]{1,0:T(8,128)S(1)} collective-permute-done((f32[128,256]{1,0:T(8,128)S(1)}, f32[128,256]{1,0:T(8,128)S(1)}, u32[]{:S(2)}, u32[]{:S(2)}) %collective-permute-start.4) | collective-permute-done | bytes 131104 | tf_op jit(solution)/shard_map/ppermute | solution.py:265
  25.2 0.0 copy-start.4
  25.2 0.7 shard_map.100
  25.9 0.1 collective-permute-start.6
  26.0 1.6 %collective-permute-start.7 = (f32[192,256]{1,0:T(8,128)S(1)}, f32[192,256]{1,0:T(8,128)S(1)}, u32[]{:S(2)}, u32[]{:S(2)}) collective-permute-start(f32[192,256]{1,0:T(8,128)S(1)} %get-tuple-element.37), channel_id=1, source_target_pairs={{0,8},{1,9},{2,10},{3,11},{4,12},{5,13},{6,14},{7,15},{8,0},{9,1},... | collective-permute-start | bytes 589832 | tf_op jit(solution)/shard_map/ppermute | solution.py:260
  27.5 1.9 %collective-permute-start.8 = (f32[192,256]{1,0:T(8,128)S(1)}, f32[192,256]{1,0:T(8,128)S(1)}, u32[]{:S(2)}, u32[]{:S(2)}) collective-permute-start(f32[192,256]{1,0:T(8,128)S(1)} %get-tuple-element.38), channel_id=1, source_target_pairs={{0,9},{1,8},{2,11},{3,10},{4,13},{5,12},{6,15},{7,14},{8,1},{9,0},... | collective-permute-start | bytes 589832 | tf_op jit(solution)/shard_map/ppermute | solution.py:260
  29.4 0.3 shard_map.97.projection
  29.8 0.6 copy-done.6
  30.4 0.6 shard_map.98.reach
  31.0 0.6 collective-permute-done.6.refs_1_.refs_5_
  31.6 5.6 %collective-permute-done.7.refs_2_.refs_6_ = f32[192,256]{1,0:T(8,128)S(1)} collective-permute-done((f32[192,256]{1,0:T(8,128)S(1)}, f32[192,256]{1,0:T(8,128)S(1)}, u32[]{:S(2)}, u32[]{:S(2)}) %collective-permute-start.7) | collective-permute-done | bytes 196640 | tf_op jit(solution)/shard_map/ppermute | solution.py:260
  37.2 0.5 shard_map.101
  37.7 14.9 %all_to_all.30.tiles = f32[16,16,128]{2,1,0:T(8,128)S(1)} all-to-all(f32[16,16,128]{2,1,0:T(8,128)S(1)} %get-tuple-element.40), channel_id=1, replica_groups=mesh['grp'=16,'leaf'=16] {'leaf'}, dimensions={0} | all-to-all | bytes 262144 | tf_op jit(solution)/shard_map/all_to_all | solution.py:256
  52.6 14.6 %all_to_all.31.gathered = f32[16,16,128]{2,1,0:T(8,128)S(1)} all-to-all(f32[16,16,128]{2,1,0:T(8,128)S(1)} %shard_map.102), channel_id=1, replica_groups=mesh['grp'=16,'leaf'=16] {'grp'}, dimensions={0} | all-to-all | bytes 262144 | tf_op jit(solution)/shard_map/all_to_all | solution.py:256
  67.3 0.5 shard_map.103
  67.8 0.0 copy-start.7
  67.8 11.8 %all_to_all.32.top_coef = f32[16,16,128]{2,1,0:T(8,128)S(1)} all-to-all(f32[16,16,128]{2,1,0:T(8,128)S(1)} %shard_map.103), channel_id=1, replica_groups=mesh['grp'=16,'leaf'=16] {'leaf'}, dimensions={0} | all-to-all | bytes 262144 | tf_op jit(solution)/shard_map/all_to_all | solution.py:256
  79.7 1.5 %shard_map.104 = (f32[512,256]{1,0:T(8,128)S(1)}, f32[512,256]{1,0:T(8,128)S(1)}, f32[128,256]{1,0:T(8,128)S(1)}, f32[128,256]{1,0:T(8,128)S(1)}) custom-call(f32[512,256]{1,0:T(8,128)S(1)} %get-tuple-element.39.inner, f32[16,16,128]{2,1,0:T(8,128)S(1)} %all_to_all.32.top_coef, s32[1,512]{1,0:T(1,128)S(1)} %bitcast.2, f32[512,128]{1,0:T(8,128)S(1)} %copy-done.7, ...), custom_call_target="tpu_custom_call" | custom-call | flops 704643072 | bytes 3803136 | tf_op jit(solution)/shard_map/pallas_call | solution.py:237
  81.2 0.7 collective-permute-start.9
  81.9 3.5 %collective-permute-start.10 = (f32[128,256]{1,0:T(8,128)S(1)}, f32[128,256]{1,0:T(8,128)S(1)}, u32[]{:S(2)}, u32[]{:S(2)}) collective-permute-start(f32[128,256]{1,0:T(8,128)S(1)} %get-tuple-element.42.refs_4_), channel_id=1, source_target_pairs={{0,6},{1,7},{2,0},{3,1},{4,2},{5,3},{6,4},{7,5},{8,14},{9,15},{10,... | collective-permute-start | bytes 393224 | tf_op jit(solution)/shard_map/ppermute | solution.py:265
  85.4 6.1 %collective-permute-done.9.refs_5_ = f32[128,256]{1,0:T(8,128)S(1)} collective-permute-done((f32[128,256]{1,0:T(8,128)S(1)}, f32[128,256]{1,0:T(8,128)S(1)}, u32[]{:S(2)}, u32[]{:S(2)}) %collective-permute-start.9) | collective-permute-done | bytes 131104 | tf_op jit(solution)/shard_map/ppermute | solution.py:264
  91.5 0.0 collective-permute-start.11
  91.5 0.4 shard_map.105.block_lift
  91.9 8.0 %collective-permute-done.11.refs_7_ = f32[128,256]{1,0:T(8,128)S(1)} collective-permute-done((f32[128,256]{1,0:T(8,128)S(1)}, f32[128,256]{1,0:T(8,128)S(1)}, u32[]{:S(2)}, u32[]{:S(2)}) %collective-permute-start.11) | collective-permute-done | bytes 131104 | tf_op jit(solution)/shard_map/ppermute | solution.py:266
  99.9 1.5 %shard_map.106 = (f32[128,256]{1,0:T(8,128)S(1)}, f32[128,256]{1,0:T(8,128)}, f32[128,256]{1,0:T(8,128)S(1)}, f32[128,256]{1,0:T(8,128)S(1)}, f32[16,16,128]{2,1,0:T(8,128)}) custom-call(f32[128,256]{1,0:T(8,128)S(1)} %get-tuple-element.41.projection, f32[128,512]{1,0:T(8,128)S(1)} %shard_map.105.block_lift, f32[128,512]{1,0:T(8,128)S(1)} %get-tuple-element.30.refs_0_, ...), custom_call_target="tpu_custom_call" | custom-call | flops 503316480 | bytes 2621440 | tf_op jit(solution)/shard_map/pallas_call | solution.py:237
  101.4 3.5 %all-to-all-start.3 = ((f32[16,16,128]{2,1,0:T(8,128)}), f32[16,16,128]{2,1,0:T(8,128)S(1)}, u32[]{:S(2)}, u32[]{:S(2)}) async-start(f32[16,16,128]{2,1,0:T(8,128)} %get-tuple-element.43), calls=%async_computation.3 | async-start | bytes 262144 | tf_op jit(solution)/shard_map/all_to_all | solution.py:256
  104.9 0.2 collective-permute-start.12
  105.1 1.8 %collective-permute-start.13 = (f32[128,256]{1,0:T(8,128)S(1)}, f32[128,256]{1,0:T(8,128)S(1)}, u32[]{:S(2)}, u32[]{:S(2)}) collective-permute-start(f32[128,256]{1,0:T(8,128)S(1)} %get-tuple-element.47), channel_id=1, source_target_pairs={{0,8},{1,9},{2,10},{3,11},{4,12},{5,13},{6,14},{7,15},{8,0},{9,1},... | collective-permute-start | bytes 393224 | tf_op jit(solution)/shard_map/ppermute | solution.py:260
  106.9 1.5 %collective-permute-start.14 = (f32[128,256]{1,0:T(8,128)S(1)}, f32[128,256]{1,0:T(8,128)S(1)}, u32[]{:S(2)}, u32[]{:S(2)}) collective-permute-start(f32[128,256]{1,0:T(8,128)S(1)} %get-tuple-element.48), channel_id=1, source_target_pairs={{0,9},{1,8},{2,11},{3,10},{4,13},{5,12},{6,15},{7,14},{8,1},{9,0},... | collective-permute-start | bytes 393224 | tf_op jit(solution)/shard_map/ppermute | solution.py:260
  108.4 2.4 %collective-permute-done.12.refs_1_ = f32[128,256]{1,0:T(8,128)S(1)} collective-permute-done((f32[128,256]{1,0:T(8,128)}, f32[128,256]{1,0:T(8,128)S(1)}, u32[]{:S(2)}, u32[]{:S(2)}) %collective-permute-start.12) | collective-permute-done | bytes 131104 | tf_op jit(solution)/shard_map/ppermute | solution.py:260
  110.8 2.5 %collective-permute-done.14.refs_3_ = f32[128,256]{1,0:T(8,128)S(1)} collective-permute-done((f32[128,256]{1,0:T(8,128)S(1)}, f32[128,256]{1,0:T(8,128)S(1)}, u32[]{:S(2)}, u32[]{:S(2)}) %collective-permute-start.14) | collective-permute-done | bytes 131104 | tf_op jit(solution)/shard_map/ppermute | solution.py:260
  113.3 0.4 shard_map.107
  113.6 10.8 %all_to_all.33.gathered = f32[16,16,128]{2,1,0:T(8,128)S(1)} all-to-all(f32[16,16,128]{2,1,0:T(8,128)S(1)} %get-tuple-element.50), channel_id=1, replica_groups=mesh['grp'=16,'leaf'=16] {'grp'}, dimensions={0} | all-to-all | bytes 262144 | tf_op jit(solution)/shard_map/all_to_all | solution.py:256
  124.5 0.5 shard_map.108
  125.0 14.7 %all_to_all.34.top_coef = f32[16,16,128]{2,1,0:T(8,128)S(1)} all-to-all(f32[16,16,128]{2,1,0:T(8,128)S(1)} %shard_map.108), channel_id=1, replica_groups=mesh['grp'=16,'leaf'=16] {'leaf'}, dimensions={0} | all-to-all | bytes 262144 | tf_op jit(solution)/shard_map/all_to_all | solution.py:256
  139.7 1.4 shard_map.109
  (24 shorter events, 0.1 us)
Async XLA Ops:
  0.6 6.7 %copy-start.5 = (f32[128,2048]{1,0:T(8,128)S(1)}, f32[128,2048]{1,0:T(8,128)}, u32[]{:S(2)}) copy-start(f32[128,2048]{1,0:T(8,128)} %capacitance.3) | copy-start | bytes 3145732
  3.9 7.3 %copy-start.8 = (f32[128,256]{1,0:T(8,128)S(1)}, f32[128,256]{1,0:T(8,128)}, u32[]{:S(2)}) copy-start(f32[128,256]{1,0:T(8,128)} %get-tuple-element.34.refs_4_) | copy-start | bytes 393220
  3.9 12.8 %copy-start.2 = (f32[512,128]{1,0:T(8,128)S(1)}, f32[512,128]{1,0:T(8,128)}, u32[]{:S(2)}) copy-start(f32[512,128]{1,0:T(8,128)} %solved.5) | copy-start | bytes 786436
  4.0 12.8 %copy-start.3 = (f32[512,128]{1,0:T(8,128)S(1)}, f32[512,128]{1,0:T(8,128)}, u32[]{:S(2)}) copy-start(f32[512,128]{1,0:T(8,128)} %top.5) | copy-start | bytes 786436
  4.0 10.3 %collective-permute-start.3 = (f32[128,256]{1,0:T(8,128)}, f32[128,256]{1,0:T(8,128)S(1)}, u32[]{:S(2)}, u32[]{:S(2)}) collective-permute-start(f32[128,256]{1,0:T(8,128)} %get-tuple-element.34.refs_4_), channel_id=1, source_target_pairs={{0,2},{1,3},{2,4},{3,5},{4,6},{5,7},{6,0},{7,1},{8,10},{9,11},{10,... | collective-permute-start | bytes 393224 | tf_op jit(solution)/shard_map/ppermute | solution.py:264
  7.7 17.5 %collective-permute-start = (f32[128,512]{1,0:T(8,128)S(1)}, f32[128,512]{1,0:T(8,128)S(1)}, u32[]{:S(2)}, u32[]{:S(2)}) collective-permute-start(f32[128,512]{1,0:T(8,128)S(1)} %get-tuple-element.31), channel_id=1, source_target_pairs={{0,1},{1,0},{2,3},{3,2},{4,5},{5,4},{6,7},{7,6},{8,9},{9,8},{10,11... | collective-permute-start | bytes 786440 | tf_op jit(solution)/shard_map/ppermute | solution.py:260
  7.9 17.3 %collective-permute-start.1 = (f32[128,512]{1,0:T(8,128)S(1)}, f32[128,512]{1,0:T(8,128)S(1)}, u32[]{:S(2)}, u32[]{:S(2)}) collective-permute-start(f32[128,512]{1,0:T(8,128)S(1)} %get-tuple-element.32), channel_id=1, source_target_pairs={{0,8},{1,9},{2,10},{3,11},{4,12},{5,13},{6,14},{7,15},{8,0},{9,1},... | collective-permute-start | bytes 786440 | tf_op jit(solution)/shard_map/ppermute | solution.py:260
  9.4 15.8 %collective-permute-start.2 = (f32[128,512]{1,0:T(8,128)S(1)}, f32[128,512]{1,0:T(8,128)S(1)}, u32[]{:S(2)}, u32[]{:S(2)}) collective-permute-start(f32[128,512]{1,0:T(8,128)S(1)} %get-tuple-element.33), channel_id=1, source_target_pairs={{0,9},{1,8},{2,11},{3,10},{4,13},{5,12},{6,15},{7,14},{8,1},{9,0},... | collective-permute-start | bytes 786440 | tf_op jit(solution)/shard_map/ppermute | solution.py:260
  11.3 13.9 %collective-permute-start.4 = (f32[128,256]{1,0:T(8,128)S(1)}, f32[128,256]{1,0:T(8,128)S(1)}, u32[]{:S(2)}, u32[]{:S(2)}) collective-permute-start(f32[128,256]{1,0:T(8,128)S(1)} %copy-done.8), channel_id=1, source_target_pairs={{0,6},{1,7},{2,0},{3,1},{4,2},{5,3},{6,4},{7,5},{8,14},{9,15},{10,... | collective-permute-start | bytes 393224 | tf_op jit(solution)/shard_map/ppermute | solution.py:265
  14.2 10.9 %collective-permute-start.5 = (f32[128,256]{1,0:T(8,128)S(1)}, f32[128,256]{1,0:T(8,128)S(1)}, u32[]{:S(2)}, u32[]{:S(2)}) collective-permute-start(f32[128,256]{1,0:T(8,128)S(1)} %collective-permute-done.3.refs_5_), channel_id=1, source_target_pairs={{0,2},{1,3},{2,4},{3,5},{4,6},{5,7},{6,0},{7,1},{8,10},{9,11},{10,... | collective-permute-start | bytes 393224 | tf_op jit(solution)/shard_map/ppermute | solution.py:266
  25.2 4.3 %copy-start.4 = (f32[512,256]{1,0:T(8,128)S(1)}, f32[512,256]{1,0:T(8,128)}, u32[]{:S(2)}) copy-start(f32[512,256]{1,0:T(8,128)} %get-tuple-element.27.local) | copy-start | bytes 1572868
  25.2 4.6 %copy-start.1 = (f32[512,512]{1,0:T(8,128)S(1)}, f32[512,512]{1,0:T(8,128)}, u32[]{:S(2)}) copy-start(f32[512,512]{1,0:T(8,128)} %inverse.5) | copy-start | bytes 3145732
  25.9 5.8 %collective-permute-start.6 = (f32[192,256]{1,0:T(8,128)S(1)}, f32[192,256]{1,0:T(8,128)S(1)}, u32[]{:S(2)}, u32[]{:S(2)}) collective-permute-start(f32[192,256]{1,0:T(8,128)S(1)} %get-tuple-element.36), channel_id=1, source_target_pairs={{0,1},{1,0},{2,3},{3,2},{4,5},{5,4},{6,7},{7,6},{8,9},{9,8},{10,11... | collective-permute-start | bytes 589832 | tf_op jit(solution)/shard_map/ppermute | solution.py:260
  26.0 11.2 %collective-permute-start.7 = (f32[192,256]{1,0:T(8,128)S(1)}, f32[192,256]{1,0:T(8,128)S(1)}, u32[]{:S(2)}, u32[]{:S(2)}) collective-permute-start(f32[192,256]{1,0:T(8,128)S(1)} %get-tuple-element.37), channel_id=1, source_target_pairs={{0,8},{1,9},{2,10},{3,11},{4,12},{5,13},{6,14},{7,15},{8,0},{9,1},... | collective-permute-start | bytes 589832 | tf_op jit(solution)/shard_map/ppermute | solution.py:260
  27.5 9.6 %collective-permute-start.8 = (f32[192,256]{1,0:T(8,128)S(1)}, f32[192,256]{1,0:T(8,128)S(1)}, u32[]{:S(2)}, u32[]{:S(2)}) collective-permute-start(f32[192,256]{1,0:T(8,128)S(1)} %get-tuple-element.38), channel_id=1, source_target_pairs={{0,9},{1,8},{2,11},{3,10},{4,13},{5,12},{6,15},{7,14},{8,1},{9,0},... | collective-permute-start | bytes 589832 | tf_op jit(solution)/shard_map/ppermute | solution.py:260
  29.4 1.0 copy-start.6
  37.2 30.1 %copy-start = (f32[128,2048]{1,0:T(8,128)S(1)}, f32[128,2048]{1,0:T(8,128)}, u32[]{:S(2)}) copy-start(f32[128,2048]{1,0:T(8,128)} %capacitance.5) | copy-start | bytes 3145732
  67.3 12.4 %copy-start.9 = (s32[512]{0:T(512)S(1)}, s32[512]{0:T(512)}, u32[]{:S(2)}) copy-start(s32[512]{0:T(512)} %param.8) | copy-start | bytes 6148
  67.8 11.9 %copy-start.7 = (f32[512,128]{1,0:T(8,128)S(1)}, f32[512,128]{1,0:T(8,128)}, u32[]{:S(2)}) copy-start(f32[512,128]{1,0:T(8,128)} %top_solved.3) | copy-start | bytes 786436
  81.2 10.3 %collective-permute-start.9 = (f32[128,256]{1,0:T(8,128)S(1)}, f32[128,256]{1,0:T(8,128)S(1)}, u32[]{:S(2)}, u32[]{:S(2)}) collective-permute-start(f32[128,256]{1,0:T(8,128)S(1)} %get-tuple-element.42.refs_4_), channel_id=1, source_target_pairs={{0,2},{1,3},{2,4},{3,5},{4,6},{5,7},{6,0},{7,1},{8,10},{9,11},{10,... | collective-permute-start | bytes 393224 | tf_op jit(solution)/shard_map/ppermute | solution.py:264
  81.9 10.0 %collective-permute-start.10 = (f32[128,256]{1,0:T(8,128)S(1)}, f32[128,256]{1,0:T(8,128)S(1)}, u32[]{:S(2)}, u32[]{:S(2)}) collective-permute-start(f32[128,256]{1,0:T(8,128)S(1)} %get-tuple-element.42.refs_4_), channel_id=1, source_target_pairs={{0,6},{1,7},{2,0},{3,1},{4,2},{5,3},{6,4},{7,5},{8,14},{9,15},{10,... | collective-permute-start | bytes 393224 | tf_op jit(solution)/shard_map/ppermute | solution.py:265
  91.5 8.4 %collective-permute-start.11 = (f32[128,256]{1,0:T(8,128)S(1)}, f32[128,256]{1,0:T(8,128)S(1)}, u32[]{:S(2)}, u32[]{:S(2)}) collective-permute-start(f32[128,256]{1,0:T(8,128)S(1)} %collective-permute-done.9.refs_5_), channel_id=1, source_target_pairs={{0,2},{1,3},{2,4},{3,5},{4,6},{5,7},{6,0},{7,1},{8,10},{9,11},{10,... | collective-permute-start | bytes 393224 | tf_op jit(solution)/shard_map/ppermute | solution.py:266
  101.4 11.9 %all-to-all-start.3 = ((f32[16,16,128]{2,1,0:T(8,128)}), f32[16,16,128]{2,1,0:T(8,128)S(1)}, u32[]{:S(2)}, u32[]{:S(2)}) async-start(f32[16,16,128]{2,1,0:T(8,128)} %get-tuple-element.43), calls=%async_computation.3 | async-start | bytes 262144 | tf_op jit(solution)/shard_map/all_to_all | solution.py:256
  104.9 5.9 %collective-permute-start.12 = (f32[128,256]{1,0:T(8,128)}, f32[128,256]{1,0:T(8,128)S(1)}, u32[]{:S(2)}, u32[]{:S(2)}) collective-permute-start(f32[128,256]{1,0:T(8,128)} %get-tuple-element.46), channel_id=1, source_target_pairs={{0,1},{1,0},{2,3},{3,2},{4,5},{5,4},{6,7},{7,6},{8,9},{9,8},{10,11... | collective-permute-start | bytes 393224 | tf_op jit(solution)/shard_map/ppermute | solution.py:260
  105.1 5.7 %collective-permute-start.13 = (f32[128,256]{1,0:T(8,128)S(1)}, f32[128,256]{1,0:T(8,128)S(1)}, u32[]{:S(2)}, u32[]{:S(2)}) collective-permute-start(f32[128,256]{1,0:T(8,128)S(1)} %get-tuple-element.47), channel_id=1, source_target_pairs={{0,8},{1,9},{2,10},{3,11},{4,12},{5,13},{6,14},{7,15},{8,0},{9,1},... | collective-permute-start | bytes 393224 | tf_op jit(solution)/shard_map/ppermute | solution.py:260
  106.9 6.3 %collective-permute-start.14 = (f32[128,256]{1,0:T(8,128)S(1)}, f32[128,256]{1,0:T(8,128)S(1)}, u32[]{:S(2)}, u32[]{:S(2)}) collective-permute-start(f32[128,256]{1,0:T(8,128)S(1)} %get-tuple-element.48), channel_id=1, source_target_pairs={{0,9},{1,8},{2,11},{3,10},{4,13},{5,12},{6,15},{7,14},{8,1},{9,0},... | collective-permute-start | bytes 393224 | tf_op jit(solution)/shard_map/ppermute | solution.py:260

commit v7 on v6

--- a/solution.py
+++ b/solution.py
@@ -145,15 +145,12 @@
     return pl.ds(pl.multiple_of(((step + k * sign + 4) % 4) * RANK, RANK), RANK)
 
 
-def partial_coefs(blocks, pieces, stacked):
+def group_kernel(lift, *refs):
+    blocks, pieces, stacked = refs[:4], refs[4:8], refs[12]
     for piece, k in zip(pieces, (0, -1, 1, 2)):
         stacked[row_of(k), :] = piece[...]
     block = jnp.concatenate([part[...] for part in blocks], axis=0)
-    return passes(split(block), split(stacked[...]))
-
-
-def group_kernel(lift, *refs):
-    rows = partial_coefs(refs[:4], refs[4:8], refs[12])
+    rows = passes(split(block), split(stacked[...]))
     for q in range(4):
         refs[8 + q][:RANK, :] = rows[q * RANK : (q + 1) * RANK]
         refs[8 + q][RANK:, :] = lift[...]
@@ -167,9 +164,20 @@
     tiles[...] = (projection[...] - both[LEAF:]).T.reshape(16, 16, RANK)
 
 
-def later_group_kernel(projection, block_lift, *refs):
-    partials, tiles = refs[8:12], refs[12]
-    rows = partial_coefs([*refs[:4], block_lift], refs[4:8], refs[13])
+def columns_of(blocks, k):
+    return jnp.concatenate([part[:, row_of(k)] for part in blocks], axis=0)
+
+
+def near_kernel(*refs):
+    blocks, pieces, out = refs[:-4], refs[-4:-1], refs[-1]
+    left = jnp.concatenate([columns_of(blocks, k) for k in (0, -1, 1)], axis=1)
+    right = jnp.concatenate([piece[...] for piece in pieces], axis=0)
+    out[...] = times(left, right)
+
+
+def later_group_kernel(projection, near, far, *refs):
+    blocks, partials, tiles = refs[:5], refs[5:9], refs[9]
+    rows = near[...] + times(columns_of(blocks, 2), far[...])
     for q in range(4):
         partials[q][...] = rows[q * RANK : (q + 1) * RANK]
     tiles[...] = (projection[...] - rows[4 * RANK :]).T.reshape(16, 16, RANK)
@@ -258,6 +266,10 @@
 
 def across_square(pieces):
     return [pieces[0]] + [lax.ppermute(pieces[q], BOTH, square_pairs(q)) for q in range(1, 4)]
+
+
+def diagonal_first(parts):
+    return [parts[0], parts[3], parts[2], parts[1]]
 
 
 def relayed(coeffs):
@@ -337,7 +349,7 @@
     inner, tiles = call(
         inner_kernel,
         [WIDE, TILES],
-        [local, leaf_solved, lift, projection, reach, *sent],
+        [local, leaf_solved, lift, projection, reach, *diagonal_first(sent)],
         flops=10 * UNIT,
     )
     (shares,) = call(sum_kernel, [TILES], [exchange(tiles, "leaf")])
@@ -352,17 +364,26 @@
     (block_lift,) = call(
         block_lift_kernel, [(RANK, 4 * RANK)], [*blocks, *sent], flops=16 * UNIT
     )
+    blocks = [*blocks, block_lift]
+    *pieces, far = relayed(coeffs)
+    (near,) = call(
+        near_kernel, [(5 * RANK, CLASSES)], [*blocks, *pieces], flops=30 * UNIT
+    )
     *partials, tiles = call(
         later_group_kernel,
         [COEFFS] * 4 + [TILES],
-        [projection, block_lift, *blocks, *relayed(coeffs)],
-        scratch=[STACK],
-        flops=40 * UNIT,
+        [projection, near, far, *blocks],
+        flops=10 * UNIT,
     )
     shares, inner = call(
         sum_inner_kernel,
         [TILES, WIDE],
-        [exchange(tiles, "leaf"), local, leaf_solved, *across_square(partials)],
+        [
+            exchange(tiles, "leaf"),
+            local,
+            leaf_solved,
+            *diagonal_first(across_square(partials)),
+        ],
         flops=8 * UNIT,
     )
     top_coef = top_solve(shares, top_capacitance)

time: 142 us -> 141 us (level)
    pallas_call x12 -> x13, Pallas kernels: 7.31 us -> 7.67 us  [call(): pl.pallas_call(kernel, out_shape=shapes, in_specs=[pl.BlockSpec(memory_sp...]
  transfers between devices with their start and end apart: 16 -> 16, of which waited for: 8 -> 9; matrix products, arithmetic and copies ran while one was open for 0% -> 0% of each run, Pallas kernels for 1% -> 2%
where the time goes in v7:
time: 141 us; the launch traced here: 140 us
  blocking collectives  66.8 us (47%)
  waiting for transfers between devices  32.8 us (23%)
  starting transfers between devices  26.5 us (19%)
  Pallas kernels  12.7 us (9%)
    all_to_all x5, blocking collectives, exchange(): return lax.all_to_all(tiles, axis, 0, 0, tiled=True)  66.8 us
    ppermute x9, starting transfers between devices, across_square(): lax.ppermute(pieces[q], BOTH, square_pairs(q))  10.7 us
    ppermute x9, waiting for transfers between devices, across_square(): lax.ppermute(pieces[q], BOTH, square_pairs(q))  10.6 us
    ppermute x2, waiting for transfers between devices, relayed(): after = lax.ppermute(coeffs, BOTH, mirrored_pairs(-1))  8.03 us
    pallas_call x13, Pallas kernels, call(): pl.pallas_call(kernel, out_shape=shapes, in_specs=[pl.BlockSpec(memory_sp...  7.67 us
    ppermute x2, waiting for transfers between devices, relayed(): opposite = lax.ppermute(before, BOTH, mirrored_pairs(1))  7.29 us
    ppermute x2, waiting for transfers between devices, relayed(): before = lax.ppermute(coeffs, BOTH, mirrored_pairs(1))  6.83 us
    ppermute x2, starting transfers between devices, relayed(): after = lax.ppermute(coeffs, BOTH, mirrored_pairs(-1))  5.67 us
  transfers between devices with their start and end apart: 16, of which 9 were waited for; matrix products, arithmetic and copies ran while one was open for 0% of the time, Pallas kernels for 2%

profile of v7, /device:TPU:32, one launch (start us, length us, event | category | flops | bytes accessed | tf_op | source)
XLA Modules:
  0.0 140.4 jit_solution(14690763564492900288)
XLA Ops:
  0.6 3.3 %shard_map.95 = (f32[512,256]{1,0:T(8,128)}, f32[128,256]{1,0:T(8,128)}) custom-call(s32[1,512]{1,0:T(1,128)} %bitcast.1, f32[512,512]{1,0:T(8,128)} %inverse.5, f32[512,128]{1,0:T(8,128)} %basis.3), custom_call_target="tpu_custom_call" | custom-call | tf_op jit(solution)/shard_map/pallas_call | solution.py:309
  4.0 0.0 copy-start.3
  4.0 3.3 %collective-permute-start.3 = (f32[128,256]{1,0:T(8,128)}, f32[128,256]{1,0:T(8,128)S(1)}, u32[]{:S(2)}, u32[]{:S(2)}) collective-permute-start(f32[128,256]{1,0:T(8,128)} %get-tuple-element.34.refs_4_), channel_id=1, source_target_pairs={{0,2},{1,3},{2,4},{3,5},{4,6},{5,7},{6,0},{7,1},{8,10},{9,11},{10,... | collective-permute-start | bytes 393224 | tf_op jit(solution)/shard_map/ppermute | solution.py:276
  7.3 0.4 shard_map.99
  7.7 0.2 collective-permute-start
  7.9 1.5 %collective-permute-start.1 = (f32[128,512]{1,0:T(8,128)S(1)}, f32[128,512]{1,0:T(8,128)S(1)}, u32[]{:S(2)}, u32[]{:S(2)}) collective-permute-start(f32[128,512]{1,0:T(8,128)S(1)} %get-tuple-element.32), channel_id=1, source_target_pairs={{0,8},{1,9},{2,10},{3,11},{4,12},{5,13},{6,14},{7,15},{8,0},{9,1},... | collective-permute-start | bytes 786440 | tf_op jit(solution)/shard_map/ppermute | solution.py:268
  9.4 1.9 %collective-permute-start.2 = (f32[128,512]{1,0:T(8,128)S(1)}, f32[128,512]{1,0:T(8,128)S(1)}, u32[]{:S(2)}, u32[]{:S(2)}) collective-permute-start(f32[128,512]{1,0:T(8,128)S(1)} %get-tuple-element.33), channel_id=1, source_target_pairs={{0,9},{1,8},{2,11},{3,10},{4,13},{5,12},{6,15},{7,14},{8,1},{9,0},... | collective-permute-start | bytes 786440 | tf_op jit(solution)/shard_map/ppermute | solution.py:268
  11.3 2.2 %collective-permute-start.4 = (f32[128,256]{1,0:T(8,128)S(1)}, f32[128,256]{1,0:T(8,128)S(1)}, u32[]{:S(2)}, u32[]{:S(2)}) collective-permute-start(f32[128,256]{1,0:T(8,128)S(1)} %copy-done.8), channel_id=1, source_target_pairs={{0,6},{1,7},{2,0},{3,1},{4,2},{5,3},{6,4},{7,5},{8,14},{9,15},{10,... | collective-permute-start | bytes 393224 | tf_op jit(solution)/shard_map/ppermute | solution.py:277
  13.5 0.8 collective-permute-done.3.refs_5_
  14.2 2.5 %collective-permute-start.5 = (f32[128,256]{1,0:T(8,128)S(1)}, f32[128,256]{1,0:T(8,128)S(1)}, u32[]{:S(2)}, u32[]{:S(2)}) collective-permute-start(f32[128,256]{1,0:T(8,128)S(1)} %collective-permute-done.3.refs_5_), channel_id=1, source_target_pairs={{0,2},{1,3},{2,4},{3,5},{4,6},{5,7},{6,0},{7,1},{8,10},{9,11},{10,... | collective-permute-start | bytes 393224 | tf_op jit(solution)/shard_map/ppermute | solution.py:278
  16.8 0.3 shard_map.96
  17.1 8.0 %collective-permute-done.4.refs_6_ = f32[128,256]{1,0:T(8,128)S(1)} collective-permute-done((f32[128,256]{1,0:T(8,128)S(1)}, f32[128,256]{1,0:T(8,128)S(1)}, u32[]{:S(2)}, u32[]{:S(2)}) %collective-permute-start.4) | collective-permute-done | bytes 131104 | tf_op jit(solution)/shard_map/ppermute | solution.py:277
  25.2 0.0 copy-start.4
  25.2 0.7 shard_map.100
  25.9 0.1 collective-permute-start.6
  26.0 1.6 %collective-permute-start.7 = (f32[192,256]{1,0:T(8,128)S(1)}, f32[192,256]{1,0:T(8,128)S(1)}, u32[]{:S(2)}, u32[]{:S(2)}) collective-permute-start(f32[192,256]{1,0:T(8,128)S(1)} %get-tuple-element.37), channel_id=1, source_target_pairs={{0,8},{1,9},{2,10},{3,11},{4,12},{5,13},{6,14},{7,15},{8,0},{9,1},... | collective-permute-start | bytes 589832 | tf_op jit(solution)/shard_map/ppermute | solution.py:268
  27.5 1.9 %collective-permute-start.8 = (f32[192,256]{1,0:T(8,128)S(1)}, f32[192,256]{1,0:T(8,128)S(1)}, u32[]{:S(2)}, u32[]{:S(2)}) collective-permute-start(f32[192,256]{1,0:T(8,128)S(1)} %get-tuple-element.38), channel_id=1, source_target_pairs={{0,1},{1,0},{2,3},{3,2},{4,5},{5,4},{6,7},{7,6},{8,9},{9,8},{10,11... | collective-permute-start | bytes 589832 | tf_op jit(solution)/shard_map/ppermute | solution.py:268
  29.4 0.3 shard_map.97.projection
  29.8 0.6 copy-done.6
  30.4 0.6 shard_map.98.reach
  31.0 2.8 %collective-permute-done.6.refs_1_.refs_7_ = f32[192,256]{1,0:T(8,128)S(1)} collective-permute-done((f32[192,256]{1,0:T(8,128)S(1)}, f32[192,256]{1,0:T(8,128)S(1)}, u32[]{:S(2)}, u32[]{:S(2)}) %collective-permute-start.6) | collective-permute-done | bytes 196640 | tf_op jit(solution)/shard_map/ppermute | solution.py:268
  33.9 3.3 %collective-permute-done.7.refs_2_.refs_6_ = f32[192,256]{1,0:T(8,128)S(1)} collective-permute-done((f32[192,256]{1,0:T(8,128)S(1)}, f32[192,256]{1,0:T(8,128)S(1)}, u32[]{:S(2)}, u32[]{:S(2)}) %collective-permute-start.7) | collective-permute-done | bytes 196640 | tf_op jit(solution)/shard_map/ppermute | solution.py:268
  37.2 0.5 shard_map.101
  37.7 14.2 %all_to_all.30.tiles = f32[16,16,128]{2,1,0:T(8,128)S(1)} all-to-all(f32[16,16,128]{2,1,0:T(8,128)S(1)} %get-tuple-element.40), channel_id=1, replica_groups=mesh['grp'=16,'leaf'=16] {'leaf'}, dimensions={0} | all-to-all | bytes 262144 | tf_op jit(solution)/shard_map/all_to_all | solution.py:264
  51.9 15.0 %all_to_all.31.gathered = f32[16,16,128]{2,1,0:T(8,128)S(1)} all-to-all(f32[16,16,128]{2,1,0:T(8,128)S(1)} %shard_map.102), channel_id=1, replica_groups=mesh['grp'=16,'leaf'=16] {'grp'}, dimensions={0} | all-to-all | bytes 262144 | tf_op jit(solution)/shard_map/all_to_all | solution.py:264
  67.0 0.5 shard_map.103
  67.5 11.8 %all_to_all.32.top_coef = f32[16,16,128]{2,1,0:T(8,128)S(1)} all-to-all(f32[16,16,128]{2,1,0:T(8,128)S(1)} %shard_map.103), channel_id=1, replica_groups=mesh['grp'=16,'leaf'=16] {'leaf'}, dimensions={0} | all-to-all | bytes 262144 | tf_op jit(solution)/shard_map/all_to_all | solution.py:264
  79.3 1.5 %shard_map.104 = (f32[512,256]{1,0:T(8,128)S(1)}, f32[512,256]{1,0:T(8,128)S(1)}, f32[128,256]{1,0:T(8,128)S(1)}, f32[128,256]{1,0:T(8,128)S(1)}) custom-call(f32[512,256]{1,0:T(8,128)S(1)} %get-tuple-element.39.inner, f32[16,16,128]{2,1,0:T(8,128)S(1)} %all_to_all.32.top_coef, s32[1,512]{1,0:T(1,128)S(1)} %bitcast.2, f32[512,128]{1,0:T(8,128)S(1)} %copy-done.7, ...), custom_call_target="tpu_custom_call" | custom-call | flops 704643072 | bytes 3803136 | tf_op jit(solution)/shard_map/pallas_call | solution.py:245
  80.8 0.7 collective-permute-start.9
  81.5 3.5 %collective-permute-start.10 = (f32[128,256]{1,0:T(8,128)S(1)}, f32[128,256]{1,0:T(8,128)S(1)}, u32[]{:S(2)}, u32[]{:S(2)}) collective-permute-start(f32[128,256]{1,0:T(8,128)S(1)} %get-tuple-element.42.refs_5_), channel_id=1, source_target_pairs={{0,6},{1,7},{2,0},{3,1},{4,2},{5,3},{6,4},{7,5},{8,14},{9,15},{10,... | collective-permute-start | bytes 393224 | tf_op jit(solution)/shard_map/ppermute | solution.py:277
  85.0 6.0 %collective-permute-done.9.refs_6_ = f32[128,256]{1,0:T(8,128)S(1)} collective-permute-done((f32[128,256]{1,0:T(8,128)S(1)}, f32[128,256]{1,0:T(8,128)S(1)}, u32[]{:S(2)}, u32[]{:S(2)}) %collective-permute-start.9) | collective-permute-done | bytes 131104 | tf_op jit(solution)/shard_map/ppermute | solution.py:276
  91.1 0.0 collective-permute-start.11
  91.1 0.4 shard_map.105.refs_4_
  91.5 0.7 shard_map.106.near
  92.2 7.3 %collective-permute-done.11.far = f32[128,256]{1,0:T(8,128)S(1)} collective-permute-done((f32[128,256]{1,0:T(8,128)S(1)}, f32[128,256]{1,0:T(8,128)S(1)}, u32[]{:S(2)}, u32[]{:S(2)}) %collective-permute-start.11) | collective-permute-done | bytes 131104 | tf_op jit(solution)/shard_map/ppermute | solution.py:278
  99.5 1.1 shard_map.107
  100.6 3.5 %all-to-all-start.3 = ((f32[16,16,128]{2,1,0:T(8,128)}), f32[16,16,128]{2,1,0:T(8,128)S(1)}, u32[]{:S(2)}, u32[]{:S(2)}) async-start(f32[16,16,128]{2,1,0:T(8,128)} %get-tuple-element.43), calls=%async_computation.3 | async-start | bytes 262144 | tf_op jit(solution)/shard_map/all_to_all | solution.py:264
  104.1 1.5 %collective-permute-start.12 = (f32[128,256]{1,0:T(8,128)}, f32[128,256]{1,0:T(8,128)S(1)}, u32[]{:S(2)}, u32[]{:S(2)}) collective-permute-start(f32[128,256]{1,0:T(8,128)} %get-tuple-element.46), channel_id=1, source_target_pairs={{0,9},{1,8},{2,11},{3,10},{4,13},{5,12},{6,15},{7,14},{8,1},{9,0},... | collective-permute-start | bytes 393224 | tf_op jit(solution)/shard_map/ppermute | solution.py:268
  105.6 0.2 collective-permute-start.13
  105.8 1.9 %collective-permute-start.14 = (f32[128,256]{1,0:T(8,128)S(1)}, f32[128,256]{1,0:T(8,128)S(1)}, u32[]{:S(2)}, u32[]{:S(2)}) collective-permute-start(f32[128,256]{1,0:T(8,128)S(1)} %get-tuple-element.48), channel_id=1, source_target_pairs={{0,1},{1,0},{2,3},{3,2},{4,5},{5,4},{6,7},{7,6},{8,9},{9,8},{10,11... | collective-permute-start | bytes 393224 | tf_op jit(solution)/shard_map/ppermute | solution.py:268
  107.7 3.3 %collective-permute-done.12.refs_1_ = f32[128,256]{1,0:T(8,128)S(1)} collective-permute-done((f32[128,256]{1,0:T(8,128)}, f32[128,256]{1,0:T(8,128)S(1)}, u32[]{:S(2)}, u32[]{:S(2)}) %collective-permute-start.12) | collective-permute-done | bytes 131104 | tf_op jit(solution)/shard_map/ppermute | solution.py:268
  111.0 1.1 collective-permute-done.13.refs_2_
  112.0 0.1 collective-permute-done.14.refs_3_
  112.1 0.4 shard_map.108
  112.5 10.8 %all_to_all.33.gathered = f32[16,16,128]{2,1,0:T(8,128)S(1)} all-to-all(f32[16,16,128]{2,1,0:T(8,128)S(1)} %get-tuple-element.50), channel_id=1, replica_groups=mesh['grp'=16,'leaf'=16] {'grp'}, dimensions={0} | all-to-all | bytes 262144 | tf_op jit(solution)/shard_map/all_to_all | solution.py:264
  123.3 0.5 shard_map.109
  123.9 15.0 %all_to_all.34.top_coef = f32[16,16,128]{2,1,0:T(8,128)S(1)} all-to-all(f32[16,16,128]{2,1,0:T(8,128)S(1)} %shard_map.109), channel_id=1, replica_groups=mesh['grp'=16,'leaf'=16] {'leaf'}, dimensions={0} | all-to-all | bytes 262144 | tf_op jit(solution)/shard_map/all_to_all | solution.py:264
  138.9 1.4 shard_map.110
  (25 shorter events, 0.1 us)
Async XLA Ops:
  0.6 6.7 %copy-start.5 = (f32[128,2048]{1,0:T(8,128)S(1)}, f32[128,2048]{1,0:T(8,128)}, u32[]{:S(2)}) copy-start(f32[128,2048]{1,0:T(8,128)} %capacitance.3) | copy-start | bytes 3145732
  3.9 7.3 %copy-start.8 = (f32[128,256]{1,0:T(8,128)S(1)}, f32[128,256]{1,0:T(8,128)}, u32[]{:S(2)}) copy-start(f32[128,256]{1,0:T(8,128)} %get-tuple-element.34.refs_4_) | copy-start | bytes 393220
  3.9 12.8 %copy-start.2 = (f32[512,128]{1,0:T(8,128)S(1)}, f32[512,128]{1,0:T(8,128)}, u32[]{:S(2)}) copy-start(f32[512,128]{1,0:T(8,128)} %solved.5) | copy-start | bytes 786436
  4.0 12.8 %copy-start.3 = (f32[512,128]{1,0:T(8,128)S(1)}, f32[512,128]{1,0:T(8,128)}, u32[]{:S(2)}) copy-start(f32[512,128]{1,0:T(8,128)} %top.5) | copy-start | bytes 786436
  4.0 10.3 %collective-permute-start.3 = (f32[128,256]{1,0:T(8,128)}, f32[128,256]{1,0:T(8,128)S(1)}, u32[]{:S(2)}, u32[]{:S(2)}) collective-permute-start(f32[128,256]{1,0:T(8,128)} %get-tuple-element.34.refs_4_), channel_id=1, source_target_pairs={{0,2},{1,3},{2,4},{3,5},{4,6},{5,7},{6,0},{7,1},{8,10},{9,11},{10,... | collective-permute-start | bytes 393224 | tf_op jit(solution)/shard_map/ppermute | solution.py:276
  7.7 17.5 %collective-permute-start = (f32[128,512]{1,0:T(8,128)S(1)}, f32[128,512]{1,0:T(8,128)S(1)}, u32[]{:S(2)}, u32[]{:S(2)}) collective-permute-start(f32[128,512]{1,0:T(8,128)S(1)} %get-tuple-element.31), channel_id=1, source_target_pairs={{0,1},{1,0},{2,3},{3,2},{4,5},{5,4},{6,7},{7,6},{8,9},{9,8},{10,11... | collective-permute-start | bytes 786440 | tf_op jit(solution)/shard_map/ppermute | solution.py:268
  7.9 17.3 %collective-permute-start.1 = (f32[128,512]{1,0:T(8,128)S(1)}, f32[128,512]{1,0:T(8,128)S(1)}, u32[]{:S(2)}, u32[]{:S(2)}) collective-permute-start(f32[128,512]{1,0:T(8,128)S(1)} %get-tuple-element.32), channel_id=1, source_target_pairs={{0,8},{1,9},{2,10},{3,11},{4,12},{5,13},{6,14},{7,15},{8,0},{9,1},... | collective-permute-start | bytes 786440 | tf_op jit(solution)/shard_map/ppermute | solution.py:268
  9.4 15.8 %collective-permute-start.2 = (f32[128,512]{1,0:T(8,128)S(1)}, f32[128,512]{1,0:T(8,128)S(1)}, u32[]{:S(2)}, u32[]{:S(2)}) collective-permute-start(f32[128,512]{1,0:T(8,128)S(1)} %get-tuple-element.33), channel_id=1, source_target_pairs={{0,9},{1,8},{2,11},{3,10},{4,13},{5,12},{6,15},{7,14},{8,1},{9,0},... | collective-permute-start | bytes 786440 | tf_op jit(solution)/shard_map/ppermute | solution.py:268
  11.3 13.9 %collective-permute-start.4 = (f32[128,256]{1,0:T(8,128)S(1)}, f32[128,256]{1,0:T(8,128)S(1)}, u32[]{:S(2)}, u32[]{:S(2)}) collective-permute-start(f32[128,256]{1,0:T(8,128)S(1)} %copy-done.8), channel_id=1, source_target_pairs={{0,6},{1,7},{2,0},{3,1},{4,2},{5,3},{6,4},{7,5},{8,14},{9,15},{10,... | collective-permute-start | bytes 393224 | tf_op jit(solution)/shard_map/ppermute | solution.py:277
  14.2 10.9 %collective-permute-start.5 = (f32[128,256]{1,0:T(8,128)S(1)}, f32[128,256]{1,0:T(8,128)S(1)}, u32[]{:S(2)}, u32[]{:S(2)}) collective-permute-start(f32[128,256]{1,0:T(8,128)S(1)} %collective-permute-done.3.refs_5_), channel_id=1, source_target_pairs={{0,2},{1,3},{2,4},{3,5},{4,6},{5,7},{6,0},{7,1},{8,10},{9,11},{10,... | collective-permute-start | bytes 393224 | tf_op jit(solution)/shard_map/ppermute | solution.py:278
  25.2 4.3 %copy-start.4 = (f32[512,256]{1,0:T(8,128)S(1)}, f32[512,256]{1,0:T(8,128)}, u32[]{:S(2)}) copy-start(f32[512,256]{1,0:T(8,128)} %get-tuple-element.27.local) | copy-start | bytes 1572868
  25.2 4.6 %copy-start.1 = (f32[512,512]{1,0:T(8,128)S(1)}, f32[512,512]{1,0:T(8,128)}, u32[]{:S(2)}) copy-start(f32[512,512]{1,0:T(8,128)} %inverse.5) | copy-start | bytes 3145732
  25.9 8.0 %collective-permute-start.6 = (f32[192,256]{1,0:T(8,128)S(1)}, f32[192,256]{1,0:T(8,128)S(1)}, u32[]{:S(2)}, u32[]{:S(2)}) collective-permute-start(f32[192,256]{1,0:T(8,128)S(1)} %get-tuple-element.36), channel_id=1, source_target_pairs={{0,9},{1,8},{2,11},{3,10},{4,13},{5,12},{6,15},{7,14},{8,1},{9,0},... | collective-permute-start | bytes 589832 | tf_op jit(solution)/shard_map/ppermute | solution.py:268
  26.0 11.2 %collective-permute-start.7 = (f32[192,256]{1,0:T(8,128)S(1)}, f32[192,256]{1,0:T(8,128)S(1)}, u32[]{:S(2)}, u32[]{:S(2)}) collective-permute-start(f32[192,256]{1,0:T(8,128)S(1)} %get-tuple-element.37), channel_id=1, source_target_pairs={{0,8},{1,9},{2,10},{3,11},{4,12},{5,13},{6,14},{7,15},{8,0},{9,1},... | collective-permute-start | bytes 589832 | tf_op jit(solution)/shard_map/ppermute | solution.py:268
  27.5 9.6 %collective-permute-start.8 = (f32[192,256]{1,0:T(8,128)S(1)}, f32[192,256]{1,0:T(8,128)S(1)}, u32[]{:S(2)}, u32[]{:S(2)}) collective-permute-start(f32[192,256]{1,0:T(8,128)S(1)} %get-tuple-element.38), channel_id=1, source_target_pairs={{0,1},{1,0},{2,3},{3,2},{4,5},{5,4},{6,7},{7,6},{8,9},{9,8},{10,11... | collective-permute-start | bytes 589832 | tf_op jit(solution)/shard_map/ppermute | solution.py:268
  29.4 1.0 copy-start.6
  37.2 29.8 %copy-start = (f32[128,2048]{1,0:T(8,128)S(1)}, f32[128,2048]{1,0:T(8,128)}, u32[]{:S(2)}) copy-start(f32[128,2048]{1,0:T(8,128)} %capacitance.5) | copy-start | bytes 3145732
  67.0 12.3 %copy-start.9 = (s32[512]{0:T(512)S(1)}, s32[512]{0:T(512)}, u32[]{:S(2)}) copy-start(s32[512]{0:T(512)} %param.8) | copy-start | bytes 6148
  67.5 11.8 %copy-start.7 = (f32[512,128]{1,0:T(8,128)S(1)}, f32[512,128]{1,0:T(8,128)}, u32[]{:S(2)}) copy-start(f32[512,128]{1,0:T(8,128)} %top_solved.3) | copy-start | bytes 786436
  80.8 10.3 %collective-permute-start.9 = (f32[128,256]{1,0:T(8,128)S(1)}, f32[128,256]{1,0:T(8,128)S(1)}, u32[]{:S(2)}, u32[]{:S(2)}) collective-permute-start(f32[128,256]{1,0:T(8,128)S(1)} %get-tuple-element.42.refs_5_), channel_id=1, source_target_pairs={{0,2},{1,3},{2,4},{3,5},{4,6},{5,7},{6,0},{7,1},{8,10},{9,11},{10,... | collective-permute-start | bytes 393224 | tf_op jit(solution)/shard_map/ppermute | solution.py:276
  81.5 10.0 %collective-permute-start.10 = (f32[128,256]{1,0:T(8,128)S(1)}, f32[128,256]{1,0:T(8,128)S(1)}, u32[]{:S(2)}, u32[]{:S(2)}) collective-permute-start(f32[128,256]{1,0:T(8,128)S(1)} %get-tuple-element.42.refs_5_), channel_id=1, source_target_pairs={{0,6},{1,7},{2,0},{3,1},{4,2},{5,3},{6,4},{7,5},{8,14},{9,15},{10,... | collective-permute-start | bytes 393224 | tf_op jit(solution)/shard_map/ppermute | solution.py:277
  91.1 8.4 %collective-permute-start.11 = (f32[128,256]{1,0:T(8,128)S(1)}, f32[128,256]{1,0:T(8,128)S(1)}, u32[]{:S(2)}, u32[]{:S(2)}) collective-permute-start(f32[128,256]{1,0:T(8,128)S(1)} %collective-permute-done.9.refs_6_), channel_id=1, source_target_pairs={{0,2},{1,3},{2,4},{3,5},{4,6},{5,7},{6,0},{7,1},{8,10},{9,11},{10,... | collective-permute-start | bytes 393224 | tf_op jit(solution)/shard_map/ppermute | solution.py:278
  100.6 11.5 %all-to-all-start.3 = ((f32[16,16,128]{2,1,0:T(8,128)}), f32[16,16,128]{2,1,0:T(8,128)S(1)}, u32[]{:S(2)}, u32[]{:S(2)}) async-start(f32[16,16,128]{2,1,0:T(8,128)} %get-tuple-element.43), calls=%async_computation.3 | async-start | bytes 262144 | tf_op jit(solution)/shard_map/all_to_all | solution.py:264
  104.1 6.8 %collective-permute-start.12 = (f32[128,256]{1,0:T(8,128)}, f32[128,256]{1,0:T(8,128)S(1)}, u32[]{:S(2)}, u32[]{:S(2)}) collective-permute-start(f32[128,256]{1,0:T(8,128)} %get-tuple-element.46), channel_id=1, source_target_pairs={{0,9},{1,8},{2,11},{3,10},{4,13},{5,12},{6,15},{7,14},{8,1},{9,0},... | collective-permute-start | bytes 393224 | tf_op jit(solution)/shard_map/ppermute | solution.py:268
  105.6 6.4 %collective-permute-start.13 = (f32[128,256]{1,0:T(8,128)S(1)}, f32[128,256]{1,0:T(8,128)S(1)}, u32[]{:S(2)}, u32[]{:S(2)}) collective-permute-start(f32[128,256]{1,0:T(8,128)S(1)} %get-tuple-element.47), channel_id=1, source_target_pairs={{0,8},{1,9},{2,10},{3,11},{4,12},{5,13},{6,14},{7,15},{8,0},{9,1},... | collective-permute-start | bytes 393224 | tf_op jit(solution)/shard_map/ppermute | solution.py:268
  105.8 6.4 %collective-permute-start.14 = (f32[128,256]{1,0:T(8,128)S(1)}, f32[128,256]{1,0:T(8,128)S(1)}, u32[]{:S(2)}, u32[]{:S(2)}) collective-permute-start(f32[128,256]{1,0:T(8,128)S(1)} %get-tuple-element.48), channel_id=1, source_target_pairs={{0,1},{1,0},{2,3},{3,2},{4,5},{5,4},{6,7},{7,6},{8,9},{9,8},{10,11... | collective-permute-start | bytes 393224 | tf_op jit(solution)/shard_map/ppermute | solution.py:268
